TPU v7x, 32 devices: a whole 2x2x4 slice. The times are simulated.
32 devices in a mesh: grp: 4 (over y, x), dp: 8 (over z, core).
Axes of the slice: x: 2, y: 2, z: 4, core: 2. Of those that a mesh axis runs over, the one named last changes fastest.
Arguments:
- blocks: bfloat16 [128, 128, 1280], P(('grp', 'dp')), may hold values from -6 to 6
- cotangent: bfloat16 [128, 128, 1280], P(('grp', 'dp')), may hold values from -6 to 6
- modality: int32 [128], P(('grp', 'dp')), may hold values from 0 to 1, as said below
- time_rank: int32 [128], P(('grp', 'dp')), may hold values from 0 to 3, as said below
- qkv_weight: bfloat16 [2, 1280, 1920], P(None, 'dp'), may hold values from -5 to 5
- out_weight: bfloat16 [2, 640, 1280], P(None, 'dp'), may hold values from -0.25 to 0.25
- norm_gain: bfloat16 [2, 1280], P(None, 'dp'), may hold values from 0.5 to 1.5
Outputs:
- encoded: bfloat16 [128, 128, 1280], P(('grp', 'dp'))
- block_grad: bfloat16 [128, 128, 1280], P(('grp', 'dp'))
- qkv_grad: float32 [4, 1280, 1920], P('grp', 'dp')
- out_grad: float32 [4, 640, 1280], P('grp', 'dp')
- gain_grad: float32 [4, 1280], P('grp', 'dp')
Inputs may be any that keep to these rules, and one draw needn't show every extreme that they name: On one index of dp, chosen by the draw, all blocks of all four grp rows have the same modality. `time_rank`: within each device's 4 blocks, a permutation of 0 to 3.
All inputs are finite; a program needn't handle non-finite values.
Results may differ from a plain program's by a relative error of at most 0.029.
The roundings to bfloat16 on the way count: a program that leaves them out, or rounds other values in their place, can miss the bound.
Values may be sent and summed in bfloat16 or wider, within the bound.
No kernel may reach another device: no remote copies, remote signals or barrier semaphores. Data moves between devices by JAX's collectives and lax.ppermute only.
A program may use at most 128 MiB of HBM per device.

v0:
```python
import math

import jax
import jax.numpy as jnp
from jax import lax
from jax.sharding import PartitionSpec as P

A_HEADS = 10
A_SIZE = 64
V_HEADS = 8
V_SIZE = 80
WIN = 128
VWIN = 64
CAP = 2


EPSILON = 1e-05


def from_partner(block, axis, distance):
    count = lax.axis_size(axis)
    route = []
    for low in range(count):
        high = low | 1 << distance
        if high != low and high < count:
            route += [(low, high), (high, low)]
    return lax.ppermute(block, axis, route)


def attend(qkv_rows, out_cot, heads, head_size, window):
    total_rows = qkv_rows.shape[0]
    inner = heads * head_size
    windows = total_rows // window
    shape = (windows, window, heads, head_size)
    query = qkv_rows[:, :inner].reshape(shape)
    keys = qkv_rows[:, inner : 2 * inner].reshape(shape)
    values = qkv_rows[:, 2 * inner :].reshape(shape)
    scale = 1.0 / math.sqrt(head_size)
    scores = jnp.einsum("wqhd,wkhd->whqk", query, keys, preferred_element_type=jnp.float32) * scale
    row_max = jnp.max(scores, axis=-1, keepdims=True)
    exponent = jnp.exp(scores - row_max)
    probs = exponent / jnp.sum(exponent, axis=-1, keepdims=True)
    probs_low = probs.astype(jnp.bfloat16)
    mixed = (
        jnp.einsum("whqk,wkhd->wqhd", probs_low, values, preferred_element_type=jnp.float32)
        .astype(jnp.bfloat16)
        .reshape(total_rows, inner)
    )
    cot_heads = out_cot.reshape(shape)
    d_probs = jnp.einsum("wqhd,wkhd->whqk", cot_heads, values, preferred_element_type=jnp.float32)
    d_values = jnp.einsum(
        "whqk,wqhd->wkhd", probs_low, cot_heads, preferred_element_type=jnp.float32
    ).astype(jnp.bfloat16)
    d_scores = (
        probs * (d_probs - jnp.sum(d_probs * probs, axis=-1, keepdims=True)) * scale
    ).astype(jnp.bfloat16)
    d_query = jnp.einsum(
        "whqk,wkhd->wqhd", d_scores, keys, preferred_element_type=jnp.float32
    ).astype(jnp.bfloat16)
    d_keys = jnp.einsum(
        "whqk,wqhd->wkhd", d_scores, query, preferred_element_type=jnp.float32
    ).astype(jnp.bfloat16)
    d_qkv = jnp.concatenate(
        [
            d_query.reshape(total_rows, inner),
            d_keys.reshape(total_rows, inner),
            d_values.reshape(total_rows, inner),
        ],
        axis=1,
    )
    return (mixed, d_qkv)


def audio_attend(qkv_rows, out_cot):
    return attend(qkv_rows, out_cot, A_HEADS, A_SIZE, WIN)


def vision_attend(qkv_rows, out_cot):
    return attend(qkv_rows, out_cot, V_HEADS, V_SIZE, VWIN)


def encode(x_rows, cot_rows, w_qkv, w_out, gain, kind_index):
    x_float = x_rows.astype(jnp.float32)
    mean_row = jnp.mean(x_float, axis=-1, keepdims=True)
    centered = x_float - mean_row
    inverse = lax.rsqrt(jnp.mean(centered * centered, axis=-1, keepdims=True) + EPSILON)
    x_hat = centered * inverse
    gain_float = gain.astype(jnp.float32)
    normed = (x_hat * gain_float).astype(jnp.bfloat16)
    qkv_rows = jnp.dot(normed, w_qkv, preferred_element_type=jnp.float32).astype(jnp.bfloat16)
    d_attn = jnp.dot(cot_rows, w_out.T, preferred_element_type=jnp.float32).astype(jnp.bfloat16)
    mixed, d_qkv = lax.cond(kind_index == 0, audio_attend, vision_attend, qkv_rows, d_attn)
    output = (x_float + jnp.dot(mixed, w_out, preferred_element_type=jnp.float32)).astype(
        jnp.bfloat16
    )
    grad_out = jnp.dot(mixed.T, cot_rows, preferred_element_type=jnp.float32)
    grad_qkv = jnp.dot(normed.T, d_qkv, preferred_element_type=jnp.float32)
    d_normed = jnp.dot(d_qkv, w_qkv.T, preferred_element_type=jnp.float32)
    grad_gain = jnp.sum(d_normed * x_hat, axis=0)
    scaled = d_normed * gain_float
    d_input = inverse * (
        scaled
        - jnp.mean(scaled, axis=-1, keepdims=True)
        - x_hat * jnp.mean(scaled * x_hat, axis=-1, keepdims=True)
    )
    input_grad = (cot_rows.astype(jnp.float32) + d_input).astype(jnp.bfloat16)
    return (output, input_grad, grad_qkv, grad_out, grad_gain)


def shards(blocks, cotangent, modality, time_rank, qkv_weight, out_weight, norm_gain):
    block_count, window, width = blocks.shape
    row_count = lax.axis_size("grp")
    slots = row_count * CAP
    one_hot = (modality[:, None] == jnp.arange(2, dtype=jnp.int32)[None, :]).astype(jnp.int32)
    earlier = jnp.cumsum(one_hot, axis=0) - one_hot
    order_in_kind = jnp.sum(earlier * one_hot, axis=1)
    slot_index = modality * 2 * CAP + order_in_kind % 2 * CAP + order_in_kind // 2
    send_blocks = jnp.zeros((slots, window, width), jnp.bfloat16).at[slot_index].set(blocks)
    send_cot = jnp.zeros((slots, window, width), jnp.bfloat16).at[slot_index].set(cotangent)
    recv_blocks, recv_cot = (
        lax.all_to_all(send_blocks, "grp", split_axis=0, concat_axis=0, tiled=True),
        lax.all_to_all(send_cot, "grp", split_axis=0, concat_axis=0, tiled=True),
    )
    kind_index = lax.axis_index("grp") // 2
    local_qkv = lax.dynamic_index_in_dim(qkv_weight, kind_index, 0, keepdims=False)
    local_out = lax.dynamic_index_in_dim(out_weight, kind_index, 0, keepdims=False)
    local_gain = lax.dynamic_index_in_dim(norm_gain, kind_index, 0, keepdims=False)
    w_qkv, w_out, gain = (
        lax.all_gather(local_qkv, "dp", axis=0, tiled=True),
        lax.all_gather(local_out, "dp", axis=0, tiled=True),
        lax.all_gather(local_gain, "dp", axis=0, tiled=True),
    )
    output, input_grad, grad_qkv, grad_out, grad_gain = encode(
        recv_blocks.reshape(slots * window, width),
        recv_cot.reshape(slots * window, width),
        w_qkv,
        w_out,
        gain,
        kind_index,
    )
    back_out, back_grad = (
        lax.all_to_all(
            output.reshape(slots, window, width), "grp", split_axis=0, concat_axis=0, tiled=True
        ),
        lax.all_to_all(
            input_grad.reshape(slots, window, width), "grp", split_axis=0, concat_axis=0, tiled=True
        ),
    )
    encoded = jnp.zeros_like(blocks).at[time_rank].set(back_out[slot_index])
    block_grad = jnp.zeros_like(blocks).at[time_rank].set(back_grad[slot_index])
    other_qkv, other_out, other_gain = (
        from_partner(grad_qkv.astype(jnp.bfloat16), "grp", 0).astype(grad_qkv.dtype),
        from_partner(grad_out.astype(jnp.bfloat16), "grp", 0).astype(grad_out.dtype),
        from_partner(grad_gain.astype(jnp.bfloat16), "grp", 0).astype(grad_gain.dtype),
    )
    share_qkv, share_out, share_gain = (
        lax.psum_scatter(grad_qkv + other_qkv, "dp", scatter_dimension=0, tiled=True),
        lax.psum_scatter(grad_out + other_out, "dp", scatter_dimension=0, tiled=True),
        lax.psum_scatter(grad_gain + other_gain, "dp", scatter_dimension=0, tiled=True),
    )
    return (encoded, block_grad, share_qkv[None], share_out[None], share_gain[None])


def solution(mesh):
    return jax.shard_map(
        shards,
        mesh=mesh,
        in_specs=(
            P(("grp", "dp"), None, None),
            P(("grp", "dp"), None, None),
            P(("grp", "dp")),
            P(("grp", "dp")),
            P(None, "dp", None),
            P(None, "dp", None),
            P(None, "dp"),
        ),
        out_specs=(
            P(("grp", "dp"), None, None),
            P(("grp", "dp"), None, None),
            P("grp", "dp", None),
            P("grp", "dp", None),
            P("grp", "dp"),
        ),
        check_vma=False,
    )
```

profile of v0, /device:TPU:0, one launch (start us, length us, event | category | flops | bytes accessed | tf_op | source)
XLA Modules:
  0.0 492.9 jit_solution(8307297401902880808)
XLA Ops:
  7.3 1.8 constant_dynamic-slice_fusion
  9.1 0.9 constant_dynamic-slice_fusion.1
  10.9 0.7 select_reduce_fusion
  11.5 0.7 compare_select_fusion
  12.2 1.7 broadcast.93.clone
  13.9 3.0 scatter_fusion
  16.9 5.2 %all-to-all-start = ((bf16[8,128,1280]{2,1,0:T(8,128)(2,1)}), bf16[8,128,1280]{2,1,0:T(8,128)(2,1)S(1)}, u32[]{:S(2)}, u32[]{:S(2)}) async-start(bf16[8,128,1280]{2,1,0:T(8,128)(2,1)} %scatter_fusion), calls=%async_computation | async-start | bytes 5242880 | tf_op jit(solution)/shard_map/all_to_all | solution.py:121
  22.1 1.7 broadcast.93.clone.1
  23.8 3.5 scatter_fusion.1
  27.3 25.3 %all-to-all-done = bf16[8,128,1280]{2,1,0:T(8,128)(2,1)S(1)} async-done(((bf16[8,128,1280]{2,1,0:T(8,128)(2,1)}), bf16[8,128,1280]{2,1,0:T(8,128)(2,1)S(1)}, u32[]{:S(2)}, u32[]{:S(2)}) %all-to-all-start) | async-done | bytes 2621472 | tf_op jit(solution)/shard_map/all_to_all | solution.py:121
  52.5 4.5 all-to-all-start.1
  58.7 16.8 %all-reduce = bf16[1280]{0:T(1024)(128)(2,1)S(1)} all-reduce(bf16[1280]{0:T(1024)(128)(2,1)S(1)} %dynamic-update-slice), channel_id=2, replica_groups=mesh['grp'=4,'dp'=8] {'dp'}, use_global_device_ids=true, to_apply=%add | all-reduce | flops 1280 | bytes 5120
  75.9 0.8 fusion.87
  76.8 2.3 fusion.93
  79.0 8.2 %all-to-all-done.1 = bf16[8,128,1280]{2,1,0:T(8,128)(2,1)} async-done(((bf16[8,128,1280]{2,1,0:T(8,128)(2,1)}), bf16[8,128,1280]{2,1,0:T(8,128)(2,1)}, u32[]{:S(2)}, u32[]{:S(2)}) %all-to-all-start.1) | async-done | bytes 2621472 | tf_op jit(solution)/shard_map/all_to_all | solution.py:122
  87.2 5.5 %fusion.111 = bf16[1024,640]{1,0:T(8,128)(2,1)} fusion(bf16[1024,1280]{1,0:T(8,128)(2,1)} %bitcast.13, bf16[1,640,1280]{2,1,0:T(8,128)(2,1)} %all-gather.8.cloned.1.call-done), kind=kOutput, calls=%fused_computation.119 | convolution fusion | flops 1678376960 | bytes 5570560 | tf_op jit(solution)/shard_map/dot_general | solution.py:91
  92.7 1.0 all-gather.6.cloned.1.call-done
  93.8 9.9 %fusion.105 = bf16[1024,1920]{1,0:T(8,128)(2,1)} fusion(bf16[1024,1280]{1,0:T(8,128)(2,1)} %fusion.93, bf16[1,1280,1920]{2,1,0:T(8,128)(2,1)} %all-gather.6.cloned.1.call-done), kind=kOutput, calls=%fused_computation.114 | convolution fusion | flops 5035130880 | bytes 11468800 | tf_op jit(solution)/shard_map/dot_general | solution.py:90
  103.6 80.8 %conditional.1 = (bf16[1024,640]{1,0:T(8,128)(2,1)}, bf16[1024,1920]{1,0:T(8,128)(2,1)}) conditional(s32[]{:T(128)} %convert_element_type.118, (bf16[1024,1920]{1,0:T(8,128)(2,1)}, bf16[1024,640]{1,0:T(8,128)(2,1)}) %tuple.16, (bf16[1024,1920]{1,0:T(8,128)(2,1)}, bf16[1024,640]{1,0:T(8,128)(2,1)}) %tuple.16), branch_computations={%region_6.10_spmd, %region_10.14_spmd} | conditional | flops 1049907584 | bytes 173220080 | solution.py:92
  107.5 6.3 %copy.122 = bf16[1024,1920]{0,1:T(8,128)(2,1)} copy(bf16[1024,1920]{1,0:T(8,128)(2,1)} %get-tuple-element.31) | data formatting | bytes 7864320 | tf_op jit(solution)/shard_map
  113.8 3.0 slice_bitcast_fusion.1
  117.6 0.7 copy-done.8
  118.7 0.9 fusion.77
  119.6 3.6 fusion.121
  123.2 1.4 copy.130
  124.6 2.9 copy.123
  127.6 1.8 copy.134
  129.3 1.1 copy-done.9
  130.4 3.3 fusion.72
  133.7 10.4 %fusion.63 = bf16[8,128,10,64]{1,3,2,0:T(8,128)(2,1)} fusion(f32[8,10,128,128]{2,3,1,0:T(8,128)} %fusion.72, bf16[8,128,10,64]{1,0,3,2:T(8,128)(2,1)} %bitcast.151, f32[8,10,128,128]{2,3,1,0:T(8,128)} %get-tuple-element.45, f32[8,10,128]{2,1,0:T(8,128)S(1)} %get-tuple-element.44), kind=kOutput, calls=%fused_computation.63 | convolution fusion | flops 177612928 | bytes 13148160 | tf_op jit(solution)/shard_map/cond/branch_1_fun/whqk,wqhd->wkhd/dot_general | solution.py:60
  144.1 2.4 copy.116
  146.5 4.4 fusion.61
  150.9 1.0 copy.119
  151.9 2.2 copy_bitcast_fusion
  154.0 10.4 %fusion.66 = bf16[8,128,10,64]{1,3,2,0:T(8,128)(2,1)} fusion(f32[8,10,128,128]{2,3,1,0:T(8,128)} %fusion.72, bf16[8,128,10,64]{1,0,3,2:T(8,128)(2,1)} %bitcast.149, f32[8,10,128,128]{2,3,1,0:T(8,128)} %get-tuple-element.45, f32[8,10,128]{2,1,0:T(8,128)S(1)} %get-tuple-element.44), kind=kOutput, calls=%fused_computation.64 | convolution fusion | flops 177612928 | bytes 13148160 | tf_op jit(solution)/shard_map/cond/branch_1_fun/whqk,wkhd->wqhd/dot_general | solution.py:57
  164.4 2.4 copy.113
  167.2 2.2 pad_maximum_fusion.1
  169.5 6.2 %copy.121 = bf16[1024,1920]{1,0:T(8,128)(2,1)} copy(bf16[1024,1920]{0,1:T(8,128)(2,1)} %pad_maximum_fusion.1) | data formatting | bytes 7864320 | tf_op jit(solution)/shard_map
  175.7 3.7 fusion.62
  179.4 1.0 copy.108
  180.4 1.5 copy.175
  181.9 2.4 copy.120
  184.5 4.2 fusion.124
  188.7 1.5 collective-permute-start.1
  190.3 8.9 %fusion.123 = (bf16[1280,1920]{1,0:T(8,128)(2,1)}, f32[1280,1920]{1,0:T(8,128)}) fusion(bf16[1024,1280]{1,0:T(8,128)(2,1)S(1)} %copy-done.13, bf16[1024,1920]{1,0:T(8,128)(2,1)S(1)} %copy-done.12), kind=kOutput, calls=%fused_computation.147 | convolution fusion | flops 5035622400 | bytes 21299200 | tf_op jit(solution)/shard_map/dot_general | solution.py:97
  199.8 27.7 %collective-permute-done.1 = bf16[640,1280]{1,0:T(8,128)(2,1)S(1)} collective-permute-done((bf16[640,1280]{1,0:T(8,128)(2,1)S(1)}, bf16[640,1280]{1,0:T(8,128)(2,1)S(1)}, u32[]{:S(2)}, u32[]{:S(2)}) %collective-permute-start.1) | collective-permute-done | bytes 1638432 | tf_op jit(solution)/shard_map/ppermute | solution.py:27
  227.4 2.0 convert_add_fusion.1
  229.5 102.7 %collective-permute-done = bf16[1280,1920]{1,0:T(8,128)(2,1)} collective-permute-done((bf16[1280,1920]{1,0:T(8,128)(2,1)}, bf16[1280,1920]{1,0:T(8,128)(2,1)}, u32[]{:S(2)}, u32[]{:S(2)}) %collective-permute-start) | collective-permute-done | bytes 4915232 | tf_op jit(solution)/shard_map/ppermute | solution.py:27
  332.2 9.8 %convert_add_fusion = f32[1280,1920]{1,0:T(8,128)} fusion(f32[1280,1920]{1,0:T(8,128)} %get-tuple-element.54, bf16[1280,1920]{1,0:T(8,128)(2,1)} %collective-permute-done), kind=kLoop, calls=%fused_computation.89 | loop fusion | flops 4915200 | bytes 24576000 | tf_op jit(solution)/shard_map/add | solution.py:157
  342.0 9.8 %fusion.99 = (f32[1280]{0:T(1024)S(1)}, f32[1024]{0:T(1024)S(1)}, f32[1024]{0:T(1024)S(1)}, f32[1024,1280]{1,0:T(8,128)S(1)}) fusion(bf16[8,128,1280]{2,1,0:T(8,128)(2,1)S(1)} %all-to-all-done, f32[1024]{0:T(1024)S(1)} %rsqrt_bitcast_fusion, f32[1024]{0:T(1024)S(1)} %get-tuple-element.48, f32[1280]{0:T(1024)S(1)} %convert_element_type.135, ...), kind=kOutput, calls=%fused_computation.107 | convolution fusion | flops 5044958208 | bytes 16738304 | tf_op jit(solution)/shard_map/dot_general | solution.py:98
  351.8 4.7 fusion.98
  356.4 37.1 %all-to-all-start.3 = ((bf16[8,128,1280]{2,1,0:T(8,128)(2,1)}), bf16[8,128,1280]{2,1,0:T(8,128)(2,1)}, u32[]{:S(2)}, u32[]{:S(2)}) async-start(bf16[8,128,1280]{2,1,0:T(8,128)(2,1)} %bitcast.139), calls=%async_computation.3 | async-start | bytes 5242880 | tf_op jit(solution)/shard_map/all_to_all | solution.py:145
  393.6 5.6 %fusion.100 = bf16[1024,1280]{1,0:T(8,128)(2,1)} fusion(bf16[8,128,1280]{2,1,0:T(8,128)(2,1)S(1)} %all-to-all-done, bf16[1024,640]{1,0:T(8,128)(2,1)} %get-tuple-element.19, bf16[1,640,1280]{2,1,0:T(8,128)(2,1)} %all-gather.8.cloned.1.call-done), kind=kOutput, calls=%fused_computation.108 | convolution fusion | flops 1681653760 | bytes 8192000 | tf_op jit(solution)/shard_map/dot_general | solution.py:93
  399.2 25.4 %all-to-all-done.3 = bf16[8,128,1280]{2,1,0:T(8,128)(2,1)} async-done(((bf16[8,128,1280]{2,1,0:T(8,128)(2,1)}), bf16[8,128,1280]{2,1,0:T(8,128)(2,1)}, u32[]{:S(2)}, u32[]{:S(2)}) %all-to-all-start.3) | async-done | bytes 2621472 | tf_op jit(solution)/shard_map/all_to_all | solution.py:145
  424.7 4.7 all-to-all-start.2
  429.4 2.0 collective-permute-start.2
  432.0 27.4 %collective-permute-done.2 = bf16[1280]{0:T(1024)(128)(2,1)S(1)} collective-permute-done((bf16[1280]{0:T(1024)(128)(2,1)S(1)}, bf16[1280]{0:T(1024)(128)(2,1)S(1)}, u32[]{:S(2)}, u32[]{:S(2)}) %collective-permute-start.2) | collective-permute-done | bytes 2592 | tf_op jit(solution)/shard_map/ppermute | solution.py:27
  459.5 15.0 %all-reduce.1 = f32[1280]{0:T(1024)S(1)} all-reduce(f32[1280]{0:T(1024)S(1)} %convert_add_fusion.2), channel_id=7, replica_groups=mesh['grp'=4,'dp'=8] {'dp'}, use_global_device_ids=true, to_apply=%region_21.22.clone | all-reduce | flops 1280 | bytes 10240
  475.2 2.4 gather_fusion.1
  477.6 0.9 scatter_fusion.3
  478.5 1.0 copy-done.3
  479.6 2.5 gather_fusion
  482.1 1.1 broadcast.90.clone
  483.2 2.9 scatter_fusion.2
  (66 shorter events, 5.3 us)
Async XLA Ops:
  7.2 1.9 copy-start
  7.2 6.7 %copy-start.14 = (bf16[4,128,1280]{2,1,0:T(8,128)(2,1)S(1)}, bf16[4,128,1280]{2,1,0:T(8,128)(2,1)}, u32[]{:S(2)}) copy-start(bf16[4,128,1280]{2,1,0:T(8,128)(2,1)} %param.9) | copy-start | bytes 3932164
  7.2 80.0 %all-gather.8.cloned.1.call-start = ((), (), s32[]{:S(2)}) async-start(), calls=%async_computation.9 | async-start | bytes 1843200 | tf_op jit(solution)/shard_map/all_gather | solution.py:130
  9.1 84.7 %all-gather.6.cloned.1.call-start = ((), (), s32[]{:S(2)}) async-start(), calls=%async_computation.8 | async-start | bytes 5529600 | tf_op jit(solution)/shard_map/all_gather | solution.py:129
  12.2 11.6 %copy-start.15 = (s32[4]{0:T(128)}, s32[4]{0:T(128)S(1)}, u32[]{:S(2)}) copy-start(s32[4]{0:T(128)S(1)} %compare_select_fusion) | copy-start | bytes 52
  16.9 35.6 %all-to-all-start = ((bf16[8,128,1280]{2,1,0:T(8,128)(2,1)}), bf16[8,128,1280]{2,1,0:T(8,128)(2,1)S(1)}, u32[]{:S(2)}, u32[]{:S(2)}) async-start(bf16[8,128,1280]{2,1,0:T(8,128)(2,1)} %scatter_fusion), calls=%async_computation | async-start | bytes 5242880 | tf_op jit(solution)/shard_map/all_to_all | solution.py:121
  27.3 29.9 %copy-start.17 = (u32[32]{0:T(128)S(1)}, u32[32]{0:T(128)}, u32[]{:S(2)}) copy-start(u32[32]{0:T(128)} %constant.95) | copy-start | bytes 388
  27.3 31.1 %copy-start.18 = (bf16[2,160]{1,0:T(2,128)(2,1)S(1)}, bf16[2,160]{1,0:T(2,128)(2,1)}, u32[]{:S(2)}) copy-start(bf16[2,160]{1,0:T(2,128)(2,1)} %param.15) | copy-start | bytes 1924
  52.5 34.7 %all-to-all-start.1 = ((bf16[8,128,1280]{2,1,0:T(8,128)(2,1)}), bf16[8,128,1280]{2,1,0:T(8,128)(2,1)}, u32[]{:S(2)}, u32[]{:S(2)}) async-start(bf16[8,128,1280]{2,1,0:T(8,128)(2,1)} %scatter_fusion.1), calls=%async_computation.1 | async-start | bytes 5242880 | tf_op jit(solution)/shard_map/all_to_all | solution.py:122
  57.1 429.1 %reduce-scatter.5.cloned.1.call-start = ((), (), s32[]{:S(2)}) async-start(), calls=%async_computation.7 | async-start | bytes 3686400 | tf_op jit(solution)/shard_map/reduce_scatter | solution.py:158
  117.2 1.1 copy-start.8
  117.6 1.1 copy-start.7
  127.5 2.9 copy-start.6
  129.3 1.1 copy-start.9
  144.1 2.4 copy-start.10
  164.4 2.8 copy-start.4
  164.4 2.8 copy-start.5
  184.5 5.8 %copy-start.12 = (bf16[1024,1920]{1,0:T(8,128)(2,1)S(1)}, bf16[1024,1920]{1,0:T(8,128)(2,1)}, u32[]{:S(2)}) copy-start(bf16[1024,1920]{1,0:T(8,128)(2,1)} %get-tuple-element.20) | copy-start | bytes 11796484
  184.5 5.8 %copy-start.13 = (bf16[1024,1280]{1,0:T(8,128)(2,1)S(1)}, bf16[1024,1280]{1,0:T(8,128)(2,1)}, u32[]{:S(2)}) copy-start(bf16[1024,1280]{1,0:T(8,128)(2,1)} %fusion.93) | copy-start | bytes 7864324
  188.7 38.7 %collective-permute-start.1 = (bf16[640,1280]{1,0:T(8,128)(2,1)S(1)}, bf16[640,1280]{1,0:T(8,128)(2,1)S(1)}, u32[]{:S(2)}, u32[]{:S(2)}) collective-permute-start(bf16[640,1280]{1,0:T(8,128)(2,1)S(1)} %get-tuple-element.55), channel_id=1, source_target_pairs={{0,8},{8,0},{16,24},{24,16},{1,9},{9,1},{17,25},{25,17},{2,10},{10... | collective-permute-start | bytes 4915208 | tf_op jit(solution)/shard_map/ppermute | solution.py:27
  199.2 133.0 %collective-permute-start = (bf16[1280,1920]{1,0:T(8,128)(2,1)}, bf16[1280,1920]{1,0:T(8,128)(2,1)}, u32[]{:S(2)}, u32[]{:S(2)}) collective-permute-start(bf16[1280,1920]{1,0:T(8,128)(2,1)} %get-tuple-element.53), channel_id=1, source_target_pairs={{0,8},{8,0},{16,24},{24,16},{1,9},{9,1},{17,25},{25,17},{2,10},{10... | collective-permute-start | bytes 14745608 | tf_op jit(solution)/shard_map/ppermute | solution.py:27
  229.4 256.7 %reduce-scatter.3.cloned.1.call-start = ((), (), s32[]{:S(2)}) async-start(), calls=%async_computation.6 | async-start | bytes 11059200 | tf_op jit(solution)/shard_map/reduce_scatter | solution.py:157
  356.4 68.2 %all-to-all-start.3 = ((bf16[8,128,1280]{2,1,0:T(8,128)(2,1)}), bf16[8,128,1280]{2,1,0:T(8,128)(2,1)}, u32[]{:S(2)}, u32[]{:S(2)}) async-start(bf16[8,128,1280]{2,1,0:T(8,128)(2,1)} %bitcast.139), calls=%async_computation.3 | async-start | bytes 5242880 | tf_op jit(solution)/shard_map/all_to_all | solution.py:145
  424.7 4.7 copy-start.19
  424.7 6.8 %copy-start.16 = (s32[4]{0:T(128)S(1)}, s32[4]{0:T(128)}, u32[]{:S(2)}) copy-start(s32[4]{0:T(128)} %copy-done.15) | copy-start | bytes 52
  424.7 54.9 %all-to-all-start.2 = ((bf16[8,128,1280]{2,1,0:T(8,128)(2,1)}), bf16[8,128,1280]{2,1,0:T(8,128)(2,1)}, u32[]{:S(2)}, u32[]{:S(2)}) async-start(bf16[8,128,1280]{2,1,0:T(8,128)(2,1)} %bitcast.155), calls=%async_computation.2 | async-start | bytes 5242880 | tf_op jit(solution)/shard_map/all_to_all | solution.py:142
  429.4 30.1 %collective-permute-start.2 = (bf16[1280]{0:T(1024)(128)(2,1)S(1)}, bf16[1280]{0:T(1024)(128)(2,1)S(1)}, u32[]{:S(2)}, u32[]{:S(2)}) collective-permute-start(bf16[1280]{0:T(1024)(128)(2,1)S(1)} %convert_element_type.131), channel_id=1, source_target_pairs={{0,8},{8,0},{16,24},{24,16},{1,9},{9,1},{17,25},{25,17},{2,10},{10... | collective-permute-start | bytes 7688 | tf_op jit(solution)/shard_map/ppermute | solution.py:27
  478.5 1.1 copy-start.3
  479.6 6.6 %copy-start.1 = (bf16[2,160,1920]{2,1,0:T(8,128)(2,1)S(1)}, bf16[2,160,1920]{2,1,0:T(8,128)(2,1)}, u32[]{:S(2)}) copy-start(bf16[2,160,1920]{2,1,0:T(8,128)(2,1)} %param.13) | copy-start | bytes 3686404
Sparse Core Ops, SparseCore 0:
  10.2 28.1 all-gather.7
  40.6 53.1 all-gather.5
  229.5 74.2 reduce-scatter.4
  342.1 135.7 reduce-scatter.2
where the time goes:
time: 499 us; the launch traced here: 493 us
  waiting for transfers between devices  218 us (44%)
  matrix products  77 us (15%)
  local copies, waits for them, and re-layouts  62.9 us (13%)
  starting transfers between devices  55.8 us (11%)
  blocking collectives  31.8 us (6%)
  other arithmetic  27.9 us (6%)
  between operations  15.5 us (3%)
    ppermute x3, waiting for transfers between devices, from_partner(): return lax.ppermute(block, axis, route)  158 us
    all_to_all x1, starting transfers between devices, shards(): lax.all_to_all(input_grad.reshape(slots, window, width), 'grp', split_axi...  37.1 us
    unnamed x2, blocking collectives  31.8 us
    all_to_all x1, waiting for transfers between devices, shards(): lax.all_to_all(input_grad.reshape(slots, window, width), 'grp', split_axi...  25.4 us
    all_to_all x1, waiting for transfers between devices, shards(): lax.all_to_all(send_blocks, 'grp', split_axis=0, concat_axis=0, tiled=True)  25.3 us
    another operation x8, local copies, waits for them, and re-layouts  22.5 us
    cond x21, local copies, waits for them, and re-layouts  11 us
    dot_general x1, matrix products, attend(): jnp.einsum('whqk,wqhd->wkhd', d_scores, query, preferred_element_type=jnp...  10.4 us
  transfers between devices with their start and end apart: 11, of which 7 were waited for; matrix products, arithmetic and copies ran while one was open for 15% of the time, Pallas kernels for 0%

commit v1 on v0

v1 whole, which is shorter than its diff:
```python
import functools
import math

import jax
import jax.numpy as jnp
from jax import lax
from jax.experimental import pallas as pl
from jax.experimental.pallas import tpu as pltpu
from jax.sharding import PartitionSpec as P

A_HEADS = 10
A_SIZE = 64
V_HEADS = 8
V_SIZE = 80
VWIN = 64
EPSILON = 1e-05
LANES = 128
AXES = ("grp", "dp")
VMEM_LIMIT = 60 * 1024 * 1024
BF16 = jnp.bfloat16
F32 = jnp.float32

VMEM = pl.BlockSpec(memory_space=pltpu.VMEM)
SMEM = pl.BlockSpec(memory_space=pltpu.SMEM)
HBM = pl.BlockSpec(memory_space=pl.ANY)


def params():
    return pltpu.CompilerParams(vmem_limit_bytes=VMEM_LIMIT)


def cost(flops, traffic):
    return pl.CostEstimate(flops=flops, bytes_accessed=traffic, transcendentals=0)


def dot_nn(a, b):
    return lax.dot_general(a, b, (((1,), (0,)), ((), ())), preferred_element_type=F32)


def dot_nt(a, b):
    return lax.dot_general(a, b, (((1,), (1,)), ((), ())), preferred_element_type=F32)


def dot_tn(a, b):
    return lax.dot_general(a, b, (((0,), (0,)), ((), ())), preferred_element_type=F32)


def normalise(x):
    mean = jnp.mean(x, axis=-1, keepdims=True)
    centered = x - mean
    inverse = lax.rsqrt(jnp.mean(centered * centered, axis=-1, keepdims=True) + EPSILON)
    return centered * inverse, inverse


def norm_kernel(kind_ref, x_ref, gain_ref, h_ref, ht_ref):
    def body(b, carry):
        x_hat, _ = normalise(x_ref[b].astype(F32))
        h = (x_hat * gain_ref[pl.ds(kind_ref[b], 1), :]).astype(BF16)
        h_ref[b] = h
        ht_ref[b] = h.T
        return carry

    lax.fori_loop(0, x_ref.shape[0], body, 0)


def attend(b, heads, size, window, qkv, da, attnt_ref, dq_ref, dk_ref, dv_ref):
    rows = qkv.shape[0]
    inner = heads * size
    scale = 1.0 / math.sqrt(size)
    same = None
    if window < rows:
        key = lax.broadcasted_iota(jnp.int32, (rows, 2 * rows), 0) // window
        query = lax.broadcasted_iota(jnp.int32, (rows, 2 * rows), 1) % rows // window
        same = key == query
    sums = {}

    def add(name, tile, value):
        known = sums.get((name, tile))
        sums[name, tile] = value if known is None else known + value

    for head in range(0, heads, 2):
        first, last = head * size // LANES, ((head + 2) * size - 1) // LANES + 1
        low, wide = first * LANES, (last - first) * LANES
        lane = lax.broadcasted_iota(jnp.int32, (rows, wide), 1) + low
        row = lax.broadcasted_iota(jnp.int32, (wide, rows), 0) + low
        lanes = [(lane >= h * size) & (lane < (h + 1) * size) for h in (head, head + 1)]
        bands = [(row >= h * size) & (row < (h + 1) * size) for h in (head, head + 1)]
        q, k, v = (qkv[:, at + low : at + low + wide] for at in (0, inner, 2 * inner))
        g = da[:, low : low + wide]
        q_pair = jnp.concatenate([jnp.where(mask, q, 0) for mask in lanes], axis=0)
        g_pair = jnp.concatenate([jnp.where(mask, g, 0) for mask in lanes], axis=0)
        scores = dot_nt(k, q_pair) * scale
        if same is not None:
            scores = jnp.where(same, scores, -1e30)
        exponent = jnp.exp(scores - jnp.max(scores, axis=0, keepdims=True))
        probs = exponent * (1.0 / jnp.sum(exponent, axis=0, keepdims=True))
        d_probs = dot_nt(v, g_pair)
        mean = jnp.sum(d_probs * probs, axis=0, keepdims=True)
        d_scores = (probs * (d_probs - mean) * scale).astype(BF16)
        probs = probs.astype(BF16)
        d_v = dot_nn(probs, g_pair)
        d_k = dot_nn(d_scores, q_pair)
        vt, kt = v.T, k.T
        mixed = dot_nn(
            jnp.concatenate([jnp.where(band, vt, 0) for band in bands], axis=1),
            jnp.concatenate([probs[:, :rows], probs[:, rows:]], axis=0),
        )
        d_q = dot_nn(
            jnp.concatenate([jnp.where(band, kt, 0) for band in bands], axis=1),
            jnp.concatenate([d_scores[:, :rows], d_scores[:, rows:]], axis=0),
        )
        for tile in range(first, last):
            span = slice(tile * LANES - low, (tile + 1) * LANES - low)
            add("v", tile, d_v[:, span])
            add("k", tile, d_k[:, span])
            add("q", tile, d_q[span])
            add("o", tile, mixed[span])
        for tile in range(first, last):
            span = slice(tile * LANES, (tile + 1) * LANES)
            if (head + 2) * size >= (tile + 1) * LANES:
                dv_ref[b, :, span] = sums.pop(("v", tile)).astype(BF16)
                dk_ref[b, :, span] = sums.pop(("k", tile)).astype(BF16)
                dq_ref[b, :, span] = sums.pop(("q", tile)).astype(BF16).T
                attnt_ref[b, span, :] = sums.pop(("o", tile)).astype(BF16)


def piece_copies(listed, wq, wo, sems):
    copies = []

    def add(source, target):
        copies.append(pltpu.make_async_copy(source, target, sems.at[len(copies)]))

    half_rows = listed[0][0].shape[1]
    wide = wq.shape[2]
    narrow = wo.shape[2] // 2
    for ref, at, kind, half, shard in listed:
        row = pl.multiple_of((shard * 2 + half) * half_rows, 16)
        out_row = pl.multiple_of(shard * half_rows, 16)
        column = pl.multiple_of(half * narrow, LANES)
        add(ref.at[at, :, pl.ds(0, wide)], wq.at[kind, pl.ds(row, half_rows), :])
        add(
            ref.at[at, :, pl.ds(wide, narrow)],
            wo.at[kind, pl.ds(out_row, half_rows), pl.ds(column, narrow)],
        )
    return copies


def routed_entries(where_ref, refs):
    g, z, c = where_ref[0], where_ref[1], where_ref[2]
    cores = (c, 1 - c)
    listed = []

    def add(ref, at, q, shard):
        listed.append((ref, at, q // 2, q % 2, shard))

    for ref, core in zip(refs[:2], cores):
        for q in range(4):
            add(ref, q, q, 2 * z + core)
    for i, far in ((2, 3), (4, 2)):
        for ref, core in zip(refs[i : i + 2], cores):
            for other in range(4):
                add(ref, other, g ^ other, 2 * lax.rem(z + far, 4) + core)
    for other in range(4):
        for ref, core in zip(refs[6 + 2 * other : 8 + 2 * other], cores):
            add(ref, 0, g ^ other, 2 * lax.rem(z + 1, 4) + core)
    return listed


def load_weights(routed, where_ref, refs, wq, wo, sems):
    if routed:
        copies = piece_copies(routed_entries(where_ref, refs), wq, wo, sems)
    else:
        copies = [
            pltpu.make_async_copy(refs[0], wq, sems.at[0]),
            pltpu.make_async_copy(refs[1], wo, sems.at[1]),
        ]
    for copy in copies:
        copy.start()
    for copy in copies:
        copy.wait()


def layer_kernel(routed, n_weights, where_ref, kind_ref, h_ref, cot_ref, *rest):
    weights, rest = rest[:n_weights], rest[n_weights:]
    attnt_ref, dq_ref, dk_ref, dv_ref, wq, wo, qkv_ref, da_ref, sems = rest
    load_weights(routed, where_ref, weights, wq, wo, sems)
    chunk = 3 * LANES

    def body(b, carry):
        kind = kind_ref[b]
        for at in range(0, wq.shape[2], chunk):
            qkv_ref[:, at : at + chunk] = dot_nn(h_ref[b], wq[kind, :, at : at + chunk]).astype(BF16)
        for at in range(0, wo.shape[1], LANES):
            da_ref[:, at : at + LANES] = dot_nt(cot_ref[b], wo[kind, at : at + LANES, :]).astype(BF16)

        @pl.when(kind == 0)
        def _():
            attend(b, A_HEADS, A_SIZE, qkv_ref.shape[0], qkv_ref, da_ref, attnt_ref, dq_ref, dk_ref, dv_ref)

        @pl.when(kind != 0)
        def _():
            attend(b, V_HEADS, V_SIZE, VWIN, qkv_ref, da_ref, attnt_ref, dq_ref, dk_ref, dv_ref)

        return carry

    lax.fori_loop(0, h_ref.shape[0], body, 0)


def result_kernel(routed, n_weights, where_ref, kind_ref, rank_ref, x_ref, cot_ref, gain_ref, attnt_ref, dq_ref, dk_ref, dv_ref, *rest):
    weights, rest = rest[:n_weights], rest[n_weights:]
    encoded_ref, grad_ref, wq, wo, wide_ref, sems = rest
    load_weights(routed, where_ref, weights, wq, wo, sems)
    inner = dq_ref.shape[2]
    chunk = 2 * LANES
    width = x_ref.shape[2]

    def body(b, carry):
        kind, rank = kind_ref[b], rank_ref[b]
        attn = attnt_ref[b].T
        for at in range(0, width, chunk):
            span = slice(at, at + chunk)
            encoded_ref[rank, :, span] = (
                x_ref[b, :, span].astype(F32) + dot_nn(attn, wo[kind, :, span])
            ).astype(BF16)
            wide_ref[:, span] = (
                dot_nt(dq_ref[b], wq[kind, span, :inner])
                + dot_nt(dk_ref[b], wq[kind, span, inner : 2 * inner])
                + dot_nt(dv_ref[b], wq[kind, span, 2 * inner :])
            )
        x_hat, inverse = normalise(x_ref[b].astype(F32))
        scaled = wide_ref[...] * gain_ref[pl.ds(kind, 1), :]
        d_input = inverse * (
            scaled
            - jnp.mean(scaled, axis=-1, keepdims=True)
            - x_hat * jnp.mean(scaled * x_hat, axis=-1, keepdims=True)
        )
        grad_ref[rank] = (cot_ref[b].astype(F32) + d_input).astype(BF16)
        return carry

    lax.fori_loop(0, x_ref.shape[0], body, 0)


def left_kernel(where_ref, kind_ref, ht_a, ht_b, left):
    g, c = where_ref[0], where_ref[2]
    count = ht_a.shape[0]
    rows = left.shape[2] // 8
    for far in range(2):
        kind = (g // 2) ^ far
        for i in range(2 * count):
            source = ht_a if i < count else ht_b
            keep = kind_ref[i] == kind
            for side in range(2):
                for z in range(4):
                    row = pl.multiple_of(((2 * z + c) * 2 + ((g % 2) ^ side)) * rows, 16)
                    value = source[i % count, pl.ds(row, rows), :]
                    at = (side * 4 + z) * rows
                    left[far, i // count, at : at + rows, (i % count) * LANES : (i % count + 1) * LANES] = (
                        jnp.where(keep, value, jnp.zeros_like(value))
                    )


def store(far, side, chunk, second, value, cut, refs):
    y_ref, x_ref, own_ref, xa_ref, yb_ref = refs
    size = value.shape[-1]
    span = slice(chunk * size, (chunk + 1) * size)
    if (far, side) == (0, 0):
        start = 2 * cut * second + chunk * size
        own_ref[:, :, start : start + size] = value
    elif not second:
        if far:
            y_ref[side, :, :, span] = value.astype(BF16)
        else:
            xa_ref[:, :, span] = value
    elif side:
        x_ref[far, :, :, span] = value.astype(BF16)
    else:
        yb_ref[:, :, span] = value


def out_grad(cut, where_ref, kind_ref, attnt_a, attnt_b, cot_a, cot_b, refs, left):
    g, c = where_ref[0], where_ref[2]
    count = attnt_a.shape[0]
    rows = left.shape[2] // 4
    half_width = cot_a.shape[2] // 2
    for far in range(2):
        kind = (g // 2) ^ far
        for i in range(2 * count):
            source = attnt_a if i < count else attnt_b
            keep = kind_ref[i] == kind
            for z in range(4):
                row = pl.multiple_of((2 * z + c) * rows, 16)
                value = source[i % count, pl.ds(row, rows), :]
                left[far, i // count, z * rows : (z + 1) * rows, (i % count) * LANES : (i % count + 1) * LANES] = (
                    jnp.where(keep, value, jnp.zeros_like(value))
                )
    for far in range(2):
        for side in range(2):
            column = ((g % 2) ^ side) * half_width
            for second, (at, size) in enumerate(((0, cut), (cut, half_width - cut))):
                span = pl.ds(pl.multiple_of(column + at, LANES), size)
                total = dot_nn(left[far, 0], cot_a[:, :, span].reshape(-1, size))
                total += dot_nn(left[far, 1], cot_b[:, :, span].reshape(-1, size))
                store(far, side, 0, second, total.reshape(4, rows, size), cut, refs)


def qkv_grad(cut, chunk, left, d_a, d_b, refs):
    rows = left.shape[2] // 8
    width = d_a.shape[2]
    for far in range(2):
        for second, (at, size) in enumerate(((0, cut), (cut, width - cut))):
            span = slice(at, at + size)
            total = dot_nn(left[far, 0], d_a[:, :, span].reshape(-1, size))
            total += dot_nn(left[far, 1], d_b[:, :, span].reshape(-1, size))
            total = total.reshape(2, 4, rows, size)
            for side in range(2):
                store(far, side, chunk, second, total[side], cut, refs)


def first_terms_kernel(cut, where_ref, kind_ref, left, attnt_a, attnt_b, cot_a, cot_b, dv_a, dv_b, *rest):
    refs, out_left = rest[:5], rest[5]
    out_grad(cut, where_ref, kind_ref, attnt_a, attnt_b, cot_a, cot_b, refs, out_left)
    qkv_grad(cut, 1, left, dv_a, dv_b, refs)


def second_terms_kernel(cut, left, dk_a, dk_b, dq_a, dq_b, *refs):
    qkv_grad(cut, 0, left, dk_a, dk_b, refs)
    qkv_grad(cut, 1, left, dq_a, dq_b, refs)


CUT = 384


def share_outputs(rows, width):
    first, second = 2 * CUT, 2 * (width - CUT)
    return [
        jax.ShapeDtypeStruct((2, 4, rows, first), BF16),
        jax.ShapeDtypeStruct((2, 4, rows, second), BF16),
        jax.ShapeDtypeStruct((4, rows, first + second), F32),
        jax.ShapeDtypeStruct((4, rows, first), F32),
        jax.ShapeDtypeStruct((4, rows, second), F32),
    ]


def left_factor(where, kinds, ht, ht_other):
    count, width, window = ht.shape
    return pl.pallas_call(
        left_kernel,
        out_shape=jax.ShapeDtypeStruct((2, 2, width // 2, count * window), BF16),
        in_specs=[SMEM, SMEM] + [VMEM] * 2,
        out_specs=VMEM,
        compiler_params=params(),
        cost_estimate=cost(0, 12 << 20),
        name="left_factor",
    )(where, kinds, ht, ht_other)


def first_terms(where, kinds, left, *pairs):
    count, inner, window = pairs[0].shape
    return pl.pallas_call(
        functools.partial(first_terms_kernel, CUT),
        out_shape=share_outputs(left.shape[2] // 8, inner),
        in_specs=[SMEM, SMEM] + [VMEM] * (1 + len(pairs)),
        out_specs=[VMEM] * 5,
        scratch_shapes=[pltpu.VMEM((2, 2, inner // 2, count * window), BF16)],
        compiler_params=params(),
        cost_estimate=cost(12 * count * window * left.shape[2] * inner, 12 << 20),
        name="first_terms",
    )(where, kinds, left, *pairs)


def second_terms(left, *pairs):
    count, window, inner = pairs[0].shape
    return pl.pallas_call(
        functools.partial(second_terms_kernel, CUT),
        out_shape=share_outputs(left.shape[2] // 8, inner),
        in_specs=[VMEM] * (1 + len(pairs)),
        out_specs=[VMEM] * 5,
        compiler_params=params(),
        cost_estimate=cost(16 * count * window * left.shape[2] * inner, 12 << 20),
        name="second_terms",
    )(left, *pairs)


def flat(groups, shards, move):
    pairs = []
    for g in range(groups):
        for d in range(shards):
            to_g, to_d = move(g, d)
            pairs.append((g * shards + d, to_g * shards + to_d))
    return pairs


def routes(groups, shards):
    chips = shards // 2
    make = functools.partial(flat, groups, shards)
    return {
        "sibling": make(lambda g, d: (g, d ^ 1)),
        "x": make(lambda g, d: (g ^ 1, d)),
        "y": make(lambda g, d: (g ^ 2, d)),
        "z": [
            make(lambda g, d, s=s: (g, (d // 2 + s) % chips * 2 + d % 2)) for s in range(chips)
        ],
    }


def send(value, route):
    return lax.ppermute(value, AXES, route)


def tied(value, *others):
    return lax.optimization_barrier((value, *others))[0]


def gather_weights(qkv_weight, out_weight, route, g, before_pass, before_last):
    kinds, rows, columns = qkv_weight.shape
    narrow = out_weight.shape[2] // 2
    quarters = jnp.concatenate(
        [
            qkv_weight.reshape(4, rows // 2, columns),
            out_weight.reshape(kinds, -1, 2, narrow).transpose(0, 2, 1, 3).reshape(4, -1, narrow),
        ],
        axis=2,
    )
    own = lax.dynamic_slice_in_dim(quarters, g, 1, 0)
    diagonal = lax.dynamic_slice_in_dim(quarters, g ^ 3, 1, 0)

    def in_plane(held):
        return send(held, route["x"]), send(held, route["y"])

    def pair(value):
        return [value, send(value, route["sibling"])]

    near = send(own, route["z"][1])
    pieces = pair(quarters)
    far = send(tied(near, before_pass), route["z"][1])
    near_x, near_y = in_plane(near)
    back = send(tied(own, near), route["z"][3])
    near_across = send(near_y, route["x"])
    pieces += pair(jnp.concatenate([near, near_x, near_y, near_across], axis=0))
    far_x, far_y = in_plane(far)
    back_across = send(tied(diagonal, far), route["z"][3])
    far_across = send(far_x, route["y"])
    back_x, back_y = in_plane(tied(back, before_last))
    pieces += pair(jnp.concatenate([far, far_x, far_y, far_across], axis=0))
    for piece in (back, back_x, back_y, back_across):
        pieces += pair(piece)
    return pieces


def reduce_plane(terms, route):
    to_y, to_x, own, x_term, y_term = terms
    from_y, from_x = send(to_y, route["y"]), send(to_x, route["x"])
    next_x = send((x_term + from_y[1].astype(F32)).astype(BF16), route["x"])
    next_y = send((y_term + from_x[1].astype(F32)).astype(BF16), route["y"])
    total = own + jnp.concatenate(
        [
            from_y[0].astype(F32) + next_x.astype(F32),
            from_x[0].astype(F32) + next_y.astype(F32),
        ],
        axis=-1,
    )
    return total, from_y


def reduce_line(total, route, z):
    mine = lax.dynamic_index_in_dim(total, z, 0, keepdims=False)
    for step in range(1, 4):
        part = lax.dynamic_index_in_dim(total, (z + step) % 4, 0, keepdims=False)
        mine += send(part.astype(BF16), route["z"][step]).astype(F32)
    return mine


def chunk_parts(share, inner):
    first, second = share[:, : 2 * CUT], share[:, 2 * CUT :]
    rest = inner - CUT
    return [
        jnp.concatenate([first[:, i * CUT : (i + 1) * CUT], second[:, i * rest : (i + 1) * rest]], axis=1)
        for i in range(2)
    ]


def whole_weights(qkv_weight, out_weight):
    return [
        lax.all_gather(qkv_weight, "dp", axis=1, tiled=True),
        lax.all_gather(out_weight, "dp", axis=1, tiled=True),
    ]


def summed_terms(kinds, h, dqkv, attn, cot):
    shards = lax.axis_size("dp")
    results = []
    for left, right in ((h, dqkv), (attn, cot)):
        parts = []
        for kind in range(2):
            keep = (kinds == kind)[:, None, None]
            parts.append(
                jnp.einsum("bwi,bwj->ij", jnp.where(keep, left, 0), right, preferred_element_type=F32)
            )
        total = lax.psum_scatter(
            jnp.stack(parts).reshape(2, shards, -1, right.shape[2]), "dp", scatter_dimension=1
        )
        total = lax.psum(total, "grp")
        results.append(lax.dynamic_index_in_dim(total, lax.axis_index("grp") // 2, 0, keepdims=False))
    return results


def shards(blocks, cotangent, modality, time_rank, qkv_weight, out_weight, norm_gain):
    groups, shard_count = lax.axis_size("grp"), lax.axis_size("dp")
    g, d = lax.axis_index("grp"), lax.axis_index("dp")
    z, c = d // 2, d % 2
    count, window, width = blocks.shape
    columns = qkv_weight.shape[2]
    inner = columns // 3
    routed = groups == 4 and shard_count == 8 and out_weight.shape[1] % 16 == 0
    where = jnp.stack([g, z, c]).astype(jnp.int32)
    gain = lax.all_gather(norm_gain, "dp", axis=1, tiled=True).astype(F32)

    rows = count * window
    h, ht = pl.pallas_call(
        norm_kernel,
        out_shape=[
            jax.ShapeDtypeStruct(blocks.shape, BF16),
            jax.ShapeDtypeStruct((count, width, window), BF16),
        ],
        in_specs=[SMEM, VMEM, VMEM],
        out_specs=[VMEM] * 2,
        compiler_params=params(),
        cost_estimate=cost(20 * rows * width, 8 * rows * width),
        name="norm",
    )(modality, blocks, gain)

    if routed:
        route = routes(groups, shard_count)
        kinds_other = send(modality.astype(F32), route["sibling"]).astype(jnp.int32)
        kinds = jnp.concatenate([modality, kinds_other])
        cot_other = send(cotangent, route["sibling"])
        ht_other = send(ht, route["sibling"])
        left = left_factor(where, kinds, ht, ht_other)
        weights = gather_weights(qkv_weight, out_weight, route, g, gain, ht_other)
        h = tied(h, left, cot_other)
    else:
        weights = whole_weights(qkv_weight, out_weight)
    n_weights = len(weights)
    weight_scratch = [
        pltpu.VMEM((2, width, columns), BF16),
        pltpu.VMEM((2, inner, width), BF16),
    ]
    weight_sems = pltpu.SemaphoreType.DMA((64,))

    attnt, dq, dk, dv = pl.pallas_call(
        functools.partial(layer_kernel, routed, n_weights),
        out_shape=[jax.ShapeDtypeStruct((count, inner, window), BF16)]
        + [jax.ShapeDtypeStruct((count, window, inner), BF16)] * 3,
        in_specs=[SMEM, SMEM, VMEM, VMEM] + [HBM] * n_weights,
        out_specs=[VMEM] * 4,
        scratch_shapes=weight_scratch
        + [pltpu.VMEM((window, columns), BF16), pltpu.VMEM((window, inner), BF16), weight_sems],
        compiler_params=params(),
        cost_estimate=cost(8 * rows * width * columns, 20 << 20),
        name="layer",
    )(where, modality, h, cotangent, *weights)

    result_attnt = attnt
    if routed:
        attnt_other, dv_other, dk_other, dq_other = [
            send(part, route["sibling"]) for part in (attnt, dv, dk, dq)
        ]
        first = first_terms(where, kinds, left, attnt, attnt_other, cotangent, cot_other, dv, dv_other)
        second = list(second_terms(left, tied(dk, first[0]), dk_other, dq, dq_other))
        result_attnt = tied(attnt, second[0])
        total, arrived = reduce_plane(first, route)
        second[0], second[1] = lax.optimization_barrier((second[0], second[1], arrived))[:2]
        shares = [reduce_line(total, route, z)]
        shares.append(reduce_line(reduce_plane(second, route)[0], route, z))
        parts = []
        for share in shares:
            other = send(share.astype(BF16), route["x"]).astype(F32)
            ordered = [jnp.where(g % 2 == i, share, other) for i in range(2)]
            parts += list(zip(*[chunk_parts(half, inner) for half in ordered]))
        out_halves, v_halves, k_halves, q_halves = parts
        share_out = jnp.concatenate(out_halves, axis=1)
        share_qkv = jnp.concatenate(
            [jnp.concatenate(halves, axis=0) for halves in (q_halves, k_halves, v_halves)], axis=1
        )
    else:
        share_qkv, share_out = summed_terms(
            modality, h, jnp.concatenate([dq, dk, dv], axis=2), attnt.transpose(0, 2, 1), cotangent
        )

    kind = g // 2
    own_weight = lax.dynamic_index_in_dim(qkv_weight, kind, 0, keepdims=False).astype(F32)
    own_gain = lax.dynamic_index_in_dim(norm_gain, kind, 0, keepdims=False).astype(F32)
    share_gain = jnp.sum(share_qkv * own_weight, axis=1) / own_gain

    encoded, block_grad = pl.pallas_call(
        functools.partial(result_kernel, routed, n_weights),
        out_shape=[jax.ShapeDtypeStruct(blocks.shape, BF16)] * 2,
        in_specs=[SMEM] * 3 + [VMEM] * 7 + [HBM] * n_weights,
        out_specs=[VMEM] * 2,
        scratch_shapes=weight_scratch + [pltpu.VMEM((window, width), F32), weight_sems],
        compiler_params=params(),
        cost_estimate=cost(2 * rows * width * (columns + inner), 20 << 20),
        name="result",
    )(where, modality, time_rank, blocks, cotangent, gain, result_attnt, dq, dk, dv, *weights)

    return (encoded, block_grad, share_qkv[None], share_out[None], share_gain[None])


def solution(mesh):
    return jax.shard_map(
        shards,
        mesh=mesh,
        in_specs=(
            P(("grp", "dp"), None, None),
            P(("grp", "dp"), None, None),
            P(("grp", "dp")),
            P(("grp", "dp")),
            P(None, "dp", None),
            P(None, "dp", None),
            P(None, "dp"),
        ),
        out_specs=(
            P(("grp", "dp"), None, None),
            P(("grp", "dp"), None, None),
            P("grp", "dp", None),
            P("grp", "dp", None),
            P("grp", "dp"),
        ),
        check_vma=False,
    )
```

time: 499 us -> 245 us (0.49)
  the two profiles are of different devices: /device:TPU:0 before, /device:TPU:8 now
where the time goes in v1:
time: 245 us; the launch traced here: 241 us
  waiting for transfers between devices  96.5 us (39%)
  Pallas kernels  63.8 us (26%)
  starting transfers between devices  41.8 us (17%)
  blocking collectives  14.4 us (6%)
  local copies, waits for them, and re-layouts  12.2 us (5%)
  other arithmetic  11 us (4%)
    ppermute x42, waiting for transfers between devices, send(): return lax.ppermute(value, AXES, route)  96.5 us
    ppermute x42, starting transfers between devices, send(): return lax.ppermute(value, AXES, route)  41.8 us
    pallas_call x1, Pallas kernels, shards(): pl.pallas_call(functools.partial(layer_kernel, routed, n_weights), out_sh...  20.6 us
    pallas_call x1, Pallas kernels, shards(): pl.pallas_call(functools.partial(result_kernel, routed, n_weights), out_s...  17.1 us
    all_gather x1, blocking collectives, shards(): gain = lax.all_gather(norm_gain, 'dp', axis=1, tiled=True).astype(F32)  14.4 us
    pallas_call x1, Pallas kernels, first_terms(): pl.pallas_call(functools.partial(first_terms_kernel, CUT), out_shape=shar...  9.45 us
    pallas_call x1, Pallas kernels, second_terms(): pl.pallas_call(functools.partial(second_terms_kernel, CUT), out_shape=sha...  8.55 us
    unnamed x42, local copies, waits for them, and re-layouts  7.76 us
  transfers between devices with their start and end apart: 42, of which 22 were waited for; matrix products, arithmetic and copies ran while one was open for 7% of the time, Pallas kernels for 14%

profile of v1, /device:TPU:8, one launch (start us, length us, event | category | flops | bytes accessed | tf_op | source)
XLA Modules:
  0.0 240.8 jit_solution(6786309310030462933)
XLA Ops:
  0.7 1.2 fusion.32
  2.1 0.8 fusion.6
  2.9 1.6 collective-permute-start.4
  4.5 14.4 %all-gather = bf16[8,160,2]{1,2,0:T(2,128)(2,1)S(1)} all-gather(bf16[1,160,2]{1,2,0:T(2,128)(2,1)S(1)} %bitcast.92), channel_id=1, replica_groups=mesh['grp'=4,'dp'=8] {'dp'}, dimensions={0}, use_global_device_ids=true | all-gather | bytes 5760 | tf_op jit(solution)/shard_map/all_gather | solution.py:516
  19.7 4.3 %norm.1 = (bf16[4,128,1280]{2,1,0:T(8,128)(2,1)}, bf16[4,1280,128]{2,1,0:T(8,128)(2,1)}) custom-call(s32[4]{0:T(128)} %kind_ref.5, bf16[4,128,1280]{2,1,0:T(8,128)(2,1)} %x_ref.3, f32[2,1280]{1,0:T(2,128)} %bitcast.89), custom_call_target="tpu_custom_call" | custom-call | flops 13107200 | bytes 5242880 | tf_op jit(solution)/shard_map/norm/pallas_call | solution.py:519
  25.3 2.0 collective-permute-start.14
  27.3 1.5 collective-permute-start.5
  28.8 1.8 constant_dynamic-update-slice_fusion.3
  30.6 6.2 %collective-permute-done.9 = bf16[1,80,2560]{2,1,0:T(8,128)(2,1)S(1)} collective-permute-done((bf16[1,80,2560]{2,1,0:T(8,128)(2,1)}, bf16[1,80,2560]{2,1,0:T(8,128)(2,1)S(1)}, u32[]{:S(2)}, u32[]{:S(2)}) %collective-permute-start.9) | collective-permute-done | bytes 409632 | tf_op jit(solution)/shard_map/ppermute | solution.py:407
  36.8 1.5 collective-permute-start.6
  38.3 0.8 constant_dynamic-update-slice_fusion.7
  39.1 1.5 collective-permute-start.10
  40.6 0.8 constant_dynamic-update-slice_fusion.2
  41.4 5.6 %collective-permute-done.6 = bf16[1,80,2560]{2,1,0:T(8,128)(2,1)S(1)} collective-permute-done((bf16[1,80,2560]{2,1,0:T(8,128)(2,1)}, bf16[1,80,2560]{2,1,0:T(8,128)(2,1)S(1)}, u32[]{:S(2)}, u32[]{:S(2)}) %collective-permute-start.6) | collective-permute-done | bytes 409632 | tf_op jit(solution)/shard_map/ppermute | solution.py:407
  47.0 1.5 collective-permute-start.11
  48.5 0.8 constant_dynamic-update-slice_fusion.1
  49.3 1.5 collective-permute-start.7
  50.8 0.8 constant_dynamic-update-slice_fusion.6
  51.6 5.0 %collective-permute-done.11 = bf16[1,80,2560]{2,1,0:T(8,128)(2,1)S(1)} collective-permute-done((bf16[1,80,2560]{2,1,0:T(8,128)(2,1)S(1)}, bf16[1,80,2560]{2,1,0:T(8,128)(2,1)S(1)}, u32[]{:S(2)}, u32[]{:S(2)}) %collective-permute-start.11) | collective-permute-done | bytes 409632 | tf_op jit(solution)/shard_map/ppermute | solution.py:407
  56.7 1.5 collective-permute-start.12
  59.0 3.6 %collective-permute-start.20 = (bf16[1,80,2560]{2,1,0:T(8,128)(2,1)S(1)}, bf16[1,80,2560]{2,1,0:T(8,128)(2,1)S(1)}, u32[]{:S(2)}, u32[]{:S(2)}) collective-permute-start(bf16[1,80,2560]{2,1,0:T(8,128)(2,1)S(1)} %copy-done.7), channel_id=1, source_target_pairs={{0,6},{1,7},{2,0},{3,1},{4,2},{5,3},{6,4},{7,5},{8,14},{9,15},{10,... | collective-permute-start | bytes 1228808 | tf_op jit(solution)/shard_map/ppermute | solution.py:407
  62.6 0.8 constant_dynamic-update-slice_fusion.rest_2_
  63.4 1.5 collective-permute-done.12
  64.9 0.8 constant_dynamic-update-slice_fusion.4.rest_4_
  66.2 1.9 collective-permute-done.20.rest_12_
  69.2 3.8 %collective-permute-done.21.rest_13_ = bf16[1,80,2560]{2,1,0:T(8,128)(2,1)S(1)} collective-permute-done((bf16[1,80,2560]{2,1,0:T(8,128)(2,1)S(1)}, bf16[1,80,2560]{2,1,0:T(8,128)(2,1)S(1)}, u32[]{:S(2)}, u32[]{:S(2)}) %collective-permute-start.21) | collective-permute-done | bytes 409632 | tf_op jit(solution)/shard_map/ppermute | solution.py:407
  73.0 1.5 collective-permute-start.16
  74.5 6.1 %collective-permute-done.18.rest_10_ = bf16[1,80,2560]{2,1,0:T(8,128)(2,1)} collective-permute-done((bf16[1,80,2560]{2,1,0:T(8,128)(2,1)S(1)}, bf16[1,80,2560]{2,1,0:T(8,128)(2,1)}, u32[]{:S(2)}, u32[]{:S(2)}) %collective-permute-start.18) | collective-permute-done | bytes 409632 | tf_op jit(solution)/shard_map/ppermute | solution.py:407
  80.6 4.1 %collective-permute-done.16.rest_8_ = bf16[1,80,2560]{2,1,0:T(8,128)(2,1)} collective-permute-done((bf16[1,80,2560]{2,1,0:T(8,128)(2,1)S(1)}, bf16[1,80,2560]{2,1,0:T(8,128)(2,1)}, u32[]{:S(2)}, u32[]{:S(2)}) %collective-permute-start.16) | collective-permute-done | bytes 409632 | tf_op jit(solution)/shard_map/ppermute | solution.py:407
  86.0 3.8 %left_factor.1.left = bf16[2,2,640,512]{3,2,1,0:T(8,128)(2,1)} custom-call(s32[3]{0:T(128)} %pad_add_fusion.where_ref, s32[8]{0:T(128)} %pad_add_fusion.1.kind_ref, bf16[4,1280,128]{2,1,0:T(8,128)(2,1)} %get-tuple-element.33.ht_a, bf16[4,1280,128]{2,1,0:T(8,128)(2,1)} %collective-permute-done.1.ht_b), custom_call_target="tpu_custom_call" | custom-call | bytes 12582912 | tf_op jit(solution)/shard_map/left_factor/pallas_call | solution.py:346
  89.9 20.6 %layer.1 = (bf16[4,640,128]{2,1,0:T(8,128)(2,1)}, bf16[4,128,640]{2,1,0:T(8,128)(2,1)}, bf16[4,128,640]{2,1,0:T(8,128)(2,1)}, bf16[4,128,640]{2,1,0:T(8,128)(2,1)}) custom-call(s32[3]{0:T(128)} %pad_add_fusion.where_ref, s32[4]{0:T(128)} %kind_ref.5, bf16[4,128,1280]{2,1,0:T(8,128)(2,1)} %get-tuple-element.34.h_ref, bf16[4,128,1280]{2,1,0:T(8,128)(2,1)} %cot_ref.3, ...), custom_call_target="tpu_custom_call" | custom-call | flops 10066329600 | bytes 20971520 | tf_op jit(solution)/shard_map/layer/pallas_call | solution.py:550
  111.3 1.9 collective-permute-done.22.attnt_b
  113.1 0.9 collective-permute-done.23.dv_b
  114.1 0.8 copy-done.17
  114.9 9.5 %first_terms.1 = (bf16[2,4,80,768]{3,2,1,0:T(8,128)(2,1)}, bf16[2,4,80,512]{3,2,1,0:T(8,128)(2,1)}, f32[4,80,1280]{2,1,0:T(8,128)}, f32[4,80,768]{2,1,0:T(8,128)}, f32[4,80,512]{2,1,0:T(8,128)}) custom-call(s32[3]{0:T(128)} %pad_add_fusion.where_ref, s32[8]{0:T(128)} %pad_add_fusion.1.kind_ref, bf16[2,2,640,512]{3,2,1,0:T(8,128)(2,1)} %left_factor.1.left, ...), custom_call_target="tpu_custom_call" | custom-call | flops 2516582400 | bytes 12582912 | tf_op jit(solution)/shard_map/first_terms/pallas_call | solution.py:359
  124.4 1.7 collective-permute-start.36
  126.6 15.2 %collective-permute-done.36 = bf16[2,4,80,512]{3,2,1,0:T(8,128)(2,1)} collective-permute-done((bf16[2,4,80,512]{3,2,1,0:T(8,128)(2,1)}, bf16[2,4,80,512]{3,2,1,0:T(8,128)(2,1)}, u32[]{:S(2)}, u32[]{:S(2)}) %collective-permute-start.36) | collective-permute-done | bytes 655392 | tf_op jit(solution)/shard_map/ppermute | solution.py:407
  141.8 2.0 fusion.3
  143.8 1.7 collective-permute-start.37
  145.5 3.6 %collective-permute-done.26 = bf16[2,4,80,768]{3,2,1,0:T(8,128)(2,1)S(1)} collective-permute-done((bf16[2,4,80,768]{3,2,1,0:T(8,128)(2,1)}, bf16[2,4,80,768]{3,2,1,0:T(8,128)(2,1)S(1)}, u32[]{:S(2)}, u32[]{:S(2)}) %collective-permute-start.26) | collective-permute-done | bytes 983072 | tf_op jit(solution)/shard_map/ppermute | solution.py:407
  149.1 0.9 fusion.1
  150.0 1.7 collective-permute-start.35
  151.7 8.5 %second_terms.1 = (bf16[2,4,80,768]{3,2,1,0:T(8,128)(2,1)}, bf16[2,4,80,512]{3,2,1,0:T(8,128)(2,1)}, f32[4,80,1280]{2,1,0:T(8,128)}, f32[4,80,768]{2,1,0:T(8,128)}, f32[4,80,512]{2,1,0:T(8,128)}) custom-call(bf16[2,2,640,512]{3,2,1,0:T(8,128)(2,1)} %left_factor.1.left, bf16[4,128,640]{2,1,0:T(8,128)(2,1)} %get-tuple-element.43.dk_a.dk_ref, ...), custom_call_target="tpu_custom_call" | custom-call | flops 3355443200 | bytes 12582912 | tf_op jit(solution)/shard_map/second_terms/pallas_call | solution.py:373
  160.6 1.1 convert_add_fusion.5
  161.7 1.6 collective-permute-done.35
  163.6 0.9 fusion.14
  165.0 1.5 collective-permute-start.40
  166.5 2.2 collective-permute-start.39
  168.7 17.1 %result.1 = (bf16[4,128,1280]{2,1,0:T(8,128)(2,1)}, bf16[4,128,1280]{2,1,0:T(8,128)(2,1)}) custom-call(s32[3]{0:T(128)} %pad_add_fusion.where_ref, s32[4]{0:T(128)} %kind_ref.5, s32[4]{0:T(128)} %rank_ref.1, bf16[4,128,1280]{2,1,0:T(8,128)(2,1)} %x_ref.3, bf16[4,128,1280]{2,1,0:T(8,128)(2,1)} %cot_ref.3, f32[2,1280]{1,0:T(2,128)} %bitcast.90, ...), custom_call_target="tpu_custom_call" | custom-call | flops 3355443200 | bytes 20971520 | tf_op jit(solution)/shard_map/result/pallas_call | solution.py:595
  185.8 1.3 collective-permute-start.27
  187.2 1.0 fusion.22
  188.2 2.4 %collective-permute-start.41 = (bf16[80,1280]{1,0:T(8,128)(2,1)S(1)}, bf16[80,1280]{1,0:T(8,128)(2,1)S(1)}, u32[]{:S(2)}, u32[]{:S(2)}) collective-permute-start(bf16[80,1280]{1,0:T(8,128)(2,1)S(1)} %get-tuple-element.61), channel_id=1, source_target_pairs={{0,8},{1,9},{2,10},{3,11},{4,12},{5,13},{6,14},{7,15},{8,0},{9,1},... | collective-permute-start | bytes 614408 | tf_op jit(solution)/shard_map/ppermute | solution.py:407
  191.5 2.9 %collective-permute-done.41 = bf16[80,1280]{1,0:T(8,128)(2,1)S(1)} collective-permute-done((bf16[80,1280]{1,0:T(8,128)(2,1)S(1)}, bf16[80,1280]{1,0:T(8,128)(2,1)S(1)}, u32[]{:S(2)}, u32[]{:S(2)}) %collective-permute-start.41) | collective-permute-done | bytes 204832 | tf_op jit(solution)/shard_map/ppermute | solution.py:407
  194.4 16.2 %collective-permute-done.27 = bf16[2,4,80,768]{3,2,1,0:T(8,128)(2,1)S(1)} collective-permute-done((bf16[2,4,80,768]{3,2,1,0:T(8,128)(2,1)}, bf16[2,4,80,768]{3,2,1,0:T(8,128)(2,1)S(1)}, u32[]{:S(2)}, u32[]{:S(2)}) %collective-permute-start.27) | collective-permute-done | bytes 983072 | tf_op jit(solution)/shard_map/ppermute | solution.py:407
  210.8 1.5 collective-permute-start.28
  212.3 1.8 collective-permute-done.30
  214.3 5.4 %collective-permute-done.28 = bf16[4,80,768]{2,1,0:T(8,128)(2,1)S(1)} collective-permute-done((bf16[4,80,768]{2,1,0:T(8,128)(2,1)S(1)}, bf16[4,80,768]{2,1,0:T(8,128)(2,1)S(1)}, u32[]{:S(2)}, u32[]{:S(2)}) %collective-permute-start.28) | collective-permute-done | bytes 491552 | tf_op jit(solution)/shard_map/ppermute | solution.py:407
  220.1 2.7 %collective-permute-start.31 = (bf16[80,1280]{1,0:T(8,128)(2,1)S(1)}, bf16[80,1280]{1,0:T(8,128)(2,1)S(1)}, u32[]{:S(2)}, u32[]{:S(2)}) collective-permute-start(bf16[80,1280]{1,0:T(8,128)(2,1)S(1)} %get-tuple-element.63), channel_id=1, source_target_pairs={{0,2},{1,3},{2,4},{3,5},{4,6},{5,7},{6,0},{7,1},{8,10},{9,11},{10,... | collective-permute-start | bytes 614408 | tf_op jit(solution)/shard_map/ppermute | solution.py:407
  222.7 1.5 collective-permute-start.32
  224.3 6.4 %collective-permute-done.31 = bf16[80,1280]{1,0:T(8,128)(2,1)S(1)} collective-permute-done((bf16[80,1280]{1,0:T(8,128)(2,1)S(1)}, bf16[80,1280]{1,0:T(8,128)(2,1)S(1)}, u32[]{:S(2)}, u32[]{:S(2)}) %collective-permute-start.31) | collective-permute-done | bytes 204832 | tf_op jit(solution)/shard_map/ppermute | solution.py:407
  230.6 1.9 collective-permute-done.33
  232.9 1.2 collective-permute-start.34
  234.9 3.8 %collective-permute-done.34 = bf16[80,1280]{1,0:T(8,128)(2,1)S(1)} collective-permute-done((bf16[80,1280]{1,0:T(8,128)(2,1)S(1)}, bf16[80,1280]{1,0:T(8,128)(2,1)S(1)}, u32[]{:S(2)}, u32[]{:S(2)}) %collective-permute-start.34) | collective-permute-done | bytes 204832 | tf_op jit(solution)/shard_map/ppermute | solution.py:407
  238.9 1.1 fusion.19
  (105 shorter events, 12.1 us)
Async XLA Ops:
  0.6 1.5 copy-start
  1.9 2.7 %copy-start.14 = (bf16[2,160]{1,0:T(2,128)(2,1)S(1)}, bf16[2,160]{1,0:T(2,128)(2,1)}, u32[]{:S(2)}) copy-start(bf16[2,160]{1,0:T(2,128)(2,1)} %param.13) | copy-start | bytes 1924
  2.9 21.4 %copy-start.8 = (bf16[1,80,2560]{2,1,0:T(8,128)(2,1)}, bf16[1,80,2560]{2,1,0:T(8,128)(2,1)S(1)}, u32[]{:S(2)}) copy-start(bf16[1,80,2560]{2,1,0:T(8,128)(2,1)S(1)} %get-tuple-element.36) | copy-start | bytes 1228804
  2.9 21.4 %collective-permute-start.4 = (bf16[1,80,2560]{2,1,0:T(8,128)(2,1)S(1)}, bf16[1,80,2560]{2,1,0:T(8,128)(2,1)}, u32[]{:S(2)}, u32[]{:S(2)}) collective-permute-start(bf16[1,80,2560]{2,1,0:T(8,128)(2,1)S(1)} %get-tuple-element.36), channel_id=1, source_target_pairs={{0,2},{1,3},{2,4},{3,5},{4,6},{5,7},{6,0},{7,1},{8,10},{9,11},{10,... | collective-permute-start | bytes 1228808 | tf_op jit(solution)/shard_map/ppermute | solution.py:407
  4.5 64.1 %collective-permute-start.2 = (bf16[4,128,1280]{2,1,0:T(8,128)(2,1)}, bf16[4,128,1280]{2,1,0:T(8,128)(2,1)}, u32[]{:S(2)}, u32[]{:S(2)}) collective-permute-start(bf16[4,128,1280]{2,1,0:T(8,128)(2,1)} %cot_ref.3), channel_id=1, source_target_pairs={{0,1},{1,0},{2,3},{3,2},{4,5},{5,4},{6,7},{7,6},{8,9},{9,8},{10,11... | collective-permute-start | bytes 3932168 | tf_op jit(solution)/shard_map/ppermute | solution.py:407
  24.0 0.7 copy-start.15
  24.0 44.6 %collective-permute-start.1 = (bf16[4,1280,128]{2,1,0:T(8,128)(2,1)}, bf16[4,1280,128]{2,1,0:T(8,128)(2,1)}, u32[]{:S(2)}, u32[]{:S(2)}) collective-permute-start(bf16[4,1280,128]{2,1,0:T(8,128)(2,1)} %get-tuple-element.33.ht_a), channel_id=1, source_target_pairs={{0,1},{1,0},{2,3},{3,2},{4,5},{5,4},{6,7},{7,6},{8,9},{9,8},{10,11... | collective-permute-start | bytes 3932168 | tf_op jit(solution)/shard_map/ppermute | solution.py:407
  24.3 12.5 %collective-permute-start.9 = (bf16[1,80,2560]{2,1,0:T(8,128)(2,1)}, bf16[1,80,2560]{2,1,0:T(8,128)(2,1)S(1)}, u32[]{:S(2)}, u32[]{:S(2)}) collective-permute-start(bf16[1,80,2560]{2,1,0:T(8,128)(2,1)} %collective-permute-done.4), channel_id=1, source_target_pairs={{0,2},{1,3},{2,4},{3,5},{4,6},{5,7},{6,0},{7,1},{8,10},{9,11},{10,... | collective-permute-start | bytes 1228808 | tf_op jit(solution)/shard_map/ppermute | solution.py:407
  24.3 1.0 copy-start.9
  24.6 41.4 %copy-start.1 = (bf16[4,80,2560]{2,1,0:T(8,128)(2,1)}, bf16[4,80,2560]{2,1,0:T(8,128)(2,1)S(1)}, u32[]{:S(2)}) copy-start(bf16[4,80,2560]{2,1,0:T(8,128)(2,1)S(1)} %pad_maximum_fusion.rest_0_) | copy-start | bytes 4915204
  25.3 33.6 %collective-permute-start.14 = (bf16[1,80,2560]{2,1,0:T(8,128)(2,1)S(1)}, bf16[1,80,2560]{2,1,0:T(8,128)(2,1)S(1)}, u32[]{:S(2)}, u32[]{:S(2)}) collective-permute-start(bf16[1,80,2560]{2,1,0:T(8,128)(2,1)S(1)} %copy-done.9), channel_id=1, source_target_pairs={{0,6},{1,7},{2,0},{3,1},{4,2},{5,3},{6,4},{7,5},{8,14},{9,15},{10,... | collective-permute-start | bytes 1228808 | tf_op jit(solution)/shard_map/ppermute | solution.py:407
  27.3 11.8 %collective-permute-start.5 = (bf16[1,80,2560]{2,1,0:T(8,128)(2,1)}, bf16[1,80,2560]{2,1,0:T(8,128)(2,1)S(1)}, u32[]{:S(2)}, u32[]{:S(2)}) collective-permute-start(bf16[1,80,2560]{2,1,0:T(8,128)(2,1)} %collective-permute-done.4), channel_id=1, source_target_pairs={{0,8},{1,9},{2,10},{3,11},{4,12},{5,13},{6,14},{7,15},{8,0},{9,1},... | collective-permute-start | bytes 1228808 | tf_op jit(solution)/shard_map/ppermute | solution.py:407
  36.8 10.2 %collective-permute-start.6 = (bf16[1,80,2560]{2,1,0:T(8,128)(2,1)}, bf16[1,80,2560]{2,1,0:T(8,128)(2,1)S(1)}, u32[]{:S(2)}, u32[]{:S(2)}) collective-permute-start(bf16[1,80,2560]{2,1,0:T(8,128)(2,1)} %collective-permute-done.4), channel_id=1, source_target_pairs={{0,16},{1,17},{2,18},{3,19},{4,20},{5,21},{6,22},{7,23},{8,24},{9,... | collective-permute-start | bytes 1228808 | tf_op jit(solution)/shard_map/ppermute | solution.py:407
  39.1 10.2 %collective-permute-start.10 = (bf16[1,80,2560]{2,1,0:T(8,128)(2,1)S(1)}, bf16[1,80,2560]{2,1,0:T(8,128)(2,1)S(1)}, u32[]{:S(2)}, u32[]{:S(2)}) collective-permute-start(bf16[1,80,2560]{2,1,0:T(8,128)(2,1)S(1)} %collective-permute-done.9), channel_id=1, source_target_pairs={{0,8},{1,9},{2,10},{3,11},{4,12},{5,13},{6,14},{7,15},{8,0},{9,1},... | collective-permute-start | bytes 1228808 | tf_op jit(solution)/shard_map/ppermute | solution.py:407
  41.4 17.5 %copy-start.7 = (bf16[1,80,2560]{2,1,0:T(8,128)(2,1)S(1)}, bf16[1,80,2560]{2,1,0:T(8,128)(2,1)}, u32[]{:S(2)}) copy-start(bf16[1,80,2560]{2,1,0:T(8,128)(2,1)} %get-tuple-element.38) | copy-start | bytes 1228804
  47.0 9.6 %collective-permute-start.11 = (bf16[1,80,2560]{2,1,0:T(8,128)(2,1)S(1)}, bf16[1,80,2560]{2,1,0:T(8,128)(2,1)S(1)}, u32[]{:S(2)}, u32[]{:S(2)}) collective-permute-start(bf16[1,80,2560]{2,1,0:T(8,128)(2,1)S(1)} %collective-permute-done.9), channel_id=1, source_target_pairs={{0,16},{1,17},{2,18},{3,19},{4,20},{5,21},{6,22},{7,23},{8,24},{9,... | collective-permute-start | bytes 1228808 | tf_op jit(solution)/shard_map/ppermute | solution.py:407
  49.3 13.2 %collective-permute-start.7 = (bf16[1,80,2560]{2,1,0:T(8,128)(2,1)S(1)}, bf16[1,80,2560]{2,1,0:T(8,128)(2,1)S(1)}, u32[]{:S(2)}, u32[]{:S(2)}) collective-permute-start(bf16[1,80,2560]{2,1,0:T(8,128)(2,1)S(1)} %collective-permute-done.6), channel_id=1, source_target_pairs={{0,8},{1,9},{2,10},{3,11},{4,12},{5,13},{6,14},{7,15},{8,0},{9,1},... | collective-permute-start | bytes 1228808 | tf_op jit(solution)/shard_map/ppermute | solution.py:407
  56.7 8.2 %collective-permute-start.12 = (bf16[1,80,2560]{2,1,0:T(8,128)(2,1)S(1)}, bf16[1,80,2560]{2,1,0:T(8,128)(2,1)S(1)}, u32[]{:S(2)}, u32[]{:S(2)}) collective-permute-start(bf16[1,80,2560]{2,1,0:T(8,128)(2,1)S(1)} %collective-permute-done.10), channel_id=1, source_target_pairs={{0,16},{1,17},{2,18},{3,19},{4,20},{5,21},{6,22},{7,23},{8,24},{9,... | collective-permute-start | bytes 1228808 | tf_op jit(solution)/shard_map/ppermute | solution.py:407
  59.0 30.9 %copy-start.10 = (bf16[1,80,2560]{2,1,0:T(8,128)(2,1)}, bf16[1,80,2560]{2,1,0:T(8,128)(2,1)S(1)}, u32[]{:S(2)}) copy-start(bf16[1,80,2560]{2,1,0:T(8,128)(2,1)S(1)} %collective-permute-done.14.rest_6_) | copy-start | bytes 1228804
  59.0 9.1 %collective-permute-start.20 = (bf16[1,80,2560]{2,1,0:T(8,128)(2,1)S(1)}, bf16[1,80,2560]{2,1,0:T(8,128)(2,1)S(1)}, u32[]{:S(2)}, u32[]{:S(2)}) collective-permute-start(bf16[1,80,2560]{2,1,0:T(8,128)(2,1)S(1)} %copy-done.7), channel_id=1, source_target_pairs={{0,6},{1,7},{2,0},{3,1},{4,2},{5,3},{6,4},{7,5},{8,14},{9,15},{10,... | collective-permute-start | bytes 1228808 | tf_op jit(solution)/shard_map/ppermute | solution.py:407
  62.6 5.5 %collective-permute-start.15 = (bf16[1,80,2560]{2,1,0:T(8,128)(2,1)S(1)}, bf16[1,80,2560]{2,1,0:T(8,128)(2,1)S(1)}, u32[]{:S(2)}, u32[]{:S(2)}) collective-permute-start(bf16[1,80,2560]{2,1,0:T(8,128)(2,1)S(1)} %collective-permute-done.14.rest_6_), channel_id=1, source_target_pairs={{0,1},{1,0},{2,3},{3,2},{4,5},{5,4},{6,7},{7,6},{8,9},{9,8},{10,11... | collective-permute-start | bytes 1228808 | tf_op jit(solution)/shard_map/ppermute | solution.py:407
  64.9 1.1 collective-permute-start
  66.0 23.8 %collective-permute-start.3 = (bf16[4,80,2560]{2,1,0:T(8,128)(2,1)S(1)}, bf16[4,80,2560]{2,1,0:T(8,128)(2,1)}, u32[]{:S(2)}, u32[]{:S(2)}) collective-permute-start(bf16[4,80,2560]{2,1,0:T(8,128)(2,1)S(1)} %pad_maximum_fusion.rest_0_), channel_id=1, source_target_pairs={{0,1},{1,0},{2,3},{3,2},{4,5},{5,4},{6,7},{7,6},{8,9},{9,8},{10,11... | collective-permute-start | bytes 4915208 | tf_op jit(solution)/shard_map/ppermute | solution.py:407
  68.1 16.6 %copy-start.11 = (bf16[1,80,2560]{2,1,0:T(8,128)(2,1)}, bf16[1,80,2560]{2,1,0:T(8,128)(2,1)S(1)}, u32[]{:S(2)}) copy-start(bf16[1,80,2560]{2,1,0:T(8,128)(2,1)S(1)} %collective-permute-done.20.rest_12_) | copy-start | bytes 1228804
  68.1 21.8 %collective-permute-start.8 = (bf16[4,80,2560]{2,1,0:T(8,128)(2,1)}, bf16[4,80,2560]{2,1,0:T(8,128)(2,1)}, u32[]{:S(2)}, u32[]{:S(2)}) collective-permute-start(bf16[4,80,2560]{2,1,0:T(8,128)(2,1)} %constant_dynamic-update-slice_fusion.rest_2_), channel_id=1, source_target_pairs={{0,1},{1,0},{2,3},{3,2},{4,5},{5,4},{6,7},{7,6},{8,9},{9,8},{10,11... | collective-permute-start | bytes 4915208 | tf_op jit(solution)/shard_map/ppermute | solution.py:407
  68.1 16.6 %copy-start.12 = (bf16[1,80,2560]{2,1,0:T(8,128)(2,1)}, bf16[1,80,2560]{2,1,0:T(8,128)(2,1)S(1)}, u32[]{:S(2)}) copy-start(bf16[1,80,2560]{2,1,0:T(8,128)(2,1)S(1)} %collective-permute-done.15.rest_7_) | copy-start | bytes 1228804
  68.1 21.8 %collective-permute-start.13 = (bf16[4,80,2560]{2,1,0:T(8,128)(2,1)}, bf16[4,80,2560]{2,1,0:T(8,128)(2,1)}, u32[]{:S(2)}, u32[]{:S(2)}) collective-permute-start(bf16[4,80,2560]{2,1,0:T(8,128)(2,1)} %constant_dynamic-update-slice_fusion.4.rest_4_), channel_id=1, source_target_pairs={{0,1},{1,0},{2,3},{3,2},{4,5},{5,4},{6,7},{7,6},{8,9},{9,8},{10,11... | collective-permute-start | bytes 4915208 | tf_op jit(solution)/shard_map/ppermute | solution.py:407
  68.6 4.4 %collective-permute-start.21 = (bf16[1,80,2560]{2,1,0:T(8,128)(2,1)S(1)}, bf16[1,80,2560]{2,1,0:T(8,128)(2,1)S(1)}, u32[]{:S(2)}, u32[]{:S(2)}) collective-permute-start(bf16[1,80,2560]{2,1,0:T(8,128)(2,1)S(1)} %collective-permute-done.20.rest_12_), channel_id=1, source_target_pairs={{0,1},{1,0},{2,3},{3,2},{4,5},{5,4},{6,7},{7,6},{8,9},{9,8},{10,11... | collective-permute-start | bytes 1228808 | tf_op jit(solution)/shard_map/ppermute | solution.py:407
  68.7 11.9 %collective-permute-start.18 = (bf16[1,80,2560]{2,1,0:T(8,128)(2,1)S(1)}, bf16[1,80,2560]{2,1,0:T(8,128)(2,1)}, u32[]{:S(2)}, u32[]{:S(2)}) collective-permute-start(bf16[1,80,2560]{2,1,0:T(8,128)(2,1)S(1)} %collective-permute-done.14.rest_6_), channel_id=1, source_target_pairs={{0,16},{1,17},{2,18},{3,19},{4,20},{5,21},{6,22},{7,23},{8,24},{9,... | collective-permute-start | bytes 1228808 | tf_op jit(solution)/shard_map/ppermute | solution.py:407
  73.0 11.7 %copy-start.13 = (bf16[1,80,2560]{2,1,0:T(8,128)(2,1)}, bf16[1,80,2560]{2,1,0:T(8,128)(2,1)S(1)}, u32[]{:S(2)}) copy-start(bf16[1,80,2560]{2,1,0:T(8,128)(2,1)S(1)} %collective-permute-done.21.rest_13_) | copy-start | bytes 1228804
  73.0 11.7 %collective-permute-start.16 = (bf16[1,80,2560]{2,1,0:T(8,128)(2,1)S(1)}, bf16[1,80,2560]{2,1,0:T(8,128)(2,1)}, u32[]{:S(2)}, u32[]{:S(2)}) collective-permute-start(bf16[1,80,2560]{2,1,0:T(8,128)(2,1)S(1)} %collective-permute-done.14.rest_6_), channel_id=1, source_target_pairs={{0,8},{1,9},{2,10},{3,11},{4,12},{5,13},{6,14},{7,15},{8,0},{9,1},... | collective-permute-start | bytes 1228808 | tf_op jit(solution)/shard_map/ppermute | solution.py:407
  80.6 9.3 %collective-permute-start.19 = (bf16[1,80,2560]{2,1,0:T(8,128)(2,1)}, bf16[1,80,2560]{2,1,0:T(8,128)(2,1)}, u32[]{:S(2)}, u32[]{:S(2)}) collective-permute-start(bf16[1,80,2560]{2,1,0:T(8,128)(2,1)} %collective-permute-done.18.rest_10_), channel_id=1, source_target_pairs={{0,1},{1,0},{2,3},{3,2},{4,5},{5,4},{6,7},{7,6},{8,9},{9,8},{10,11... | collective-permute-start | bytes 1228808 | tf_op jit(solution)/shard_map/ppermute | solution.py:407
  84.7 5.1 %collective-permute-start.17 = (bf16[1,80,2560]{2,1,0:T(8,128)(2,1)}, bf16[1,80,2560]{2,1,0:T(8,128)(2,1)}, u32[]{:S(2)}, u32[]{:S(2)}) collective-permute-start(bf16[1,80,2560]{2,1,0:T(8,128)(2,1)} %collective-permute-done.16.rest_8_), channel_id=1, source_target_pairs={{0,1},{1,0},{2,3},{3,2},{4,5},{5,4},{6,7},{7,6},{8,9},{9,8},{10,11... | collective-permute-start | bytes 1228808 | tf_op jit(solution)/shard_map/ppermute | solution.py:407
  110.5 2.6 %collective-permute-start.22 = (bf16[4,640,128]{2,1,0:T(8,128)(2,1)}, bf16[4,640,128]{2,1,0:T(8,128)(2,1)S(1)}, u32[]{:S(2)}, u32[]{:S(2)}) collective-permute-start(bf16[4,640,128]{2,1,0:T(8,128)(2,1)} %get-tuple-element.46.attnt_a.attnt_ref), channel_id=1, source_target_pairs={{0,1},{1,0},{2,3},{3,2},{4,5},{5,4},{6,7},{7,6},{8,9},{9,8},{10,11... | collective-permute-start | bytes 1966088 | tf_op jit(solution)/shard_map/ppermute | solution.py:407
  111.2 2.9 %collective-permute-start.23 = (bf16[4,128,640]{2,1,0:T(8,128)(2,1)}, bf16[4,128,640]{2,1,0:T(8,128)(2,1)S(1)}, u32[]{:S(2)}, u32[]{:S(2)}) collective-permute-start(bf16[4,128,640]{2,1,0:T(8,128)(2,1)} %get-tuple-element.41.dv_a.dv_ref), channel_id=1, source_target_pairs={{0,1},{1,0},{2,3},{3,2},{4,5},{5,4},{6,7},{7,6},{8,9},{9,8},{10,11... | collective-permute-start | bytes 1966088 | tf_op jit(solution)/shard_map/ppermute | solution.py:407
  113.1 0.9 copy-start.16
  114.1 0.8 copy-start.17
  124.4 24.8 %copy-start.4 = (f32[4,80,768]{2,1,0:T(8,128)S(1)}, f32[4,80,768]{2,1,0:T(8,128)}, u32[]{:S(2)}) copy-start(f32[4,80,768]{2,1,0:T(8,128)} %get-tuple-element.56) | copy-start | bytes 2949124
  124.4 24.8 %collective-permute-start.26 = (bf16[2,4,80,768]{3,2,1,0:T(8,128)(2,1)}, bf16[2,4,80,768]{3,2,1,0:T(8,128)(2,1)S(1)}, u32[]{:S(2)}, u32[]{:S(2)}) collective-permute-start(bf16[2,4,80,768]{3,2,1,0:T(8,128)(2,1)} %get-tuple-element.42), channel_id=1, source_target_pairs={{0,16},{1,17},{2,18},{3,19},{4,20},{5,21},{6,22},{7,23},{8,24},{9,... | collective-permute-start | bytes 2949128 | tf_op jit(solution)/shard_map/ppermute | solution.py:407
  124.4 17.5 %collective-permute-start.36 = (bf16[2,4,80,512]{3,2,1,0:T(8,128)(2,1)}, bf16[2,4,80,512]{3,2,1,0:T(8,128)(2,1)}, u32[]{:S(2)}, u32[]{:S(2)}) collective-permute-start(bf16[2,4,80,512]{3,2,1,0:T(8,128)(2,1)} %get-tuple-element.57), channel_id=1, source_target_pairs={{0,8},{1,9},{2,10},{3,11},{4,12},{5,13},{6,14},{7,15},{8,0},{9,1},... | collective-permute-start | bytes 1966088 | tf_op jit(solution)/shard_map/ppermute | solution.py:407
  126.1 25.6 %collective-permute-start.24 = (bf16[4,128,640]{2,1,0:T(8,128)(2,1)}, bf16[4,128,640]{2,1,0:T(8,128)(2,1)}, u32[]{:S(2)}, u32[]{:S(2)}) collective-permute-start(bf16[4,128,640]{2,1,0:T(8,128)(2,1)} %get-tuple-element.43.dk_a.dk_ref), channel_id=1, source_target_pairs={{0,1},{1,0},{2,3},{3,2},{4,5},{5,4},{6,7},{7,6},{8,9},{9,8},{10,11... | collective-permute-start | bytes 1966088 | tf_op jit(solution)/shard_map/ppermute | solution.py:407
  126.2 25.5 %collective-permute-start.25 = (bf16[4,128,640]{2,1,0:T(8,128)(2,1)}, bf16[4,128,640]{2,1,0:T(8,128)(2,1)}, u32[]{:S(2)}, u32[]{:S(2)}) collective-permute-start(bf16[4,128,640]{2,1,0:T(8,128)(2,1)} %get-tuple-element.44.dq_a.dq_ref), channel_id=1, source_target_pairs={{0,1},{1,0},{2,3},{3,2},{4,5},{5,4},{6,7},{7,6},{8,9},{9,8},{10,11... | collective-permute-start | bytes 1966088 | tf_op jit(solution)/shard_map/ppermute | solution.py:407
  143.8 16.8 %collective-permute-start.37 = (bf16[4,80,512]{2,1,0:T(8,128)(2,1)}, bf16[4,80,512]{2,1,0:T(8,128)(2,1)S(1)}, u32[]{:S(2)}, u32[]{:S(2)}) collective-permute-start(bf16[4,80,512]{2,1,0:T(8,128)(2,1)} %fusion.3), channel_id=1, source_target_pairs={{0,16},{1,17},{2,18},{3,19},{4,20},{5,21},{6,22},{7,23},{8,24},{9,... | collective-permute-start | bytes 983048 | tf_op jit(solution)/shard_map/ppermute | solution.py:407
  150.0 13.3 %collective-permute-start.35 = (bf16[4,80,768]{2,1,0:T(8,128)(2,1)}, bf16[4,80,768]{2,1,0:T(8,128)(2,1)S(1)}, u32[]{:S(2)}, u32[]{:S(2)}) collective-permute-start(bf16[4,80,768]{2,1,0:T(8,128)(2,1)} %fusion.1), channel_id=1, source_target_pairs={{0,8},{1,9},{2,10},{3,11},{4,12},{5,13},{6,14},{7,15},{8,0},{9,1},... | collective-permute-start | bytes 1474568 | tf_op jit(solution)/shard_map/ppermute | solution.py:407
  160.3 30.4 %collective-permute-start.29 = (bf16[2,4,80,512]{3,2,1,0:T(8,128)(2,1)}, bf16[2,4,80,512]{3,2,1,0:T(8,128)(2,1)S(1)}, u32[]{:S(2)}, u32[]{:S(2)}) collective-permute-start(bf16[2,4,80,512]{3,2,1,0:T(8,128)(2,1)} %get-tuple-element.53), channel_id=1, source_target_pairs={{0,8},{1,9},{2,10},{3,11},{4,12},{5,13},{6,14},{7,15},{8,0},{9,1},... | collective-permute-start | bytes 1966088 | tf_op jit(solution)/shard_map/ppermute | solution.py:407
  161.7 1.7 copy-start.2
  164.5 22.7 %collective-permute-start.38 = (bf16[80,1280]{1,0:T(8,128)(2,1)}, bf16[80,1280]{1,0:T(8,128)(2,1)S(1)}, u32[]{:S(2)}, u32[]{:S(2)}) collective-permute-start(bf16[80,1280]{1,0:T(8,128)(2,1)} %get-tuple-element.66), channel_id=1, source_target_pairs={{0,2},{1,3},{2,4},{3,5},{4,6},{5,7},{6,0},{7,1},{8,10},{9,11},{10,... | collective-permute-start | bytes 614408 | tf_op jit(solution)/shard_map/ppermute | solution.py:407
  165.0 22.2 %collective-permute-start.40 = (bf16[80,1280]{1,0:T(8,128)(2,1)}, bf16[80,1280]{1,0:T(8,128)(2,1)S(1)}, u32[]{:S(2)}, u32[]{:S(2)}) collective-permute-start(bf16[80,1280]{1,0:T(8,128)(2,1)} %get-tuple-element.67), channel_id=1, source_target_pairs={{0,6},{1,7},{2,0},{3,1},{4,2},{5,3},{6,4},{7,5},{8,14},{9,15},{10,... | collective-permute-start | bytes 614408 | tf_op jit(solution)/shard_map/ppermute | solution.py:407
  166.5 20.7 %collective-permute-start.39 = (bf16[80,1280]{1,0:T(8,128)(2,1)}, bf16[80,1280]{1,0:T(8,128)(2,1)}, u32[]{:S(2)}, u32[]{:S(2)}) collective-permute-start(bf16[80,1280]{1,0:T(8,128)(2,1)} %get-tuple-element.68), channel_id=1, source_target_pairs={{0,4},{1,5},{2,6},{3,7},{4,0},{5,1},{6,2},{7,3},{8,12},{9,13},{10,... | collective-permute-start | bytes 614408 | tf_op jit(solution)/shard_map/ppermute | solution.py:407
  185.8 4.8 %copy-start.6 = (f32[4,80,512]{2,1,0:T(8,128)S(1)}, f32[4,80,512]{2,1,0:T(8,128)}, u32[]{:S(2)}) copy-start(f32[4,80,512]{2,1,0:T(8,128)} %get-tuple-element.54) | copy-start | bytes 1966084
  185.8 24.8 %collective-permute-start.27 = (bf16[2,4,80,768]{3,2,1,0:T(8,128)(2,1)}, bf16[2,4,80,768]{3,2,1,0:T(8,128)(2,1)S(1)}, u32[]{:S(2)}, u32[]{:S(2)}) collective-permute-start(bf16[2,4,80,768]{3,2,1,0:T(8,128)(2,1)} %get-tuple-element.51), channel_id=1, source_target_pairs={{0,16},{1,17},{2,18},{3,19},{4,20},{5,21},{6,22},{7,23},{8,24},{9,... | collective-permute-start | bytes 2949128 | tf_op jit(solution)/shard_map/ppermute | solution.py:407
  188.2 6.2 %collective-permute-start.41 = (bf16[80,1280]{1,0:T(8,128)(2,1)S(1)}, bf16[80,1280]{1,0:T(8,128)(2,1)S(1)}, u32[]{:S(2)}, u32[]{:S(2)}) collective-permute-start(bf16[80,1280]{1,0:T(8,128)(2,1)S(1)} %get-tuple-element.61), channel_id=1, source_target_pairs={{0,8},{1,9},{2,10},{3,11},{4,12},{5,13},{6,14},{7,15},{8,0},{9,1},... | collective-permute-start | bytes 614408 | tf_op jit(solution)/shard_map/ppermute | solution.py:407
  190.6 20.0 %copy-start.5 = (f32[4,80,768]{2,1,0:T(8,128)S(1)}, f32[4,80,768]{2,1,0:T(8,128)}, u32[]{:S(2)}) copy-start(f32[4,80,768]{2,1,0:T(8,128)} %get-tuple-element.52) | copy-start | bytes 2949124
  190.7 23.5 %collective-permute-start.30 = (bf16[4,80,512]{2,1,0:T(8,128)(2,1)S(1)}, bf16[4,80,512]{2,1,0:T(8,128)(2,1)S(1)}, u32[]{:S(2)}, u32[]{:S(2)}) collective-permute-start(bf16[4,80,512]{2,1,0:T(8,128)(2,1)S(1)} %fusion.4), channel_id=1, source_target_pairs={{0,16},{1,17},{2,18},{3,19},{4,20},{5,21},{6,22},{7,23},{8,24},{9,... | collective-permute-start | bytes 983048 | tf_op jit(solution)/shard_map/ppermute | solution.py:407
  210.8 8.9 %collective-permute-start.28 = (bf16[4,80,768]{2,1,0:T(8,128)(2,1)S(1)}, bf16[4,80,768]{2,1,0:T(8,128)(2,1)S(1)}, u32[]{:S(2)}, u32[]{:S(2)}) collective-permute-start(bf16[4,80,768]{2,1,0:T(8,128)(2,1)S(1)} %fusion.2), channel_id=1, source_target_pairs={{0,8},{1,9},{2,10},{3,11},{4,12},{5,13},{6,14},{7,15},{8,0},{9,1},... | collective-permute-start | bytes 1474568 | tf_op jit(solution)/shard_map/ppermute | solution.py:407
  214.3 5.5 %copy-start.3 = (f32[4,80,1280]{2,1,0:T(8,128)S(1)}, f32[4,80,1280]{2,1,0:T(8,128)}, u32[]{:S(2)}) copy-start(f32[4,80,1280]{2,1,0:T(8,128)} %get-tuple-element.49) | copy-start | bytes 4915204
  220.1 10.6 %collective-permute-start.31 = (bf16[80,1280]{1,0:T(8,128)(2,1)S(1)}, bf16[80,1280]{1,0:T(8,128)(2,1)S(1)}, u32[]{:S(2)}, u32[]{:S(2)}) collective-permute-start(bf16[80,1280]{1,0:T(8,128)(2,1)S(1)} %get-tuple-element.63), channel_id=1, source_target_pairs={{0,2},{1,3},{2,4},{3,5},{4,6},{5,7},{6,0},{7,1},{8,10},{9,11},{10,... | collective-permute-start | bytes 614408 | tf_op jit(solution)/shard_map/ppermute | solution.py:407
  222.7 9.8 %collective-permute-start.33 = (bf16[80,1280]{1,0:T(8,128)(2,1)S(1)}, bf16[80,1280]{1,0:T(8,128)(2,1)S(1)}, u32[]{:S(2)}, u32[]{:S(2)}) collective-permute-start(bf16[80,1280]{1,0:T(8,128)(2,1)S(1)} %get-tuple-element.64), channel_id=1, source_target_pairs={{0,6},{1,7},{2,0},{3,1},{4,2},{5,3},{6,4},{7,5},{8,14},{9,15},{10,... | collective-permute-start | bytes 614408 | tf_op jit(solution)/shard_map/ppermute | solution.py:407
  222.7 10.1 %collective-permute-start.32 = (bf16[80,1280]{1,0:T(8,128)(2,1)S(1)}, bf16[80,1280]{1,0:T(8,128)(2,1)S(1)}, u32[]{:S(2)}, u32[]{:S(2)}) collective-permute-start(bf16[80,1280]{1,0:T(8,128)(2,1)S(1)} %get-tuple-element.65), channel_id=1, source_target_pairs={{0,4},{1,5},{2,6},{3,7},{4,0},{5,1},{6,2},{7,3},{8,12},{9,13},{10,... | collective-permute-start | bytes 614408 | tf_op jit(solution)/shard_map/ppermute | solution.py:407
  232.9 5.8 %collective-permute-start.34 = (bf16[80,1280]{1,0:T(8,128)(2,1)S(1)}, bf16[80,1280]{1,0:T(8,128)(2,1)S(1)}, u32[]{:S(2)}, u32[]{:S(2)}) collective-permute-start(bf16[80,1280]{1,0:T(8,128)(2,1)S(1)} %get-tuple-element.59), channel_id=1, source_target_pairs={{0,8},{1,9},{2,10},{3,11},{4,12},{5,13},{6,14},{7,15},{8,0},{9,1},... | collective-permute-start | bytes 614408 | tf_op jit(solution)/shard_map/ppermute | solution.py:407

commit v2 on v1

v2 whole, which is shorter than its diff:
```python
import functools
import math

import jax
import jax.numpy as jnp
from jax import lax
from jax.experimental import pallas as pl
from jax.experimental.pallas import tpu as pltpu
from jax.sharding import PartitionSpec as P

A_HEADS = 10
A_SIZE = 64
V_HEADS = 8
V_SIZE = 80
VWIN = 64
EPSILON = 1e-05
LANES = 128
AXES = ("grp", "dp")
VMEM_LIMIT = 60 * 1024 * 1024
BF16 = jnp.bfloat16
F32 = jnp.float32

VMEM = pl.BlockSpec(memory_space=pltpu.VMEM)
SMEM = pl.BlockSpec(memory_space=pltpu.SMEM)
HBM = pl.BlockSpec(memory_space=pl.ANY)


def params():
    return pltpu.CompilerParams(vmem_limit_bytes=VMEM_LIMIT)


def cost(microseconds):
    return pl.CostEstimate(flops=int(microseconds * 1.15e9), bytes_accessed=0, transcendentals=0)


def dot_nn(a, b):
    return lax.dot_general(a, b, (((1,), (0,)), ((), ())), preferred_element_type=F32)


def dot_nt(a, b):
    return lax.dot_general(a, b, (((1,), (1,)), ((), ())), preferred_element_type=F32)


def dot_tn(a, b):
    return lax.dot_general(a, b, (((0,), (0,)), ((), ())), preferred_element_type=F32)


def normalise(x):
    mean = jnp.mean(x, axis=-1, keepdims=True)
    centered = x - mean
    inverse = lax.rsqrt(jnp.mean(centered * centered, axis=-1, keepdims=True) + EPSILON)
    return centered * inverse, inverse


def norm_kernel(kind_ref, x_ref, gain_ref, h_ref, ht_ref):
    def body(b, carry):
        x_hat, _ = normalise(x_ref[b].astype(F32))
        h = (x_hat * gain_ref[pl.ds(kind_ref[b], 1), :]).astype(BF16)
        h_ref[b] = h
        ht_ref[b] = h.T
        return carry

    lax.fori_loop(0, x_ref.shape[0], body, 0)


def attend(b, heads, size, window, qkv, da, attnt_ref, dq_ref, dk_ref, dv_ref):
    rows = qkv.shape[0]
    inner = heads * size
    scale = 1.0 / math.sqrt(size)
    same = None
    if window < rows:
        key = lax.broadcasted_iota(jnp.int32, (rows, 2 * rows), 0) // window
        query = lax.broadcasted_iota(jnp.int32, (rows, 2 * rows), 1) % rows // window
        same = key == query
    sums = {}

    def add(name, tile, value):
        known = sums.get((name, tile))
        sums[name, tile] = value if known is None else known + value

    for head in range(0, heads, 2):
        first, last = head * size // LANES, ((head + 2) * size - 1) // LANES + 1
        low, wide = first * LANES, (last - first) * LANES
        lane = lax.broadcasted_iota(jnp.int32, (rows, wide), 1) + low
        row = lax.broadcasted_iota(jnp.int32, (wide, rows), 0) + low
        lanes = [(lane >= h * size) & (lane < (h + 1) * size) for h in (head, head + 1)]
        bands = [(row >= h * size) & (row < (h + 1) * size) for h in (head, head + 1)]
        q, k, v = (qkv[:, at + low : at + low + wide] for at in (0, inner, 2 * inner))
        g = da[:, low : low + wide]
        q_pair = jnp.concatenate([jnp.where(mask, q, 0) for mask in lanes], axis=0)
        g_pair = jnp.concatenate([jnp.where(mask, g, 0) for mask in lanes], axis=0)
        scores = dot_nt(k, q_pair) * scale
        if same is not None:
            scores = jnp.where(same, scores, -1e30)
        exponent = jnp.exp(scores - jnp.max(scores, axis=0, keepdims=True))
        probs = exponent * (1.0 / jnp.sum(exponent, axis=0, keepdims=True))
        d_probs = dot_nt(v, g_pair)
        mean = jnp.sum(d_probs * probs, axis=0, keepdims=True)
        d_scores = (probs * (d_probs - mean) * scale).astype(BF16)
        probs = probs.astype(BF16)
        d_v = dot_nn(probs, g_pair)
        d_k = dot_nn(d_scores, q_pair)
        vt, kt = v.T, k.T
        mixed = dot_nn(
            jnp.concatenate([jnp.where(band, vt, 0) for band in bands], axis=1),
            jnp.concatenate([probs[:, :rows], probs[:, rows:]], axis=0),
        )
        d_q = dot_nn(
            jnp.concatenate([jnp.where(band, kt, 0) for band in bands], axis=1),
            jnp.concatenate([d_scores[:, :rows], d_scores[:, rows:]], axis=0),
        )
        for tile in range(first, last):
            span = slice(tile * LANES - low, (tile + 1) * LANES - low)
            add("v", tile, d_v[:, span])
            add("k", tile, d_k[:, span])
            add("q", tile, d_q[span])
            add("o", tile, mixed[span])
        for tile in range(first, last):
            span = slice(tile * LANES, (tile + 1) * LANES)
            if (head + 2) * size >= (tile + 1) * LANES:
                dv_ref[b, :, span] = sums.pop(("v", tile)).astype(BF16)
                dk_ref[b, :, span] = sums.pop(("k", tile)).astype(BF16)
                dq_ref[b, :, span] = sums.pop(("q", tile)).astype(BF16).T
                attnt_ref[b, span, :] = sums.pop(("o", tile)).astype(BF16)


def routed_copies(where_ref, refs, wq, wo, sems):
    g, z, c = where_ref[0], where_ref[1], where_ref[2]
    half_rows, wide, narrow = refs[0].shape[1], wq.shape[2], wo.shape[2] // 2
    groups = [(2 + 8 * i + 2 * other, other, step) for i, step in enumerate((3, 2, 1)) for other in range(4)]
    by_kind = []
    for far in range(2):
        kind = (g // 2) ^ far
        first, second = [], []
        for side in range(2):
            half = (g % 2) ^ side
            found = [(refs[i], 2 * kind + half, 2 * z + core) for i, core in ((0, c), (1, 1 - c))]
            for i, other, step in groups:
                if other == 2 * far + side:
                    chip = 2 * lax.rem(z + step, 4)
                    found += [(refs[i], 0, chip + c), (refs[i + 1], 0, chip + 1 - c)]
            for ref, at, shard in found:
                row = pl.multiple_of((shard * 2 + half) * half_rows, 16)
                out_row = pl.multiple_of(shard * half_rows, 16)
                column = pl.multiple_of(half * narrow, LANES)
                first.append(
                    pltpu.make_async_copy(
                        ref.at[at, :, pl.ds(0, wide)],
                        wq.at[kind, pl.ds(row, half_rows), :],
                        sems.at[far, len(first)],
                    )
                )
                second.append(
                    pltpu.make_async_copy(
                        ref.at[at, :, pl.ds(wide, narrow)],
                        wo.at[kind, pl.ds(out_row, half_rows), pl.ds(column, narrow)],
                        sems.at[far, 16 + len(second)],
                    )
                )
        by_kind.append(first + second)
    return by_kind


def weight_copies(routed, where_ref, refs, wq, wo, sems):
    if routed:
        return routed_copies(where_ref, refs, wq, wo, sems)
    return [
        [
            pltpu.make_async_copy(ref.at[kind], to.at[kind], sems.at[kind, i])
            for i, (ref, to) in enumerate(zip(refs, (wq, wo)))
        ]
        for kind in range(2)
    ]


def by_encoder(routed, where_ref, kind_ref, copies, body):
    for group in copies:
        for copy in group:
            copy.start()
    blocks = kind_ref.shape[0]
    first = where_ref[0] // 2 if routed else 0

    def step(i, carry):
        b, far = lax.rem(i, blocks), lax.div(i, blocks)
        for turn, group in enumerate(copies):

            @pl.when(i == turn * blocks)
            def _():
                for copy in group:
                    copy.wait()

        kind = first ^ far

        @pl.when(kind_ref[b] == kind)
        def _():
            body(b, kind)

        return carry

    lax.fori_loop(0, 2 * blocks, step, 0)


def layer_kernel(routed, n_weights, where_ref, kind_ref, h_ref, cot_ref, *rest):
    weights, rest = rest[:n_weights], rest[n_weights:]
    attnt_ref, dq_ref, dk_ref, dv_ref, wq, wo, qkv_ref, da_ref, sems = rest
    chunk = 3 * LANES

    def body(b, kind):
        for at in range(0, wq.shape[2], chunk):
            qkv_ref[:, at : at + chunk] = dot_nn(h_ref[b], wq[kind, :, at : at + chunk]).astype(BF16)
        for at in range(0, wo.shape[1], LANES):
            da_ref[:, at : at + LANES] = dot_nt(cot_ref[b], wo[kind, at : at + LANES, :]).astype(BF16)

        @pl.when(kind == 0)
        def _():
            attend(b, A_HEADS, A_SIZE, qkv_ref.shape[0], qkv_ref, da_ref, attnt_ref, dq_ref, dk_ref, dv_ref)

        @pl.when(kind != 0)
        def _():
            attend(b, V_HEADS, V_SIZE, VWIN, qkv_ref, da_ref, attnt_ref, dq_ref, dk_ref, dv_ref)

    by_encoder(routed, where_ref, kind_ref, weight_copies(routed, where_ref, weights, wq, wo, sems), body)


def result_kernel(routed, n_weights, where_ref, kind_ref, rank_ref, x_ref, cot_ref, gain_ref, attnt_ref, dq_ref, dk_ref, dv_ref, *rest):
    weights, rest = rest[:n_weights], rest[n_weights:]
    encoded_ref, grad_ref, wq, wo, wide_ref, sems = rest
    inner = dq_ref.shape[2]
    chunk = 2 * LANES
    width = x_ref.shape[2]

    def body(b, kind):
        rank = rank_ref[b]
        attn = attnt_ref[b].T
        for at in range(0, width, chunk):
            span = slice(at, at + chunk)
            encoded_ref[rank, :, span] = (
                x_ref[b, :, span].astype(F32) + dot_nn(attn, wo[kind, :, span])
            ).astype(BF16)
            wide_ref[:, span] = (
                dot_nt(dq_ref[b], wq[kind, span, :inner])
                + dot_nt(dk_ref[b], wq[kind, span, inner : 2 * inner])
                + dot_nt(dv_ref[b], wq[kind, span, 2 * inner :])
            )
        x_hat, inverse = normalise(x_ref[b].astype(F32))
        scaled = wide_ref[...] * gain_ref[pl.ds(kind, 1), :]
        d_input = inverse * (
            scaled
            - jnp.mean(scaled, axis=-1, keepdims=True)
            - x_hat * jnp.mean(scaled * x_hat, axis=-1, keepdims=True)
        )
        grad_ref[rank] = (cot_ref[b].astype(F32) + d_input).astype(BF16)

    by_encoder(routed, where_ref, kind_ref, weight_copies(routed, where_ref, weights, wq, wo, sems), body)


def left_kernel(where_ref, kind_ref, ht_a, ht_b, left):
    g, c = where_ref[0], where_ref[2]
    count = ht_a.shape[0]
    rows = left.shape[2] // 8
    for far in range(2):
        kind = (g // 2) ^ far
        for i in range(2 * count):
            source = ht_a if i < count else ht_b
            keep = kind_ref[i] == kind
            for side in range(2):
                for z in range(4):
                    row = pl.multiple_of(((2 * z + c) * 2 + ((g % 2) ^ side)) * rows, 16)
                    value = source[i % count, pl.ds(row, rows), :]
                    at = (side * 4 + z) * rows
                    left[far, i // count, at : at + rows, (i % count) * LANES : (i % count + 1) * LANES] = (
                        jnp.where(keep, value, jnp.zeros_like(value))
                    )


def out_terms_kernel(where_ref, kind_ref, attnt_a, attnt_b, cot_a, cot_b, own_ref, far_ref, sent_ref, left):
    g, z, c = where_ref[0], where_ref[1], where_ref[2]
    count = attnt_a.shape[0]
    rows = left.shape[2] // 4
    half_width = cot_a.shape[2] // 2
    for far in range(2):
        kind = (g // 2) ^ far
        for i in range(2 * count):
            source = attnt_a if i < count else attnt_b
            keep = kind_ref[i] == kind
            for step in range(4):
                row = pl.multiple_of((2 * (z ^ step) + c) * rows, 16)
                value = source[i % count, pl.ds(row, rows), :]
                left[far, i // count, step * rows : (step + 1) * rows, (i % count) * LANES : (i % count + 1) * LANES] = (
                    jnp.where(keep, value, jnp.zeros_like(value))
                )
    for far in range(2):
        for side in range(2):
            span = pl.ds(pl.multiple_of(((g % 2) ^ side) * half_width, LANES), half_width)
            total = dot_nn(left[far, 0], cot_a[:, :, span].reshape(-1, half_width))
            total += dot_nn(left[far, 1], cot_b[:, :, span].reshape(-1, half_width))
            total = total.reshape(4, rows, half_width)
            own_ref[2 * far + side] = total[0]
            far_ref[2 * far + side] = total[2]
            sent_ref[0, 2 * far + side] = total[1].astype(BF16)
            sent_ref[1, 2 * far + side] = total[3].astype(BF16)


def qkv_terms_kernel(left, *rest):
    pairs, (y_ref, x_ref, own_ref, xa_ref, yb_ref) = rest[:6], rest[6:]
    rows = left.shape[2] // 8
    width, cut = pairs[0].shape[2], xa_ref.shape[2]
    chunk = 3 * LANES
    for far in range(2):
        for part in range(3):
            d_a, d_b = pairs[2 * part : 2 * part + 2]
            for low in range(0, width, chunk):
                size = min(chunk, width - low)
                span = slice(low, low + size)
                total = dot_nn(left[far, 0], d_a[:, :, span].reshape(-1, size))
                total += dot_nn(left[far, 1], d_b[:, :, span].reshape(-1, size))
                total = total.reshape(2, 4, rows, size)
                at = part * width + low
                first = slice(at, at + size)
                last = slice(at - cut, at - cut + size)
                if far == 0:
                    own_ref[:, :, first] = total[0]
                for side in range(2):
                    if (far, side) == (0, 0):
                        continue
                    if at < cut and far:
                        y_ref[side, :, :, first] = total[side].astype(BF16)
                    elif at < cut:
                        xa_ref[:, :, first] = total[side]
                    elif side:
                        x_ref[far, :, :, last] = total[side].astype(BF16)
                    else:
                        yb_ref[:, :, last] = total[side]


QKV_CUT = 1024
STEPS = ((slice(0, 512), slice(0, 512)), (slice(512, None), slice(512, None)))
OUT_CUT = 384


def left_factor(where, kinds, ht, ht_other):
    count, width, window = ht.shape
    return pl.pallas_call(
        left_kernel,
        out_shape=jax.ShapeDtypeStruct((2, 2, width // 2, count * window), BF16),
        in_specs=[SMEM, SMEM] + [VMEM] * 2,
        out_specs=VMEM,
        compiler_params=params(),
        cost_estimate=cost(0.01),
        name="left_factor",
    )(where, kinds, ht, ht_other)


def out_terms(where, kinds, *pairs):
    count, inner, window = pairs[0].shape
    rows, width = inner // 8, pairs[2].shape[2] // 2
    return pl.pallas_call(
        out_terms_kernel,
        out_shape=[
            jax.ShapeDtypeStruct((4, rows, width), F32),
            jax.ShapeDtypeStruct((4, rows, width), F32),
            jax.ShapeDtypeStruct((2, 4, rows, width), BF16),
        ],
        in_specs=[SMEM, SMEM] + [VMEM] * len(pairs),
        out_specs=[VMEM] * 3,
        scratch_shapes=[pltpu.VMEM((2, 2, inner // 2, count * window), BF16)],
        compiler_params=params(),
        cost_estimate=cost(0.01),
        name="out_terms",
    )(where, kinds, *pairs)


def qkv_terms(left, *pairs):
    rows, columns = left.shape[2] // 8, 3 * pairs[0].shape[2]
    rest = columns - QKV_CUT
    return pl.pallas_call(
        qkv_terms_kernel,
        out_shape=[
            jax.ShapeDtypeStruct((2, 4, rows, QKV_CUT), BF16),
            jax.ShapeDtypeStruct((2, 4, rows, rest), BF16),
            jax.ShapeDtypeStruct((4, rows, columns), F32),
            jax.ShapeDtypeStruct((4, rows, QKV_CUT), F32),
            jax.ShapeDtypeStruct((4, rows, rest), F32),
        ],
        in_specs=[VMEM] * (1 + len(pairs)),
        out_specs=[VMEM] * 5,
        compiler_params=params(),
        cost_estimate=cost(0.01),
        name="qkv_terms",
    )(left, *pairs)


def flat(groups, shards, move):
    pairs = []
    for g in range(groups):
        for d in range(shards):
            to_g, to_d = move(g, d)
            pairs.append((g * shards + d, to_g * shards + to_d))
    return pairs


def routes(groups, shards):
    chips = shards // 2
    make = functools.partial(flat, groups, shards)
    return {
        "sibling": make(lambda g, d: (g, d ^ 1)),
        "x": make(lambda g, d: (g ^ 1, d)),
        "y": make(lambda g, d: (g ^ 2, d)),
        "z1": make(lambda g, d: (g, d ^ 2)),
        "z2": make(lambda g, d: (g, d ^ 4)),
        "z": [
            make(lambda g, d, s=s: (g, (d // 2 + s) % chips * 2 + d % 2)) for s in range(chips)
        ],
    }


def send(value, route):
    return lax.ppermute(value, AXES, route)


def tied(value, *others):
    return lax.optimization_barrier((value, *others))[0]


def gather_small(norm_gain, modality, route, z, c):
    kinds, rows = norm_gain.shape
    gains = norm_gain.astype(F32).reshape(1, -1)
    sibling = send(jnp.concatenate([gains, modality.astype(F32)[None]], axis=1), route["sibling"])
    others, kinds_other = sibling[:, : kinds * rows], sibling[0, kinds * rows :].astype(jnp.int32)
    pair = jnp.concatenate([jnp.where(c == 0, gains, others), jnp.where(c == 0, others, gains)], axis=0)
    chips = jnp.arange(4)[:, None, None]
    total = jnp.where(chips == z, pair[None], 0)
    for step in range(1, 4):
        total += jnp.where(chips == (z + 4 - step) % 4, send(pair, route["z"][step])[None], 0)
    return total.reshape(8, kinds, rows).transpose(1, 0, 2).reshape(kinds, -1), kinds_other


def quarter_of(qkv_weight, out_weight, q):
    rows, narrow = qkv_weight.shape[1] // 2, out_weight.shape[2] // 2
    own_qkv = lax.dynamic_slice(qkv_weight, (q // 2, q % 2 * rows, 0), (1, rows, qkv_weight.shape[2]))
    own_out = lax.dynamic_slice(out_weight, (q // 2, 0, q % 2 * narrow), (1, out_weight.shape[1], narrow))
    return jnp.concatenate([own_qkv, own_out], axis=2)


def quarters_of(qkv_weight, out_weight):
    kinds, rows, columns = qkv_weight.shape
    narrow = out_weight.shape[2] // 2
    return jnp.concatenate(
        [
            qkv_weight.reshape(4, rows // 2, columns),
            out_weight.reshape(kinds, -1, 2, narrow).transpose(0, 2, 1, 3).reshape(4, -1, narrow),
        ],
        axis=2,
    )


def send_terms(terms, route):
    to_y, to_x = terms[:2]
    return send(to_y, route["y"]), send(to_x, route["x"])


def reduce_plane(terms, arrived, route):
    _, _, own, x_term, y_term = terms
    from_y, from_x = arrived
    next_x = send((x_term + from_y[1].astype(F32)).astype(BF16), route["x"])
    next_y = send((y_term + from_x[1].astype(F32)).astype(BF16), route["y"])
    return own + jnp.concatenate(
        [
            from_y[0].astype(F32) + next_x.astype(F32),
            from_x[0].astype(F32) + next_y.astype(F32),
        ],
        axis=-1,
    )


def line_parts(total, z):
    parts = [lax.dynamic_index_in_dim(total, (z + step) % 4, 0, keepdims=False) for step in range(4)]
    return [parts[0]] + [part.astype(BF16) for part in parts[1:]]


def send_line(parts, route):
    return [send(parts[step], route["z"][step]) for step in range(1, 4)]


def add_line(own, arrived):
    return own + sum(part.astype(F32) for part in arrived)


def plane_terms(total, cut):
    first, second = total[..., :cut], total[..., cut:]
    return [
        first[2:].astype(BF16),
        jnp.stack([second[1], second[3]]).astype(BF16),
        total[0],
        first[1],
        second[2],
    ]


def both_halves(share, g, route):
    other = send(share.astype(BF16), route["x"]).astype(F32)
    return [jnp.where(g % 2 == i, share, other) for i in range(2)]


def whole_weights(qkv_weight, out_weight):
    return [
        lax.all_gather(qkv_weight, "dp", axis=1, tiled=True),
        lax.all_gather(out_weight, "dp", axis=1, tiled=True),
    ]


def summed_terms(kinds, h, dqkv, attn, cot):
    shards = lax.axis_size("dp")
    results = []
    for left, right in ((h, dqkv), (attn, cot)):
        parts = []
        for kind in range(2):
            keep = (kinds == kind)[:, None, None]
            parts.append(
                jnp.einsum("bwi,bwj->ij", jnp.where(keep, left, 0), right, preferred_element_type=F32)
            )
        total = lax.psum_scatter(
            jnp.stack(parts).reshape(2, shards, -1, right.shape[2]), "dp", scatter_dimension=1
        )
        total = lax.psum(total, "grp")
        results.append(lax.dynamic_index_in_dim(total, lax.axis_index("grp") // 2, 0, keepdims=False))
    return results


def shards(blocks, cotangent, modality, time_rank, qkv_weight, out_weight, norm_gain):
    groups, shard_count = lax.axis_size("grp"), lax.axis_size("dp")
    g, d = lax.axis_index("grp"), lax.axis_index("dp")
    z, c = d // 2, d % 2
    count, window, width = blocks.shape
    columns = qkv_weight.shape[2]
    inner = columns // 3
    routed = groups == 4 and shard_count == 8 and out_weight.shape[1] % 16 == 0
    where = jnp.stack([g, z, c]).astype(jnp.int32)
    rows = count * window

    def normed(blocks, gain):
        return pl.pallas_call(
            norm_kernel,
            out_shape=[
                jax.ShapeDtypeStruct(blocks.shape, BF16),
                jax.ShapeDtypeStruct((count, width, window), BF16),
            ],
            in_specs=[SMEM, VMEM, VMEM],
            out_specs=[VMEM] * 2,
            compiler_params=params(),
            cost_estimate=cost(0.01),
            name="norm",
        )(modality, blocks, gain)

    if routed:
        route = routes(groups, shard_count)

        def in_plane(held):
            return send(held, route["x"]), send(held, route["y"])

        def sibling(value, *after):
            return send(tied(value, *after) if after else value, route["sibling"])

        own = quarter_of(qkv_weight, out_weight, g)
        near = send(own, route["z"][1])
        gain, kinds_other = gather_small(tied(norm_gain, own), modality, route, z, c)
        near = tied(near, gain)
        far = send(near, route["z"][1])
        near_x, near_y = in_plane(near)
        h, ht = normed(tied(blocks, near), gain)
        quarters = quarters_of(tied(qkv_weight, near), out_weight)
        diagonal = lax.dynamic_slice_in_dim(quarters, g ^ 3, 1, 0)
        quarters_other = sibling(quarters)
        cot_other = sibling(cotangent, near)
        far = tied(far, near_x, near_y, h, quarters_other)
        far_x, far_y = in_plane(far)
        back = send(tied(own, far), route["z"][3])
        kinds = jnp.concatenate([modality, kinds_other])
        ht_other = sibling(ht, far)
        left = left_factor(where, kinds, ht, ht_other)
        near_other = sibling(near, far)
        near_x_other = sibling(near_x, near_other)
        near_y_other = sibling(near_y, near_other)
        back = tied(back, far_x, far_y, left, near_other)
        back_x, back_y = in_plane(back)
        near_across = send(tied(diagonal, back), route["z"][1])
        far_other = sibling(far, back)
        far_x_other = sibling(far_x, far_other)
        far_y_other = sibling(far_y, far_other)
        back_other = sibling(back, far_other)
        far_across = send(tied(far_x, back_x, back_y), route["y"])
        back_across = send(tied(diagonal, near_across), route["z"][3])
        weights = [quarters, quarters_other, near, near_other, near_x, near_x_other, near_y, near_y_other]
        weights += [near_across, sibling(near_across), far, far_other, far_x, far_x_other, far_y, far_y_other]
        weights += [far_across, sibling(far_across), back, back_other, back_x, sibling(back_x)]
        weights += [back_y, sibling(back_y), back_across, sibling(back_across)]
    else:
        gain = lax.all_gather(norm_gain, "dp", axis=1, tiled=True).astype(F32)
        weights = whole_weights(qkv_weight, out_weight)
        h, ht = normed(blocks, gain)
    n_weights = len(weights)
    weight_scratch = [
        pltpu.VMEM((2, width, columns), BF16),
        pltpu.VMEM((2, inner, width), BF16),
    ]
    weight_sems = pltpu.SemaphoreType.DMA((2, 32))

    attnt, dq, dk, dv = pl.pallas_call(
        functools.partial(layer_kernel, routed, n_weights),
        out_shape=[jax.ShapeDtypeStruct((count, inner, window), BF16)]
        + [jax.ShapeDtypeStruct((count, window, inner), BF16)] * 3,
        in_specs=[SMEM, SMEM, VMEM, VMEM] + [HBM] * n_weights,
        out_specs=[VMEM] * 4,
        scratch_shapes=weight_scratch
        + [pltpu.VMEM((window, columns), BF16), pltpu.VMEM((window, inner), BF16), weight_sems],
        compiler_params=params(),
        cost_estimate=cost(0.01),
        name="layer",
    )(where, modality, h, cotangent, *weights)

    def results(attnt):
        return pl.pallas_call(
            functools.partial(result_kernel, routed, n_weights),
            out_shape=[jax.ShapeDtypeStruct(blocks.shape, BF16)] * 2,
            in_specs=[SMEM] * 3 + [VMEM] * 7 + [HBM] * n_weights,
            out_specs=[VMEM] * 2,
            scratch_shapes=weight_scratch + [pltpu.VMEM((window, width), F32), weight_sems],
            compiler_params=params(),
            cost_estimate=cost(0.01),
            name="result",
        )(where, modality, time_rank, blocks, cotangent, gain, attnt, dq, dk, dv, *weights)

    if routed:
        dq_other, dk_other, dv_other, attnt_other = [
            send(part, route["sibling"]) for part in (dq, dk, dv, attnt)
        ]
        terms = qkv_terms(left, dq, dq_other, dk, dk_other, dv, dv_other)
        arrived = send_terms(terms, route)
        out_own, out_far, out_sent = out_terms(
            where, kinds, tied(attnt, terms[0]), attnt_other, cotangent, cot_other
        )
        out_near = send(out_sent, route["z1"])
        encoded, block_grad = results(tied(attnt, out_own))
        out_near, *arrived = lax.optimization_barrier((out_near, *arrived, encoded))[:3]
        parts = []
        for first, last in STEPS:
            step_arrived = (arrived[0][..., first], arrived[1][..., last])
            own = jnp.concatenate([terms[2][..., :QKV_CUT][..., first], terms[2][..., QKV_CUT:][..., last]], axis=2)
            step_terms = (None, None, own, terms[3][..., first], terms[4][..., last])
            parts.append(line_parts(reduce_plane(step_terms, step_arrived, route), z))
        out_next = send((out_far + out_near[1].astype(F32)).astype(BF16), route["z2"])
        shares = [add_line(part[0], send_line(part, route)) for part in parts]
        out_total = tied(out_own + out_near[0].astype(F32) + out_next.astype(F32), *parts[1])
        terms = plane_terms(out_total, OUT_CUT)
        share = reduce_plane(terms, send_terms(terms, route), route)
        share_out = jnp.concatenate(both_halves(share, g, route), axis=1)
        (first_a, first_b), (last_a, last_b) = [
            tuple(zip(*[(half[:, :512], half[:, 512:]) for half in both_halves(share, g, route)]))
            for share in shares
        ]
        share_qkv = jnp.concatenate(
            [jnp.concatenate(halves, axis=0) for halves in (first_a, last_a, first_b, last_b)], axis=1
        )
    else:
        encoded, block_grad = results(attnt)
        share_qkv, share_out = summed_terms(
            modality, h, jnp.concatenate([dq, dk, dv], axis=2), attnt.transpose(0, 2, 1), cotangent
        )

    kind = g // 2
    own_weight = lax.dynamic_index_in_dim(qkv_weight, kind, 0, keepdims=False).astype(F32)
    own_gain = lax.dynamic_index_in_dim(norm_gain, kind, 0, keepdims=False).astype(F32)
    share_gain = jnp.sum(share_qkv * own_weight, axis=1) / own_gain

    return (encoded, block_grad, share_qkv[None], share_out[None], share_gain[None])


def solution(mesh):
    return jax.shard_map(
        shards,
        mesh=mesh,
        in_specs=(
            P(("grp", "dp"), None, None),
            P(("grp", "dp"), None, None),
            P(("grp", "dp")),
            P(("grp", "dp")),
            P(None, "dp", None),
            P(None, "dp", None),
            P(None, "dp"),
        ),
        out_specs=(
            P(("grp", "dp"), None, None),
            P(("grp", "dp"), None, None),
            P("grp", "dp", None),
            P("grp", "dp", None),
            P("grp", "dp"),
        ),
        check_vma=False,
    )
```

time: 245 us -> 214 us (0.87); the launches traced: 241 us -> 214 us
  waiting for transfers between devices: 96.5 us -> 65.2 us
  starting transfers between devices: 41.8 us -> 62.6 us
  blocking collectives: 14.4 us -> 0 us
  other arithmetic: 11 us -> 14.9 us
  local copies, waits for them, and re-layouts: 12.2 us -> 8.71 us
  Pallas kernels: 63.8 us -> 61.1 us
    ppermute x42 -> x56, waiting for transfers between devices: 96.5 us -> 65.2 us  [send(): return lax.ppermute(value, AXES, route)]
    ppermute x42 -> x56, starting transfers between devices: 41.8 us -> 62.6 us  [send(): return lax.ppermute(value, AXES, route)]
    all_gather x1 -> x0, blocking collectives: 14.4 us -> none  [shards(): gain = lax.all_gather(norm_gain, 'dp', axis=1, tiled=True).astype(F32)]
    unnamed x42 -> x68, local copies, waits for them, and re-layouts: 7.76 us -> 4.45 us
  transfers between devices with their start and end apart: 42 -> 56, of which waited for: 22 -> 25; matrix products, arithmetic and copies ran while one was open for 7% -> 7% of each run, Pallas kernels for 14% -> 29%
where the time goes in v2:
time: 214 us
  waiting for transfers between devices  65.2 us (30%)
  starting transfers between devices  62.6 us (29%)
  Pallas kernels  61.1 us (29%)
  other arithmetic  14.9 us (7%)
  local copies, waits for them, and re-layouts  8.71 us (4%)
    ppermute x56, waiting for transfers between devices, send(): return lax.ppermute(value, AXES, route)  65.2 us
    ppermute x56, starting transfers between devices, send(): return lax.ppermute(value, AXES, route)  62.6 us
    pallas_call x1, Pallas kernels, shards(): pl.pallas_call(functools.partial(layer_kernel, routed, n_weights), out_sh...  19.7 us
    pallas_call x1, Pallas kernels, results(): pl.pallas_call(functools.partial(result_kernel, routed, n_weights), out_s...  16.1 us
    pallas_call x1, Pallas kernels, qkv_terms(): pl.pallas_call(qkv_terms_kernel, out_shape=[jax.ShapeDtypeStruct((2, 4, r...  11.3 us
    pallas_call x1, Pallas kernels, out_terms(): pl.pallas_call(out_terms_kernel, out_shape=[jax.ShapeDtypeStruct((4, rows...  5.76 us
    unnamed x68, local copies, waits for them, and re-layouts  4.45 us
    pallas_call x1, Pallas kernels, normed(): pl.pallas_call(norm_kernel, out_shape=[jax.ShapeDtypeStruct(blocks.shape,...  4.31 us
  transfers between devices with their start and end apart: 56, of which 25 were waited for; matrix products, arithmetic and copies ran while one was open for 7% of the time, Pallas kernels for 29%

profile of v2, /device:TPU:8, one launch (start us, length us, event | category | flops | bytes accessed | tf_op | source)
XLA Modules:
  0.0 214.0 jit_solution(14150397320706459115)
XLA Ops:
  0.7 1.0 constant_dynamic-slice_fusion.2
  1.7 0.9 constant_dynamic-slice_fusion.1
  2.7 1.6 collective-permute-start.4
  4.8 0.9 collective-permute-done
  5.7 1.6 collective-permute-start.1
  7.3 1.2 collective-permute-start.2
  9.6 4.5 %collective-permute-done.1 = f32[2,320]{1,0:T(2,128)S(1)} collective-permute-done((f32[2,320]{1,0:T(2,128)S(1)}, f32[2,320]{1,0:T(2,128)S(1)}, u32[]{:S(2)}, u32[]{:S(2)}) %collective-permute-start.1) | collective-permute-done | bytes 2592 | tf_op jit(solution)/shard_map/ppermute | solution.py:418
  18.7 1.5 collective-permute-start.7
  20.2 1.5 collective-permute-start.8
  21.7 4.3 %norm.1 = (bf16[4,128,1280]{2,1,0:T(8,128)(2,1)}, bf16[4,1280,128]{2,1,0:T(8,128)(2,1)}) custom-call(s32[4]{0:T(128)} %kind_ref.5, bf16[4,128,1280]{2,1,0:T(8,128)(2,1)} %x_ref.2, f32[2,1280]{1,0:T(2,128)} %reshape.101.gain_ref), custom_call_target="tpu_custom_call" | custom-call | flops 11500000 | tf_op jit(solution)/shard_map/norm/pallas_call | solution.py:542
  26.0 3.1 %collective-permute-done.6.rest_10_ = bf16[1,80,2560]{2,1,0:T(8,128)(2,1)} collective-permute-done((bf16[1,80,2560]{2,1,0:T(8,128)(2,1)S(1)}, bf16[1,80,2560]{2,1,0:T(8,128)(2,1)}, u32[]{:S(2)}, u32[]{:S(2)}) %collective-permute-start.6) | collective-permute-done | bytes 409632 | tf_op jit(solution)/shard_map/ppermute | solution.py:418
  29.6 1.2 collective-permute-done.8.rest_6_
  32.1 1.5 collective-permute-start.14
  33.6 2.6 %collective-permute-start.12 = (bf16[1,80,2560]{2,1,0:T(8,128)(2,1)}, bf16[1,80,2560]{2,1,0:T(8,128)(2,1)}, u32[]{:S(2)}, u32[]{:S(2)}) collective-permute-start(bf16[1,80,2560]{2,1,0:T(8,128)(2,1)} %copy-done.30), channel_id=1, source_target_pairs={{0,6},{1,7},{2,0},{3,1},{4,2},{5,3},{6,4},{7,5},{8,14},{9,15},{10,... | collective-permute-start | bytes 1228808 | tf_op jit(solution)/shard_map/ppermute | solution.py:418
  37.6 3.9 %left_factor.1.left = bf16[2,2,640,512]{3,2,1,0:T(8,128)(2,1)} custom-call(s32[3]{0:T(128)} %pad_add_fusion.where_ref, s32[8]{0:T(128)} %pad_add_fusion.1.kind_ref, bf16[4,1280,128]{2,1,0:T(8,128)(2,1)} %get-tuple-element.57.ht_a, bf16[4,1280,128]{2,1,0:T(8,128)(2,1)} %collective-permute-done.15.ht_b), custom_call_target="tpu_custom_call" | custom-call | flops 11500000 | tf_op jit(solution)/shard_map/left_factor/pallas_call | solution.py:343
  41.5 3.9 %collective-permute-done.12.rest_18_ = bf16[1,80,2560]{2,1,0:T(8,128)(2,1)} collective-permute-done((bf16[1,80,2560]{2,1,0:T(8,128)(2,1)}, bf16[1,80,2560]{2,1,0:T(8,128)(2,1)}, u32[]{:S(2)}, u32[]{:S(2)}) %collective-permute-start.12) | collective-permute-done | bytes 409632 | tf_op jit(solution)/shard_map/ppermute | solution.py:418
  45.4 1.8 collective-permute-start.16
  47.2 1.5 collective-permute-start.21
  49.2 7.6 %collective-permute-done.16.rest_8_ = bf16[1,80,2560]{2,1,0:T(8,128)(2,1)S(1)} collective-permute-done((bf16[1,80,2560]{2,1,0:T(8,128)(2,1)}, bf16[1,80,2560]{2,1,0:T(8,128)(2,1)S(1)}, u32[]{:S(2)}, u32[]{:S(2)}) %collective-permute-start.16) | collective-permute-done | bytes 409632 | tf_op jit(solution)/shard_map/ppermute | solution.py:418
  56.8 3.8 %collective-permute-start.28 = (bf16[1,80,2560]{2,1,0:T(8,128)(2,1)}, bf16[1,80,2560]{2,1,0:T(8,128)(2,1)S(1)}, u32[]{:S(2)}, u32[]{:S(2)}) collective-permute-start(bf16[1,80,2560]{2,1,0:T(8,128)(2,1)} %fusion.7), channel_id=1, source_target_pairs={{0,6},{1,7},{2,0},{3,1},{4,2},{5,3},{6,4},{7,5},{8,14},{9,15},{10,... | collective-permute-start | bytes 1228808 | tf_op jit(solution)/shard_map/ppermute | solution.py:418
  61.8 8.4 %collective-permute-done.28.rest_24_ = bf16[1,80,2560]{2,1,0:T(8,128)(2,1)S(1)} collective-permute-done((bf16[1,80,2560]{2,1,0:T(8,128)(2,1)}, bf16[1,80,2560]{2,1,0:T(8,128)(2,1)S(1)}, u32[]{:S(2)}, u32[]{:S(2)}) %collective-permute-start.28) | collective-permute-done | bytes 409632 | tf_op jit(solution)/shard_map/ppermute | solution.py:418
  70.8 1.9 collective-permute-done.23.rest_16_
  74.5 1.2 collective-permute-done.29.rest_25_
  76.6 19.7 %layer.1 = (bf16[4,640,128]{2,1,0:T(8,128)(2,1)}, bf16[4,128,640]{2,1,0:T(8,128)(2,1)}, bf16[4,128,640]{2,1,0:T(8,128)(2,1)}, bf16[4,128,640]{2,1,0:T(8,128)(2,1)}) custom-call(s32[3]{0:T(128)} %pad_add_fusion.where_ref, s32[4]{0:T(128)} %kind_ref.5, bf16[4,128,1280]{2,1,0:T(8,128)(2,1)} %get-tuple-element.49.h_ref, bf16[4,128,1280]{2,1,0:T(8,128)(2,1)} %cot_ref.3, ...), custom_call_target="tpu_custom_call" | custom-call | flops 11500000 | tf_op jit(solution)/shard_map/layer/pallas_call | solution.py:608
  97.4 1.3 collective-permute-done.30.rest_1_
  98.7 1.9 collective-permute-done.31.rest_3_
  100.5 0.9 collective-permute-done.32.rest_5_
  102.4 11.3 %qkv_terms.1 = (bf16[2,4,80,1024]{3,2,1,0:T(8,128)(2,1)}, bf16[2,4,80,896]{3,2,1,0:T(8,128)(2,1)}, f32[4,80,1920]{2,1,0:T(8,128)}, f32[4,80,1024]{2,1,0:T(8,128)}, f32[4,80,896]{2,1,0:T(8,128)}) custom-call(bf16[2,2,640,512]{3,2,1,0:T(8,128)(2,1)} %left_factor.1.left, bf16[4,128,640]{2,1,0:T(8,128)(2,1)} %get-tuple-element.67.rest_0_.dq_ref, ...), custom_call_target="tpu_custom_call" | custom-call | flops 11500000 | tf_op jit(solution)/shard_map/qkv_terms/pallas_call | solution.py:376
  113.9 1.4 collective-permute-start.37
  115.3 5.8 %out_terms.1 = (f32[4,80,640]{2,1,0:T(8,128)}, f32[4,80,640]{2,1,0:T(8,128)}, bf16[2,4,80,640]{3,2,1,0:T(8,128)(2,1)}) custom-call(s32[3]{0:T(128)} %pad_add_fusion.where_ref, s32[8]{0:T(128)} %pad_add_fusion.1.kind_ref, bf16[4,640,128]{2,1,0:T(8,128)(2,1)} %get-tuple-element.74.attnt_a.attnt_ref, bf16[4,640,128]{2,1,0:T(8,128)(2,1)} %collective-permute-done.33.attnt_b, ...), custom_call_target="tpu_custom_call" | custom-call | flops 11500000 | tf_op jit(solution)/shard_map/out_terms/pallas_call | solution.py:357
  121.1 1.9 collective-permute-start.35
  123.0 16.1 %result.1 = (bf16[4,128,1280]{2,1,0:T(8,128)(2,1)}, bf16[4,128,1280]{2,1,0:T(8,128)(2,1)}) custom-call(s32[3]{0:T(128)} %pad_add_fusion.where_ref, s32[4]{0:T(128)} %kind_ref.5, s32[4]{0:T(128)} %rank_ref.1, bf16[4,128,1280]{2,1,0:T(8,128)(2,1)} %x_ref.2, bf16[4,128,1280]{2,1,0:T(8,128)(2,1)} %cot_ref.3, f32[2,1280]{1,0:T(2,128)} %reshape.101.gain_ref, ...), custom_call_target="tpu_custom_call" | custom-call | flops 11500000 | tf_op jit(solution)/shard_map/result/pallas_call | solution.py:622
  139.4 2.0 collective-permute-done.35
  141.3 3.4 %collective-permute-done.36 = bf16[2,4,80,1024]{3,2,1,0:T(8,128)(2,1)} collective-permute-done((bf16[2,4,80,1024]{3,2,1,0:T(8,128)(2,1)}, bf16[2,4,80,1024]{3,2,1,0:T(8,128)(2,1)}, u32[]{:S(2)}, u32[]{:S(2)}) %collective-permute-start.36) | collective-permute-done | bytes 1310752 | tf_op jit(solution)/shard_map/ppermute | solution.py:418
  144.8 1.5 fusion.5
  146.3 1.4 collective-permute-start.38
  148.4 1.0 fusion.6
  149.7 1.1 fusion.1
  150.8 1.0 fusion.4
  151.9 4.8 %collective-permute-start.50 = (bf16[4,80,640]{2,1,0:T(8,128)(2,1)S(1)}, bf16[4,80,640]{2,1,0:T(8,128)(2,1)S(1)}, u32[]{:S(2)}, u32[]{:S(2)}) collective-permute-start(bf16[4,80,640]{2,1,0:T(8,128)(2,1)S(1)} %fusion.1), channel_id=1, source_target_pairs={{0,4},{1,5},{2,6},{3,7},{4,0},{5,1},{6,2},{7,3},{8,12},{9,13},{10,... | collective-permute-start | bytes 1228808 | tf_op jit(solution)/shard_map/ppermute | solution.py:418
  156.7 1.7 collective-permute-start.39
  158.4 1.0 convert_add_fusion.9
  159.5 2.8 %collective-permute-done.44 = bf16[4,80,512]{2,1,0:T(8,128)(2,1)S(1)} collective-permute-done((bf16[4,80,512]{2,1,0:T(8,128)(2,1)S(1)}, bf16[4,80,512]{2,1,0:T(8,128)(2,1)S(1)}, u32[]{:S(2)}, u32[]{:S(2)}) %collective-permute-start.44) | collective-permute-done | bytes 327712 | tf_op jit(solution)/shard_map/ppermute | solution.py:418
  162.3 1.3 convert_add_fusion.7
  163.8 2.2 %collective-permute-start.46 = (bf16[80,896]{1,0:T(8,128)(2,1)S(1)}, bf16[80,896]{1,0:T(8,128)(2,1)S(1)}, u32[]{:S(2)}, u32[]{:S(2)}) collective-permute-start(bf16[80,896]{1,0:T(8,128)(2,1)S(1)} %get-tuple-element.104), channel_id=1, source_target_pairs={{0,2},{1,3},{2,4},{3,5},{4,6},{5,7},{6,0},{7,1},{8,10},{9,11},{10,... | collective-permute-start | bytes 430088 | tf_op jit(solution)/shard_map/ppermute | solution.py:418
  166.0 2.7 %collective-permute-start.47 = (bf16[80,896]{1,0:T(8,128)(2,1)S(1)}, bf16[80,896]{1,0:T(8,128)(2,1)S(1)}, u32[]{:S(2)}, u32[]{:S(2)}) collective-permute-start(bf16[80,896]{1,0:T(8,128)(2,1)S(1)} %get-tuple-element.106), channel_id=1, source_target_pairs={{0,4},{1,5},{2,6},{3,7},{4,0},{5,1},{6,2},{7,3},{8,12},{9,13},{10,... | collective-permute-start | bytes 430088 | tf_op jit(solution)/shard_map/ppermute | solution.py:418
  168.7 1.9 collective-permute-start.48
  170.6 1.1 convert_add_fusion.5
  172.1 7.1 %collective-permute-done.50 = bf16[4,80,640]{2,1,0:T(8,128)(2,1)S(1)} collective-permute-done((bf16[4,80,640]{2,1,0:T(8,128)(2,1)S(1)}, bf16[4,80,640]{2,1,0:T(8,128)(2,1)S(1)}, u32[]{:S(2)}, u32[]{:S(2)}) %collective-permute-start.50) | collective-permute-done | bytes 409632 | tf_op jit(solution)/shard_map/ppermute | solution.py:418
  179.3 3.7 %collective-permute-start.41 = (bf16[80,1024]{1,0:T(8,128)(2,1)S(1)}, bf16[80,1024]{1,0:T(8,128)(2,1)S(1)}, u32[]{:S(2)}, u32[]{:S(2)}) collective-permute-start(bf16[80,1024]{1,0:T(8,128)(2,1)S(1)} %get-tuple-element.99), channel_id=1, source_target_pairs={{0,4},{1,5},{2,6},{3,7},{4,0},{5,1},{6,2},{7,3},{8,12},{9,13},{10,... | collective-permute-start | bytes 491528 | tf_op jit(solution)/shard_map/ppermute | solution.py:418
  183.0 1.1 fusion.2
  184.1 5.8 %collective-permute-start.42 = (bf16[80,1024]{1,0:T(8,128)(2,1)S(1)}, bf16[80,1024]{1,0:T(8,128)(2,1)S(1)}, u32[]{:S(2)}, u32[]{:S(2)}) collective-permute-start(bf16[80,1024]{1,0:T(8,128)(2,1)S(1)} %get-tuple-element.98), channel_id=1, source_target_pairs={{0,6},{1,7},{2,0},{3,1},{4,2},{5,3},{6,4},{7,5},{8,14},{9,15},{10,... | collective-permute-start | bytes 491528 | tf_op jit(solution)/shard_map/ppermute | solution.py:418
  189.9 3.5 %collective-permute-done.48 = bf16[80,896]{1,0:T(8,128)(2,1)S(1)} collective-permute-done((bf16[80,896]{1,0:T(8,128)(2,1)S(1)}, bf16[80,896]{1,0:T(8,128)(2,1)S(1)}, u32[]{:S(2)}, u32[]{:S(2)}) %collective-permute-start.48) | collective-permute-done | bytes 143392 | tf_op jit(solution)/shard_map/ppermute | solution.py:418
  193.6 1.4 collective-permute-start.51
  195.0 1.6 collective-permute-start.53
  198.1 1.7 collective-permute-start.43
  199.9 1.5 collective-permute-start.54
  201.4 1.0 collective-permute-start.52
  202.4 1.6 collective-permute-done.54
  204.1 1.8 collective-permute-done.43
  206.0 1.2 copy-done.3
  207.2 1.2 fusion
  208.4 0.9 collective-permute-start.55
  209.9 3.2 %collective-permute-done.55 = bf16[80,640]{1,0:T(8,128)(2,1)S(1)} collective-permute-done((bf16[80,640]{1,0:T(8,128)(2,1)S(1)}, bf16[80,640]{1,0:T(8,128)(2,1)S(1)}, u32[]{:S(2)}, u32[]{:S(2)}) %collective-permute-start.55) | collective-permute-done | bytes 102432 | tf_op jit(solution)/shard_map/ppermute | solution.py:418
  (196 shorter events, 21.3 us)
Async XLA Ops:
  2.7 13.4 %collective-permute-start.4 = (bf16[1,80,2560]{2,1,0:T(8,128)(2,1)S(1)}, bf16[1,80,2560]{2,1,0:T(8,128)(2,1)S(1)}, u32[]{:S(2)}, u32[]{:S(2)}) collective-permute-start(bf16[1,80,2560]{2,1,0:T(8,128)(2,1)S(1)} %pad_maximum_fusion.1), channel_id=1, source_target_pairs={{0,2},{1,3},{2,4},{3,5},{4,6},{5,7},{6,0},{7,1},{8,10},{9,11},{10,... | collective-permute-start | bytes 1228808 | tf_op jit(solution)/shard_map/ppermute | solution.py:418
  4.5 1.2 collective-permute-start
  5.7 8.4 %collective-permute-start.1 = (f32[2,320]{1,0:T(2,128)S(1)}, f32[2,320]{1,0:T(2,128)S(1)}, u32[]{:S(2)}, u32[]{:S(2)}) collective-permute-start(f32[2,320]{1,0:T(2,128)S(1)} %pad_maximum_fusion.4), channel_id=1, source_target_pairs={{0,2},{1,3},{2,4},{3,5},{4,6},{5,7},{6,0},{7,1},{8,10},{9,11},{10,... | collective-permute-start | bytes 7688 | tf_op jit(solution)/shard_map/ppermute | solution.py:418
  7.3 7.8 %collective-permute-start.2 = (f32[2,320]{1,0:T(2,128)S(1)}, f32[2,320]{1,0:T(2,128)S(1)}, u32[]{:S(2)}, u32[]{:S(2)}) collective-permute-start(f32[2,320]{1,0:T(2,128)S(1)} %pad_maximum_fusion.4), channel_id=1, source_target_pairs={{0,4},{1,5},{2,6},{3,7},{4,0},{5,1},{6,2},{7,3},{8,12},{9,13},{10,... | collective-permute-start | bytes 7688 | tf_op jit(solution)/shard_map/ppermute | solution.py:418
  8.6 6.6 %collective-permute-start.3 = (f32[2,320]{1,0:T(2,128)S(1)}, f32[2,320]{1,0:T(2,128)S(1)}, u32[]{:S(2)}, u32[]{:S(2)}) collective-permute-start(f32[2,320]{1,0:T(2,128)S(1)} %pad_maximum_fusion.4), channel_id=1, source_target_pairs={{0,6},{1,7},{2,0},{3,1},{4,2},{5,3},{6,4},{7,5},{8,14},{9,15},{10,... | collective-permute-start | bytes 7688 | tf_op jit(solution)/shard_map/ppermute | solution.py:418
  17.0 20.6 %copy-start = (bf16[4,80,2560]{2,1,0:T(8,128)(2,1)}, bf16[4,80,2560]{2,1,0:T(8,128)(2,1)S(1)}, u32[]{:S(2)}) copy-start(bf16[4,80,2560]{2,1,0:T(8,128)(2,1)S(1)} %pad_maximum_fusion.rest_0_) | copy-start | bytes 4915204
  17.0 19.2 %copy-start.32 = (s32[4]{0:T(128)S(1)}, s32[4]{0:T(128)}, u32[]{:S(2)}) copy-start(s32[4]{0:T(128)} %kind_ref.5) | copy-start | bytes 52
  17.0 13.8 %collective-permute-start.5 = (bf16[4,80,2560]{2,1,0:T(8,128)(2,1)S(1)}, bf16[4,80,2560]{2,1,0:T(8,128)(2,1)}, u32[]{:S(2)}, u32[]{:S(2)}) collective-permute-start(bf16[4,80,2560]{2,1,0:T(8,128)(2,1)S(1)} %pad_maximum_fusion.rest_0_), channel_id=1, source_target_pairs={{0,1},{1,0},{2,3},{3,2},{4,5},{5,4},{6,7},{7,6},{8,9},{9,8},{10,11... | collective-permute-start | bytes 4915208 | tf_op jit(solution)/shard_map/ppermute | solution.py:418
  17.9 11.2 %collective-permute-start.6 = (bf16[1,80,2560]{2,1,0:T(8,128)(2,1)S(1)}, bf16[1,80,2560]{2,1,0:T(8,128)(2,1)}, u32[]{:S(2)}, u32[]{:S(2)}) collective-permute-start(bf16[1,80,2560]{2,1,0:T(8,128)(2,1)S(1)} %copy-done.6), channel_id=1, source_target_pairs={{0,2},{1,3},{2,4},{3,5},{4,6},{5,7},{6,0},{7,1},{8,10},{9,11},{10,... | collective-permute-start | bytes 1228808 | tf_op jit(solution)/shard_map/ppermute | solution.py:418
  18.7 10.9 %collective-permute-start.7 = (bf16[1,80,2560]{2,1,0:T(8,128)(2,1)S(1)}, bf16[1,80,2560]{2,1,0:T(8,128)(2,1)}, u32[]{:S(2)}, u32[]{:S(2)}) collective-permute-start(bf16[1,80,2560]{2,1,0:T(8,128)(2,1)S(1)} %copy-done.6), channel_id=1, source_target_pairs={{0,8},{1,9},{2,10},{3,11},{4,12},{5,13},{6,14},{7,15},{8,0},{9,1},... | collective-permute-start | bytes 1228808 | tf_op jit(solution)/shard_map/ppermute | solution.py:418
  20.2 10.7 %collective-permute-start.8 = (bf16[1,80,2560]{2,1,0:T(8,128)(2,1)S(1)}, bf16[1,80,2560]{2,1,0:T(8,128)(2,1)}, u32[]{:S(2)}, u32[]{:S(2)}) collective-permute-start(bf16[1,80,2560]{2,1,0:T(8,128)(2,1)S(1)} %copy-done.6), channel_id=1, source_target_pairs={{0,16},{1,17},{2,18},{3,19},{4,20},{5,21},{6,22},{7,23},{8,24},{9,... | collective-permute-start | bytes 1228808 | tf_op jit(solution)/shard_map/ppermute | solution.py:418
  30.8 6.8 %collective-permute-start.15 = (bf16[4,1280,128]{2,1,0:T(8,128)(2,1)}, bf16[4,1280,128]{2,1,0:T(8,128)(2,1)}, u32[]{:S(2)}, u32[]{:S(2)}) collective-permute-start(bf16[4,1280,128]{2,1,0:T(8,128)(2,1)} %get-tuple-element.57.ht_a), channel_id=1, source_target_pairs={{0,1},{1,0},{2,3},{3,2},{4,5},{5,4},{6,7},{7,6},{8,9},{9,8},{10,11... | collective-permute-start | bytes 3932168 | tf_op jit(solution)/shard_map/ppermute | solution.py:418
  31.5 13.8 %collective-permute-start.13 = (bf16[1,80,2560]{2,1,0:T(8,128)(2,1)}, bf16[1,80,2560]{2,1,0:T(8,128)(2,1)}, u32[]{:S(2)}, u32[]{:S(2)}) collective-permute-start(bf16[1,80,2560]{2,1,0:T(8,128)(2,1)} %collective-permute-done.6.rest_10_), channel_id=1, source_target_pairs={{0,8},{1,9},{2,10},{3,11},{4,12},{5,13},{6,14},{7,15},{8,0},{9,1},... | collective-permute-start | bytes 1228808 | tf_op jit(solution)/shard_map/ppermute | solution.py:418
  32.1 13.3 %collective-permute-start.14 = (bf16[1,80,2560]{2,1,0:T(8,128)(2,1)}, bf16[1,80,2560]{2,1,0:T(8,128)(2,1)}, u32[]{:S(2)}, u32[]{:S(2)}) collective-permute-start(bf16[1,80,2560]{2,1,0:T(8,128)(2,1)} %collective-permute-done.6.rest_10_), channel_id=1, source_target_pairs={{0,16},{1,17},{2,18},{3,19},{4,20},{5,21},{6,22},{7,23},{8,24},{9,... | collective-permute-start | bytes 1228808 | tf_op jit(solution)/shard_map/ppermute | solution.py:418
  33.6 11.8 %collective-permute-start.12 = (bf16[1,80,2560]{2,1,0:T(8,128)(2,1)}, bf16[1,80,2560]{2,1,0:T(8,128)(2,1)}, u32[]{:S(2)}, u32[]{:S(2)}) collective-permute-start(bf16[1,80,2560]{2,1,0:T(8,128)(2,1)} %copy-done.30), channel_id=1, source_target_pairs={{0,6},{1,7},{2,0},{3,1},{4,2},{5,3},{6,4},{7,5},{8,14},{9,15},{10,... | collective-permute-start | bytes 1228808 | tf_op jit(solution)/shard_map/ppermute | solution.py:418
  36.2 9.1 %collective-permute-start.9 = (bf16[1,80,2560]{2,1,0:T(8,128)(2,1)}, bf16[1,80,2560]{2,1,0:T(8,128)(2,1)}, u32[]{:S(2)}, u32[]{:S(2)}) collective-permute-start(bf16[1,80,2560]{2,1,0:T(8,128)(2,1)} %copy-done.5), channel_id=1, source_target_pairs={{0,1},{1,0},{2,3},{3,2},{4,5},{5,4},{6,7},{7,6},{8,9},{9,8},{10,11... | collective-permute-start | bytes 1228808 | tf_op jit(solution)/shard_map/ppermute | solution.py:418
  37.6 35.8 %copy-start.1 = (bf16[4,128,1280]{2,1,0:T(8,128)(2,1)S(1)}, bf16[4,128,1280]{2,1,0:T(8,128)(2,1)}, u32[]{:S(2)}) copy-start(bf16[4,128,1280]{2,1,0:T(8,128)(2,1)} %cot_ref.3) | copy-start | bytes 3932164
  45.4 11.4 %collective-permute-start.16 = (bf16[1,80,2560]{2,1,0:T(8,128)(2,1)}, bf16[1,80,2560]{2,1,0:T(8,128)(2,1)S(1)}, u32[]{:S(2)}, u32[]{:S(2)}) collective-permute-start(bf16[1,80,2560]{2,1,0:T(8,128)(2,1)} %fusion.7), channel_id=1, source_target_pairs={{0,2},{1,3},{2,4},{3,5},{4,6},{5,7},{6,0},{7,1},{8,10},{9,11},{10,... | collective-permute-start | bytes 1228808 | tf_op jit(solution)/shard_map/ppermute | solution.py:418
  47.2 9.6 %collective-permute-start.18 = (bf16[1,80,2560]{2,1,0:T(8,128)(2,1)}, bf16[1,80,2560]{2,1,0:T(8,128)(2,1)S(1)}, u32[]{:S(2)}, u32[]{:S(2)}) collective-permute-start(bf16[1,80,2560]{2,1,0:T(8,128)(2,1)} %collective-permute-done.6.rest_10_), channel_id=1, source_target_pairs={{0,1},{1,0},{2,3},{3,2},{4,5},{5,4},{6,7},{7,6},{8,9},{9,8},{10,11... | collective-permute-start | bytes 1228808 | tf_op jit(solution)/shard_map/ppermute | solution.py:418
  47.2 13.4 %collective-permute-start.21 = (bf16[1,80,2560]{2,1,0:T(8,128)(2,1)}, bf16[1,80,2560]{2,1,0:T(8,128)(2,1)S(1)}, u32[]{:S(2)}, u32[]{:S(2)}) collective-permute-start(bf16[1,80,2560]{2,1,0:T(8,128)(2,1)} %collective-permute-done.12.rest_18_), channel_id=1, source_target_pairs={{0,8},{1,9},{2,10},{3,11},{4,12},{5,13},{6,14},{7,15},{8,0},{9,1},... | collective-permute-start | bytes 1228808 | tf_op jit(solution)/shard_map/ppermute | solution.py:418
  48.7 12.1 %collective-permute-start.22 = (bf16[1,80,2560]{2,1,0:T(8,128)(2,1)}, bf16[1,80,2560]{2,1,0:T(8,128)(2,1)S(1)}, u32[]{:S(2)}, u32[]{:S(2)}) collective-permute-start(bf16[1,80,2560]{2,1,0:T(8,128)(2,1)} %collective-permute-done.12.rest_18_), channel_id=1, source_target_pairs={{0,16},{1,17},{2,18},{3,19},{4,20},{5,21},{6,22},{7,23},{8,24},{9,... | collective-permute-start | bytes 1228808 | tf_op jit(solution)/shard_map/ppermute | solution.py:418
  49.2 12.1 %collective-permute-start.11 = (bf16[1,80,2560]{2,1,0:T(8,128)(2,1)}, bf16[1,80,2560]{2,1,0:T(8,128)(2,1)S(1)}, u32[]{:S(2)}, u32[]{:S(2)}) collective-permute-start(bf16[1,80,2560]{2,1,0:T(8,128)(2,1)} %collective-permute-done.8.rest_6_), channel_id=1, source_target_pairs={{0,1},{1,0},{2,3},{3,2},{4,5},{5,4},{6,7},{7,6},{8,9},{9,8},{10,11... | collective-permute-start | bytes 1228808 | tf_op jit(solution)/shard_map/ppermute | solution.py:418
  56.8 19.7 %copy-start.7 = (bf16[1,80,2560]{2,1,0:T(8,128)(2,1)}, bf16[1,80,2560]{2,1,0:T(8,128)(2,1)S(1)}, u32[]{:S(2)}) copy-start(bf16[1,80,2560]{2,1,0:T(8,128)(2,1)S(1)} %collective-permute-done.16.rest_8_) | copy-start | bytes 1228804
  56.8 4.6 %collective-permute-start.10 = (bf16[1,80,2560]{2,1,0:T(8,128)(2,1)}, bf16[1,80,2560]{2,1,0:T(8,128)(2,1)S(1)}, u32[]{:S(2)}, u32[]{:S(2)}) collective-permute-start(bf16[1,80,2560]{2,1,0:T(8,128)(2,1)} %collective-permute-done.7.rest_4_), channel_id=1, source_target_pairs={{0,1},{1,0},{2,3},{3,2},{4,5},{5,4},{6,7},{7,6},{8,9},{9,8},{10,11... | collective-permute-start | bytes 1228808 | tf_op jit(solution)/shard_map/ppermute | solution.py:418
  56.8 19.7 %copy-start.8 = (bf16[1,80,2560]{2,1,0:T(8,128)(2,1)}, bf16[1,80,2560]{2,1,0:T(8,128)(2,1)S(1)}, u32[]{:S(2)}) copy-start(bf16[1,80,2560]{2,1,0:T(8,128)(2,1)S(1)} %collective-permute-done.18.rest_11_) | copy-start | bytes 1228804
  56.8 13.5 %collective-permute-start.28 = (bf16[1,80,2560]{2,1,0:T(8,128)(2,1)}, bf16[1,80,2560]{2,1,0:T(8,128)(2,1)S(1)}, u32[]{:S(2)}, u32[]{:S(2)}) collective-permute-start(bf16[1,80,2560]{2,1,0:T(8,128)(2,1)} %fusion.7), channel_id=1, source_target_pairs={{0,6},{1,7},{2,0},{3,1},{4,2},{5,3},{6,4},{7,5},{8,14},{9,15},{10,... | collective-permute-start | bytes 1228808 | tf_op jit(solution)/shard_map/ppermute | solution.py:418
  60.6 15.9 %copy-start.9 = (bf16[1,80,2560]{2,1,0:T(8,128)(2,1)}, bf16[1,80,2560]{2,1,0:T(8,128)(2,1)S(1)}, u32[]{:S(2)}) copy-start(bf16[1,80,2560]{2,1,0:T(8,128)(2,1)S(1)} %collective-permute-done.21.rest_20_) | copy-start | bytes 1228804
  60.6 9.7 %collective-permute-start.25 = (bf16[1,80,2560]{2,1,0:T(8,128)(2,1)}, bf16[1,80,2560]{2,1,0:T(8,128)(2,1)S(1)}, u32[]{:S(2)}, u32[]{:S(2)}) collective-permute-start(bf16[1,80,2560]{2,1,0:T(8,128)(2,1)} %collective-permute-done.12.rest_18_), channel_id=1, source_target_pairs={{0,1},{1,0},{2,3},{3,2},{4,5},{5,4},{6,7},{7,6},{8,9},{9,8},{10,11... | collective-permute-start | bytes 1228808 | tf_op jit(solution)/shard_map/ppermute | solution.py:418
  60.8 15.7 %copy-start.10 = (bf16[1,80,2560]{2,1,0:T(8,128)(2,1)}, bf16[1,80,2560]{2,1,0:T(8,128)(2,1)S(1)}, u32[]{:S(2)}) copy-start(bf16[1,80,2560]{2,1,0:T(8,128)(2,1)S(1)} %collective-permute-done.22.rest_22_) | copy-start | bytes 1228804
  60.8 11.9 %collective-permute-start.23 = (bf16[1,80,2560]{2,1,0:T(8,128)(2,1)}, bf16[1,80,2560]{2,1,0:T(8,128)(2,1)S(1)}, u32[]{:S(2)}, u32[]{:S(2)}) collective-permute-start(bf16[1,80,2560]{2,1,0:T(8,128)(2,1)} %collective-permute-done.13.rest_12_), channel_id=1, source_target_pairs={{0,16},{1,17},{2,18},{3,19},{4,20},{5,21},{6,22},{7,23},{8,24},{9,... | collective-permute-start | bytes 1228808 | tf_op jit(solution)/shard_map/ppermute | solution.py:418
  61.3 15.2 %copy-start.11 = (bf16[1,80,2560]{2,1,0:T(8,128)(2,1)}, bf16[1,80,2560]{2,1,0:T(8,128)(2,1)S(1)}, u32[]{:S(2)}) copy-start(bf16[1,80,2560]{2,1,0:T(8,128)(2,1)S(1)} %collective-permute-done.11.rest_7_) | copy-start | bytes 1228804
  61.3 11.4 %collective-permute-start.20 = (bf16[1,80,2560]{2,1,0:T(8,128)(2,1)}, bf16[1,80,2560]{2,1,0:T(8,128)(2,1)S(1)}, u32[]{:S(2)}, u32[]{:S(2)}) collective-permute-start(bf16[1,80,2560]{2,1,0:T(8,128)(2,1)} %collective-permute-done.14.rest_14_), channel_id=1, source_target_pairs={{0,1},{1,0},{2,3},{3,2},{4,5},{5,4},{6,7},{7,6},{8,9},{9,8},{10,11... | collective-permute-start | bytes 1228808 | tf_op jit(solution)/shard_map/ppermute | solution.py:418
  61.4 11.9 %collective-permute-start.19 = (bf16[1,80,2560]{2,1,0:T(8,128)(2,1)}, bf16[1,80,2560]{2,1,0:T(8,128)(2,1)S(1)}, u32[]{:S(2)}, u32[]{:S(2)}) collective-permute-start(bf16[1,80,2560]{2,1,0:T(8,128)(2,1)} %collective-permute-done.13.rest_12_), channel_id=1, source_target_pairs={{0,1},{1,0},{2,3},{3,2},{4,5},{5,4},{6,7},{7,6},{8,9},{9,8},{10,11... | collective-permute-start | bytes 1228808 | tf_op jit(solution)/shard_map/ppermute | solution.py:418
  70.3 3.1 %collective-permute-start.17 = (bf16[1,80,2560]{2,1,0:T(8,128)(2,1)S(1)}, bf16[1,80,2560]{2,1,0:T(8,128)(2,1)S(1)}, u32[]{:S(2)}, u32[]{:S(2)}) collective-permute-start(bf16[1,80,2560]{2,1,0:T(8,128)(2,1)S(1)} %collective-permute-done.16.rest_8_), channel_id=1, source_target_pairs={{0,1},{1,0},{2,3},{3,2},{4,5},{5,4},{6,7},{7,6},{8,9},{9,8},{10,11... | collective-permute-start | bytes 1228808 | tf_op jit(solution)/shard_map/ppermute | solution.py:418
  70.3 3.5 %collective-permute-start.26 = (bf16[1,80,2560]{2,1,0:T(8,128)(2,1)S(1)}, bf16[1,80,2560]{2,1,0:T(8,128)(2,1)S(1)}, u32[]{:S(2)}, u32[]{:S(2)}) collective-permute-start(bf16[1,80,2560]{2,1,0:T(8,128)(2,1)S(1)} %collective-permute-done.21.rest_20_), channel_id=1, source_target_pairs={{0,1},{1,0},{2,3},{3,2},{4,5},{5,4},{6,7},{7,6},{8,9},{9,8},{10,11... | collective-permute-start | bytes 1228808 | tf_op jit(solution)/shard_map/ppermute | solution.py:418
  72.7 1.7 collective-permute-start.27
  72.8 2.9 %collective-permute-start.29 = (bf16[1,80,2560]{2,1,0:T(8,128)(2,1)S(1)}, bf16[1,80,2560]{2,1,0:T(8,128)(2,1)S(1)}, u32[]{:S(2)}, u32[]{:S(2)}) collective-permute-start(bf16[1,80,2560]{2,1,0:T(8,128)(2,1)S(1)} %collective-permute-done.28.rest_24_), channel_id=1, source_target_pairs={{0,1},{1,0},{2,3},{3,2},{4,5},{5,4},{6,7},{7,6},{8,9},{9,8},{10,11... | collective-permute-start | bytes 1228808 | tf_op jit(solution)/shard_map/ppermute | solution.py:418
  73.3 3.2 %collective-permute-start.24 = (bf16[1,80,2560]{2,1,0:T(8,128)(2,1)S(1)}, bf16[1,80,2560]{2,1,0:T(8,128)(2,1)}, u32[]{:S(2)}, u32[]{:S(2)}) collective-permute-start(bf16[1,80,2560]{2,1,0:T(8,128)(2,1)S(1)} %collective-permute-done.23.rest_16_), channel_id=1, source_target_pairs={{0,1},{1,0},{2,3},{3,2},{4,5},{5,4},{6,7},{7,6},{8,9},{9,8},{10,11... | collective-permute-start | bytes 1228808 | tf_op jit(solution)/shard_map/ppermute | solution.py:418
  73.3 41.9 %collective-permute-start.34 = (bf16[4,128,1280]{2,1,0:T(8,128)(2,1)S(1)}, bf16[4,128,1280]{2,1,0:T(8,128)(2,1)}, u32[]{:S(2)}, u32[]{:S(2)}) collective-permute-start(bf16[4,128,1280]{2,1,0:T(8,128)(2,1)S(1)} %copy-done.1), channel_id=1, source_target_pairs={{0,1},{1,0},{2,3},{3,2},{4,5},{5,4},{6,7},{7,6},{8,9},{9,8},{10,11... | collective-permute-start | bytes 3932168 | tf_op jit(solution)/shard_map/ppermute | solution.py:418
  96.3 2.4 %collective-permute-start.30 = (bf16[4,128,640]{2,1,0:T(8,128)(2,1)}, bf16[4,128,640]{2,1,0:T(8,128)(2,1)S(1)}, u32[]{:S(2)}, u32[]{:S(2)}) collective-permute-start(bf16[4,128,640]{2,1,0:T(8,128)(2,1)} %get-tuple-element.67.rest_0_.dq_ref), channel_id=1, source_target_pairs={{0,1},{1,0},{2,3},{3,2},{4,5},{5,4},{6,7},{7,6},{8,9},{9,8},{10,11... | collective-permute-start | bytes 1966088 | tf_op jit(solution)/shard_map/ppermute | solution.py:418
  96.4 4.2 %collective-permute-start.31 = (bf16[4,128,640]{2,1,0:T(8,128)(2,1)}, bf16[4,128,640]{2,1,0:T(8,128)(2,1)S(1)}, u32[]{:S(2)}, u32[]{:S(2)}) collective-permute-start(bf16[4,128,640]{2,1,0:T(8,128)(2,1)} %get-tuple-element.68.rest_2_.dk_ref), channel_id=1, source_target_pairs={{0,1},{1,0},{2,3},{3,2},{4,5},{5,4},{6,7},{7,6},{8,9},{9,8},{10,11... | collective-permute-start | bytes 1966088 | tf_op jit(solution)/shard_map/ppermute | solution.py:418
  96.9 4.6 %collective-permute-start.32 = (bf16[4,128,640]{2,1,0:T(8,128)(2,1)}, bf16[4,128,640]{2,1,0:T(8,128)(2,1)S(1)}, u32[]{:S(2)}, u32[]{:S(2)}) collective-permute-start(bf16[4,128,640]{2,1,0:T(8,128)(2,1)} %get-tuple-element.69.rest_4_.dv_ref), channel_id=1, source_target_pairs={{0,1},{1,0},{2,3},{3,2},{4,5},{5,4},{6,7},{7,6},{8,9},{9,8},{10,11... | collective-permute-start | bytes 1966088 | tf_op jit(solution)/shard_map/ppermute | solution.py:418
  97.0 18.3 %collective-permute-start.33 = (bf16[4,640,128]{2,1,0:T(8,128)(2,1)}, bf16[4,640,128]{2,1,0:T(8,128)(2,1)}, u32[]{:S(2)}, u32[]{:S(2)}) collective-permute-start(bf16[4,640,128]{2,1,0:T(8,128)(2,1)} %get-tuple-element.74.attnt_a.attnt_ref), channel_id=1, source_target_pairs={{0,1},{1,0},{2,3},{3,2},{4,5},{5,4},{6,7},{7,6},{8,9},{9,8},{10,11... | collective-permute-start | bytes 1966088 | tf_op jit(solution)/shard_map/ppermute | solution.py:418
  113.6 31.1 %collective-permute-start.36 = (bf16[2,4,80,1024]{3,2,1,0:T(8,128)(2,1)}, bf16[2,4,80,1024]{3,2,1,0:T(8,128)(2,1)}, u32[]{:S(2)}, u32[]{:S(2)}) collective-permute-start(bf16[2,4,80,1024]{3,2,1,0:T(8,128)(2,1)} %get-tuple-element.70), channel_id=1, source_target_pairs={{0,16},{1,17},{2,18},{3,19},{4,20},{5,21},{6,22},{7,23},{8,24},{9,... | collective-permute-start | bytes 3932168 | tf_op jit(solution)/shard_map/ppermute | solution.py:418
  113.9 27.5 %collective-permute-start.37 = (bf16[2,4,80,896]{3,2,1,0:T(8,128)(2,1)}, bf16[2,4,80,896]{3,2,1,0:T(8,128)(2,1)}, u32[]{:S(2)}, u32[]{:S(2)}) collective-permute-start(bf16[2,4,80,896]{3,2,1,0:T(8,128)(2,1)} %get-tuple-element.79), channel_id=1, source_target_pairs={{0,8},{1,9},{2,10},{3,11},{4,12},{5,13},{6,14},{7,15},{8,0},{9,1},... | collective-permute-start | bytes 3440648 | tf_op jit(solution)/shard_map/ppermute | solution.py:418
  121.1 20.3 %collective-permute-start.35 = (bf16[2,4,80,640]{3,2,1,0:T(8,128)(2,1)}, bf16[2,4,80,640]{3,2,1,0:T(8,128)(2,1)}, u32[]{:S(2)}, u32[]{:S(2)}) collective-permute-start(bf16[2,4,80,640]{3,2,1,0:T(8,128)(2,1)} %get-tuple-element.78), channel_id=1, source_target_pairs={{0,2},{1,3},{2,0},{3,1},{4,6},{5,7},{6,4},{7,5},{8,10},{9,11},{10,... | collective-permute-start | bytes 2457608 | tf_op jit(solution)/shard_map/ppermute | solution.py:418
  146.3 13.2 %collective-permute-start.38 = (bf16[4,80,512]{2,1,0:T(8,128)(2,1)S(1)}, bf16[4,80,512]{2,1,0:T(8,128)(2,1)S(1)}, u32[]{:S(2)}, u32[]{:S(2)}) collective-permute-start(bf16[4,80,512]{2,1,0:T(8,128)(2,1)S(1)} %get-tuple-element.92), channel_id=1, source_target_pairs={{0,8},{1,9},{2,10},{3,11},{4,12},{5,13},{6,14},{7,15},{8,0},{9,1},... | collective-permute-start | bytes 983048 | tf_op jit(solution)/shard_map/ppermute | solution.py:418
  147.7 14.6 %collective-permute-start.44 = (bf16[4,80,512]{2,1,0:T(8,128)(2,1)S(1)}, bf16[4,80,512]{2,1,0:T(8,128)(2,1)S(1)}, u32[]{:S(2)}, u32[]{:S(2)}) collective-permute-start(bf16[4,80,512]{2,1,0:T(8,128)(2,1)S(1)} %get-tuple-element.93), channel_id=1, source_target_pairs={{0,8},{1,9},{2,10},{3,11},{4,12},{5,13},{6,14},{7,15},{8,0},{9,1},... | collective-permute-start | bytes 983048 | tf_op jit(solution)/shard_map/ppermute | solution.py:418
  149.4 9.1 %collective-permute-start.45 = (bf16[4,80,384]{2,1,0:T(8,128)(2,1)S(1)}, bf16[4,80,384]{2,1,0:T(8,128)(2,1)S(1)}, u32[]{:S(2)}, u32[]{:S(2)}) collective-permute-start(bf16[4,80,384]{2,1,0:T(8,128)(2,1)S(1)} %fusion.6), channel_id=1, source_target_pairs={{0,16},{1,17},{2,18},{3,19},{4,20},{5,21},{6,22},{7,23},{8,24},{9,... | collective-permute-start | bytes 737288 | tf_op jit(solution)/shard_map/ppermute | solution.py:418
  151.9 27.4 %collective-permute-start.50 = (bf16[4,80,640]{2,1,0:T(8,128)(2,1)S(1)}, bf16[4,80,640]{2,1,0:T(8,128)(2,1)S(1)}, u32[]{:S(2)}, u32[]{:S(2)}) collective-permute-start(bf16[4,80,640]{2,1,0:T(8,128)(2,1)S(1)} %fusion.1), channel_id=1, source_target_pairs={{0,4},{1,5},{2,6},{3,7},{4,0},{5,1},{6,2},{7,3},{8,12},{9,13},{10,... | collective-permute-start | bytes 1228808 | tf_op jit(solution)/shard_map/ppermute | solution.py:418
  156.7 13.9 %collective-permute-start.39 = (bf16[4,80,512]{2,1,0:T(8,128)(2,1)S(1)}, bf16[4,80,512]{2,1,0:T(8,128)(2,1)S(1)}, u32[]{:S(2)}, u32[]{:S(2)}) collective-permute-start(bf16[4,80,512]{2,1,0:T(8,128)(2,1)S(1)} %fusion.4), channel_id=1, source_target_pairs={{0,16},{1,17},{2,18},{3,19},{4,20},{5,21},{6,22},{7,23},{8,24},{9,... | collective-permute-start | bytes 983048 | tf_op jit(solution)/shard_map/ppermute | solution.py:418
  163.8 20.4 %collective-permute-start.46 = (bf16[80,896]{1,0:T(8,128)(2,1)S(1)}, bf16[80,896]{1,0:T(8,128)(2,1)S(1)}, u32[]{:S(2)}, u32[]{:S(2)}) collective-permute-start(bf16[80,896]{1,0:T(8,128)(2,1)S(1)} %get-tuple-element.104), channel_id=1, source_target_pairs={{0,2},{1,3},{2,4},{3,5},{4,6},{5,7},{6,0},{7,1},{8,10},{9,11},{10,... | collective-permute-start | bytes 430088 | tf_op jit(solution)/shard_map/ppermute | solution.py:418
  166.0 23.9 %collective-permute-start.47 = (bf16[80,896]{1,0:T(8,128)(2,1)S(1)}, bf16[80,896]{1,0:T(8,128)(2,1)S(1)}, u32[]{:S(2)}, u32[]{:S(2)}) collective-permute-start(bf16[80,896]{1,0:T(8,128)(2,1)S(1)} %get-tuple-element.106), channel_id=1, source_target_pairs={{0,4},{1,5},{2,6},{3,7},{4,0},{5,1},{6,2},{7,3},{8,12},{9,13},{10,... | collective-permute-start | bytes 430088 | tf_op jit(solution)/shard_map/ppermute | solution.py:418
  168.7 24.7 %collective-permute-start.48 = (bf16[80,896]{1,0:T(8,128)(2,1)S(1)}, bf16[80,896]{1,0:T(8,128)(2,1)S(1)}, u32[]{:S(2)}, u32[]{:S(2)}) collective-permute-start(bf16[80,896]{1,0:T(8,128)(2,1)S(1)} %get-tuple-element.105), channel_id=1, source_target_pairs={{0,6},{1,7},{2,0},{3,1},{4,2},{5,3},{6,4},{7,5},{8,14},{9,15},{10,... | collective-permute-start | bytes 430088 | tf_op jit(solution)/shard_map/ppermute | solution.py:418
  172.0 24.6 %collective-permute-start.40 = (bf16[80,1024]{1,0:T(8,128)(2,1)S(1)}, bf16[80,1024]{1,0:T(8,128)(2,1)S(1)}, u32[]{:S(2)}, u32[]{:S(2)}) collective-permute-start(bf16[80,1024]{1,0:T(8,128)(2,1)S(1)} %get-tuple-element.97), channel_id=1, source_target_pairs={{0,2},{1,3},{2,4},{3,5},{4,6},{5,7},{6,0},{7,1},{8,10},{9,11},{10,... | collective-permute-start | bytes 491528 | tf_op jit(solution)/shard_map/ppermute | solution.py:418
  179.3 18.7 %collective-permute-start.41 = (bf16[80,1024]{1,0:T(8,128)(2,1)S(1)}, bf16[80,1024]{1,0:T(8,128)(2,1)S(1)}, u32[]{:S(2)}, u32[]{:S(2)}) collective-permute-start(bf16[80,1024]{1,0:T(8,128)(2,1)S(1)} %get-tuple-element.99), channel_id=1, source_target_pairs={{0,4},{1,5},{2,6},{3,7},{4,0},{5,1},{6,2},{7,3},{8,12},{9,13},{10,... | collective-permute-start | bytes 491528 | tf_op jit(solution)/shard_map/ppermute | solution.py:418
  184.1 13.9 %collective-permute-start.42 = (bf16[80,1024]{1,0:T(8,128)(2,1)S(1)}, bf16[80,1024]{1,0:T(8,128)(2,1)S(1)}, u32[]{:S(2)}, u32[]{:S(2)}) collective-permute-start(bf16[80,1024]{1,0:T(8,128)(2,1)S(1)} %get-tuple-element.98), channel_id=1, source_target_pairs={{0,6},{1,7},{2,0},{3,1},{4,2},{5,3},{6,4},{7,5},{8,14},{9,15},{10,... | collective-permute-start | bytes 491528 | tf_op jit(solution)/shard_map/ppermute | solution.py:418
  193.6 7.8 %collective-permute-start.51 = (bf16[2,80,384]{2,1,0:T(8,128)(2,1)S(1)}, bf16[2,80,384]{2,1,0:T(8,128)(2,1)S(1)}, u32[]{:S(2)}, u32[]{:S(2)}) collective-permute-start(bf16[2,80,384]{2,1,0:T(8,128)(2,1)S(1)} %slice.200), channel_id=1, source_target_pairs={{0,16},{1,17},{2,18},{3,19},{4,20},{5,21},{6,22},{7,23},{8,24},{9,... | collective-permute-start | bytes 368648 | tf_op jit(solution)/shard_map/ppermute | solution.py:418
  195.0 4.8 %collective-permute-start.53 = (bf16[2,80,256]{2,1,0:T(8,128)(2,1)S(1)}, bf16[2,80,256]{2,1,0:T(8,128)(2,1)S(1)}, u32[]{:S(2)}, u32[]{:S(2)}) collective-permute-start(bf16[2,80,256]{2,1,0:T(8,128)(2,1)S(1)} %pad_maximum_fusion.3), channel_id=1, source_target_pairs={{0,8},{1,9},{2,10},{3,11},{4,12},{5,13},{6,14},{7,15},{8,0},{9,1},... | collective-permute-start | bytes 245768 | tf_op jit(solution)/shard_map/ppermute | solution.py:418
  196.6 7.3 %collective-permute-start.49 = (bf16[80,896]{1,0:T(8,128)(2,1)S(1)}, bf16[80,896]{1,0:T(8,128)(2,1)S(1)}, u32[]{:S(2)}, u32[]{:S(2)}) collective-permute-start(bf16[80,896]{1,0:T(8,128)(2,1)S(1)} %get-tuple-element.89), channel_id=1, source_target_pairs={{0,8},{1,9},{2,10},{3,11},{4,12},{5,13},{6,14},{7,15},{8,0},{9,1},... | collective-permute-start | bytes 430088 | tf_op jit(solution)/shard_map/ppermute | solution.py:418
  198.1 7.7 %collective-permute-start.43 = (bf16[80,1024]{1,0:T(8,128)(2,1)S(1)}, bf16[80,1024]{1,0:T(8,128)(2,1)S(1)}, u32[]{:S(2)}, u32[]{:S(2)}) collective-permute-start(bf16[80,1024]{1,0:T(8,128)(2,1)S(1)} %get-tuple-element.87), channel_id=1, source_target_pairs={{0,8},{1,9},{2,10},{3,11},{4,12},{5,13},{6,14},{7,15},{8,0},{9,1},... | collective-permute-start | bytes 491528 | tf_op jit(solution)/shard_map/ppermute | solution.py:418
  199.9 4.1 %collective-permute-start.54 = (bf16[80,256]{1,0:T(8,128)(2,1)S(1)}, bf16[80,256]{1,0:T(8,128)(2,1)S(1)}, u32[]{:S(2)}, u32[]{:S(2)}) collective-permute-start(bf16[80,256]{1,0:T(8,128)(2,1)S(1)} %fusion.16), channel_id=1, source_target_pairs={{0,16},{1,17},{2,18},{3,19},{4,20},{5,21},{6,22},{7,23},{8,24},{9,... | collective-permute-start | bytes 122888 | tf_op jit(solution)/shard_map/ppermute | solution.py:418
  201.4 6.9 %collective-permute-start.52 = (bf16[80,384]{1,0:T(8,128)(2,1)S(1)}, bf16[80,384]{1,0:T(8,128)(2,1)S(1)}, u32[]{:S(2)}, u32[]{:S(2)}) collective-permute-start(bf16[80,384]{1,0:T(8,128)(2,1)S(1)} %fusion.15), channel_id=1, source_target_pairs={{0,8},{1,9},{2,10},{3,11},{4,12},{5,13},{6,14},{7,15},{8,0},{9,1},... | collective-permute-start | bytes 184328 | tf_op jit(solution)/shard_map/ppermute | solution.py:418
  208.4 4.7 %collective-permute-start.55 = (bf16[80,640]{1,0:T(8,128)(2,1)S(1)}, bf16[80,640]{1,0:T(8,128)(2,1)S(1)}, u32[]{:S(2)}, u32[]{:S(2)}) collective-permute-start(bf16[80,640]{1,0:T(8,128)(2,1)S(1)} %fusion.20), channel_id=1, source_target_pairs={{0,8},{1,9},{2,10},{3,11},{4,12},{5,13},{6,14},{7,15},{8,0},{9,1},... | collective-permute-start | bytes 307208 | tf_op jit(solution)/shard_map/ppermute | solution.py:418
  (26 other events, 120.2 us)

commit v3 on v2

--- a/solution.py
+++ b/solution.py
@@ -273,7 +273,7 @@
                     )
 
 
-def out_terms_kernel(where_ref, kind_ref, attnt_a, attnt_b, cot_a, cot_b, own_ref, far_ref, sent_ref, left):
+def out_terms_kernel(where_ref, kind_ref, attnt_a, attnt_b, cot_a, cot_b, own_ref, sent_ref, left):
     g, z, c = where_ref[0], where_ref[1], where_ref[2]
     count = attnt_a.shape[0]
     rows = left.shape[2] // 4
@@ -284,7 +284,7 @@
             source = attnt_a if i < count else attnt_b
             keep = kind_ref[i] == kind
             for step in range(4):
-                row = pl.multiple_of((2 * (z ^ step) + c) * rows, 16)
+                row = pl.multiple_of((2 * lax.rem(z + step, 4) + c) * rows, 16)
                 value = source[i % count, pl.ds(row, rows), :]
                 left[far, i // count, step * rows : (step + 1) * rows, (i % count) * LANES : (i % count + 1) * LANES] = (
                     jnp.where(keep, value, jnp.zeros_like(value))
@@ -296,9 +296,8 @@
             total += dot_nn(left[far, 1], cot_b[:, :, span].reshape(-1, half_width))
             total = total.reshape(4, rows, half_width)
             own_ref[2 * far + side] = total[0]
-            far_ref[2 * far + side] = total[2]
-            sent_ref[0, 2 * far + side] = total[1].astype(BF16)
-            sent_ref[1, 2 * far + side] = total[3].astype(BF16)
+            for step in range(4):
+                sent_ref[lax.rem(z + step, 4), 2 * far + side] = total[step].astype(BF16)
 
 
 def qkv_terms_kernel(left, *rest):
@@ -358,11 +357,10 @@
         out_terms_kernel,
         out_shape=[
             jax.ShapeDtypeStruct((4, rows, width), F32),
-            jax.ShapeDtypeStruct((4, rows, width), F32),
-            jax.ShapeDtypeStruct((2, 4, rows, width), BF16),
+            jax.ShapeDtypeStruct((4, 4, rows, width), BF16),
         ],
         in_specs=[SMEM, SMEM] + [VMEM] * len(pairs),
-        out_specs=[VMEM] * 3,
+        out_specs=[VMEM] * 2,
         scratch_shapes=[pltpu.VMEM((2, 2, inner // 2, count * window), BF16)],
         compiler_params=params(),
         cost_estimate=cost(0.01),
@@ -406,8 +404,6 @@
         "sibling": make(lambda g, d: (g, d ^ 1)),
         "x": make(lambda g, d: (g ^ 1, d)),
         "y": make(lambda g, d: (g ^ 2, d)),
-        "z1": make(lambda g, d: (g, d ^ 2)),
-        "z2": make(lambda g, d: (g, d ^ 4)),
         "z": [
             make(lambda g, d, s=s: (g, (d // 2 + s) % chips * 2 + d % 2)) for s in range(chips)
         ],
@@ -473,17 +469,24 @@
     )
 
 
+def send_line(value):
+    count = lax.axis_size("dp")
+    lines = [list(range(core, count, 2)) for core in range(2)]
+    return lax.all_to_all(value, "dp", split_axis=0, concat_axis=0, axis_index_groups=lines, tiled=True)
+
+
+def add_line(own, arrived, z):
+    others = jnp.arange(arrived.shape[0]).reshape((-1,) + (1,) * own.ndim) != z
+    return own + jnp.sum(jnp.where(others, arrived.astype(F32), 0), axis=0)
+
+
 def line_parts(total, z):
     parts = [lax.dynamic_index_in_dim(total, (z + step) % 4, 0, keepdims=False) for step in range(4)]
     return [parts[0]] + [part.astype(BF16) for part in parts[1:]]
 
 
-def send_line(parts, route):
-    return [send(parts[step], route["z"][step]) for step in range(1, 4)]
-
-
-def add_line(own, arrived):
-    return own + sum(part.astype(F32) for part in arrived)
+def reduce_line(parts, route):
+    return parts[0] + sum(send(parts[step], route["z"][step]).astype(F32) for step in range(1, 4))
 
 
 def plane_terms(total, cut):
@@ -588,8 +591,8 @@
         far_x_other = sibling(far_x, far_other)
         far_y_other = sibling(far_y, far_other)
         back_other = sibling(back, far_other)
-        far_across = send(tied(far_x, back_x, back_y), route["y"])
-        back_across = send(tied(diagonal, near_across), route["z"][3])
+        far_across = send(tied(far_x, back), route["y"])
+        back_across = send(tied(diagonal, back), route["z"][3])
         weights = [quarters, quarters_other, near, near_other, near_x, near_x_other, near_y, near_y_other]
         weights += [near_across, sibling(near_across), far, far_other, far_x, far_x_other, far_y, far_y_other]
         weights += [far_across, sibling(far_across), back, back_other, back_x, sibling(back_x)]
@@ -636,31 +639,34 @@
         ]
         terms = qkv_terms(left, dq, dq_other, dk, dk_other, dv, dv_other)
         arrived = send_terms(terms, route)
-        out_own, out_far, out_sent = out_terms(
+        out_own, out_sent = out_terms(
             where, kinds, tied(attnt, terms[0]), attnt_other, cotangent, cot_other
         )
-        out_near = send(out_sent, route["z1"])
+        out_arrived = send_line(out_sent)
         encoded, block_grad = results(tied(attnt, out_own))
-        out_near, *arrived = lax.optimization_barrier((out_near, *arrived, encoded))[:3]
+        arrived = lax.optimization_barrier((*arrived, encoded))[:2]
         parts = []
         for first, last in STEPS:
             step_arrived = (arrived[0][..., first], arrived[1][..., last])
             own = jnp.concatenate([terms[2][..., :QKV_CUT][..., first], terms[2][..., QKV_CUT:][..., last]], axis=2)
             step_terms = (None, None, own, terms[3][..., first], terms[4][..., last])
             parts.append(line_parts(reduce_plane(step_terms, step_arrived, route), z))
-        out_next = send((out_far + out_near[1].astype(F32)).astype(BF16), route["z2"])
-        shares = [add_line(part[0], send_line(part, route)) for part in parts]
-        out_total = tied(out_own + out_near[0].astype(F32) + out_next.astype(F32), *parts[1])
-        terms = plane_terms(out_total, OUT_CUT)
-        share = reduce_plane(terms, send_terms(terms, route), route)
-        share_out = jnp.concatenate(both_halves(share, g, route), axis=1)
-        (first_a, first_b), (last_a, last_b) = [
-            tuple(zip(*[(half[:, :512], half[:, 512:]) for half in both_halves(share, g, route)]))
-            for share in shares
+        out_arrived = tied(out_arrived, *parts[0])
+        terms = plane_terms(add_line(out_own, out_arrived, z), OUT_CUT)
+        arrived = send_terms(terms, route)
+        parts[1][0] = tied(parts[1][0], *arrived)
+        shares = [reduce_line(part, route) for part in parts]
+        shares[1] = jnp.concatenate([shares[1], reduce_plane(terms, arrived, route)], axis=1)
+        first_halves, last_halves = [both_halves(share, g, route) for share in shares]
+        cut = last_halves[0].shape[1] - cotangent.shape[2] // 2
+        share_out = jnp.concatenate([half[:, cut:] for half in last_halves], axis=1)
+        columns_of = [
+            [half[:, :512] for half in first_halves],
+            [half[:, :512] for half in last_halves],
+            [half[:, 512:] for half in first_halves],
+            [half[:, 512:cut] for half in last_halves],
         ]
-        share_qkv = jnp.concatenate(
-            [jnp.concatenate(halves, axis=0) for halves in (first_a, last_a, first_b, last_b)], axis=1
-        )
+        share_qkv = jnp.concatenate([jnp.concatenate(halves, axis=0) for halves in columns_of], axis=1)
     else:
         encoded, block_grad = results(attnt)
         share_qkv, share_out = summed_terms(

time: 214 us -> 223 us (1.042)
  waiting for transfers between devices: 65.2 us -> 83.1 us
  starting transfers between devices: 62.6 us -> 50.1 us
    ppermute x56 -> x53, starting transfers between devices: 62.6 us -> 43.1 us  [send(): return lax.ppermute(value, AXES, route)]
    ppermute x56 -> x53, waiting for transfers between devices: 65.2 us -> 83.1 us  [send(): return lax.ppermute(value, AXES, route)]
    all_to_all x0 -> x1, starting transfers between devices: none -> 7.02 us  [send_line(): lax.all_to_all(value, 'dp', split_axis=0, concat_axis=0, axis_index_group...]
  transfers between devices with their start and end apart: 56 -> 54, of which waited for: 25 -> 27; matrix products, arithmetic and copies ran while one was open for 7% -> 8% of each run, Pallas kernels for 29% -> 19%
where the time goes in v3:
time: 223 us; the launch traced here: 221 us
  waiting for transfers between devices  83.1 us (37%)
  Pallas kernels  61 us (27%)
  starting transfers between devices  50.1 us (22%)
  other arithmetic  15 us (7%)
  local copies, waits for them, and re-layouts  10.8 us (5%)
    ppermute x53, waiting for transfers between devices, send(): return lax.ppermute(value, AXES, route)  83.1 us
    ppermute x53, starting transfers between devices, send(): return lax.ppermute(value, AXES, route)  43.1 us
    pallas_call x1, Pallas kernels, shards(): pl.pallas_call(functools.partial(layer_kernel, routed, n_weights), out_sh...  19.6 us
    pallas_call x1, Pallas kernels, results(): pl.pallas_call(functools.partial(result_kernel, routed, n_weights), out_s...  16 us
    pallas_call x1, Pallas kernels, qkv_terms(): pl.pallas_call(qkv_terms_kernel, out_shape=[jax.ShapeDtypeStruct((2, 4, r...  11.4 us
    all_to_all x1, starting transfers between devices, send_line(): lax.all_to_all(value, 'dp', split_axis=0, concat_axis=0, axis_index_group...  7.02 us
    pallas_call x1, Pallas kernels, out_terms(): pl.pallas_call(out_terms_kernel, out_shape=[jax.ShapeDtypeStruct((4, rows...  5.84 us
  transfers between devices with their start and end apart: 54, of which 27 were waited for; matrix products, arithmetic and copies ran while one was open for 8% of the time, Pallas kernels for 19%

profile of v3, /device:TPU:8, one launch (start us, length us, event | category | flops | bytes accessed | tf_op | source)
XLA Modules:
  0.0 221.4 jit_solution(4511290827838059396)
XLA Ops:
  0.7 1.0 constant_dynamic-slice_fusion.2
  1.7 0.9 constant_dynamic-slice_fusion.1
  2.7 1.6 collective-permute-start.4
  4.8 0.9 collective-permute-done
  5.7 1.6 collective-permute-start.1
  7.3 1.2 collective-permute-start.2
  9.6 4.5 %collective-permute-done.1 = f32[2,320]{1,0:T(2,128)S(1)} collective-permute-done((f32[2,320]{1,0:T(2,128)S(1)}, f32[2,320]{1,0:T(2,128)S(1)}, u32[]{:S(2)}, u32[]{:S(2)}) %collective-permute-start.1) | collective-permute-done | bytes 2592 | tf_op jit(solution)/shard_map/ppermute | solution.py:414
  14.2 0.9 collective-permute-done.2
  18.7 1.5 collective-permute-start.7
  20.2 1.5 collective-permute-start.8
  21.7 4.3 %norm.1 = (bf16[4,128,1280]{2,1,0:T(8,128)(2,1)}, bf16[4,1280,128]{2,1,0:T(8,128)(2,1)}) custom-call(s32[4]{0:T(128)} %kind_ref.5, bf16[4,128,1280]{2,1,0:T(8,128)(2,1)} %x_ref.2, f32[2,1280]{1,0:T(2,128)} %reshape.103.gain_ref), custom_call_target="tpu_custom_call" | custom-call | flops 11500000 | tf_op jit(solution)/shard_map/norm/pallas_call | solution.py:545
  26.0 3.1 %collective-permute-done.6.rest_10_ = bf16[1,80,2560]{2,1,0:T(8,128)(2,1)} collective-permute-done((bf16[1,80,2560]{2,1,0:T(8,128)(2,1)S(1)}, bf16[1,80,2560]{2,1,0:T(8,128)(2,1)}, u32[]{:S(2)}, u32[]{:S(2)}) %collective-permute-start.6) | collective-permute-done | bytes 409632 | tf_op jit(solution)/shard_map/ppermute | solution.py:414
  29.6 1.2 collective-permute-done.8.rest_6_
  31.4 1.5 collective-permute-start.14
  32.9 2.7 %collective-permute-start.12 = (bf16[1,80,2560]{2,1,0:T(8,128)(2,1)}, bf16[1,80,2560]{2,1,0:T(8,128)(2,1)}, u32[]{:S(2)}, u32[]{:S(2)}) collective-permute-start(bf16[1,80,2560]{2,1,0:T(8,128)(2,1)} %copy-done.25), channel_id=1, source_target_pairs={{0,6},{1,7},{2,0},{3,1},{4,2},{5,3},{6,4},{7,5},{8,14},{9,15},{10,... | collective-permute-start | bytes 1228808 | tf_op jit(solution)/shard_map/ppermute | solution.py:414
  36.9 3.9 %left_factor.1.left = bf16[2,2,640,512]{3,2,1,0:T(8,128)(2,1)} custom-call(s32[3]{0:T(128)} %pad_add_fusion.where_ref, s32[8]{0:T(128)} %pad_add_fusion.1.kind_ref, bf16[4,1280,128]{2,1,0:T(8,128)(2,1)} %get-tuple-element.55.ht_a, bf16[4,1280,128]{2,1,0:T(8,128)(2,1)} %collective-permute-done.15.ht_b), custom_call_target="tpu_custom_call" | custom-call | flops 11500000 | tf_op jit(solution)/shard_map/left_factor/pallas_call | solution.py:342
  40.7 3.9 %collective-permute-done.12.rest_18_ = bf16[1,80,2560]{2,1,0:T(8,128)(2,1)} collective-permute-done((bf16[1,80,2560]{2,1,0:T(8,128)(2,1)}, bf16[1,80,2560]{2,1,0:T(8,128)(2,1)}, u32[]{:S(2)}, u32[]{:S(2)}) %collective-permute-start.12) | collective-permute-done | bytes 409632 | tf_op jit(solution)/shard_map/ppermute | solution.py:414
  46.0 1.8 collective-permute-start.16
  47.7 1.5 collective-permute-start.28
  49.2 0.9 collective-permute-start.24
  50.1 1.0 collective-permute-start.26
  51.1 6.8 %collective-permute-done.21.rest_16_ = bf16[1,80,2560]{2,1,0:T(8,128)(2,1)S(1)} collective-permute-done((bf16[1,80,2560]{2,1,0:T(8,128)(2,1)}, bf16[1,80,2560]{2,1,0:T(8,128)(2,1)S(1)}, u32[]{:S(2)}, u32[]{:S(2)}) %collective-permute-start.21) | collective-permute-done | bytes 409632 | tf_op jit(solution)/shard_map/ppermute | solution.py:414
  58.7 10.5 %collective-permute-done.28.rest_24_ = bf16[1,80,2560]{2,1,0:T(8,128)(2,1)S(1)} collective-permute-done((bf16[1,80,2560]{2,1,0:T(8,128)(2,1)S(1)}, bf16[1,80,2560]{2,1,0:T(8,128)(2,1)S(1)}, u32[]{:S(2)}, u32[]{:S(2)}) %collective-permute-start.28) | collective-permute-done | bytes 409632 | tf_op jit(solution)/shard_map/ppermute | solution.py:414
  71.4 1.0 collective-permute-done.19.rest_13_
  72.8 1.2 collective-permute-done.25.rest_21_
  74.8 19.6 %layer.1 = (bf16[4,640,128]{2,1,0:T(8,128)(2,1)}, bf16[4,128,640]{2,1,0:T(8,128)(2,1)}, bf16[4,128,640]{2,1,0:T(8,128)(2,1)}, bf16[4,128,640]{2,1,0:T(8,128)(2,1)}) custom-call(s32[3]{0:T(128)} %pad_add_fusion.where_ref, s32[4]{0:T(128)} %kind_ref.5, bf16[4,128,1280]{2,1,0:T(8,128)(2,1)} %get-tuple-element.47.h_ref, bf16[4,128,1280]{2,1,0:T(8,128)(2,1)} %cot_ref.3, ...), custom_call_target="tpu_custom_call" | custom-call | flops 11500000 | tf_op jit(solution)/shard_map/layer/pallas_call | solution.py:611
  95.5 1.4 collective-permute-done.30.rest_1_
  96.9 1.9 collective-permute-done.31.rest_3_
  98.8 1.9 collective-permute-done.32.rest_5_
  100.7 11.4 %qkv_terms.1 = (bf16[2,4,80,1024]{3,2,1,0:T(8,128)(2,1)}, bf16[2,4,80,896]{3,2,1,0:T(8,128)(2,1)}, f32[4,80,1920]{2,1,0:T(8,128)}, f32[4,80,1024]{2,1,0:T(8,128)}, f32[4,80,896]{2,1,0:T(8,128)}) custom-call(bf16[2,2,640,512]{3,2,1,0:T(8,128)(2,1)} %left_factor.1.left, bf16[4,128,640]{2,1,0:T(8,128)(2,1)} %get-tuple-element.64.rest_0_.dq_ref, ...), custom_call_target="tpu_custom_call" | custom-call | flops 11500000 | tf_op jit(solution)/shard_map/qkv_terms/pallas_call | solution.py:374
  112.0 1.1 collective-permute-start.35
  113.2 1.6 collective-permute-start.36
  114.8 2.2 collective-permute-done.33.attnt_b
  117.0 5.8 %out_terms.1 = (f32[4,80,640]{2,1,0:T(8,128)}, bf16[4,4,80,640]{3,2,1,0:T(8,128)(2,1)}) custom-call(s32[3]{0:T(128)} %pad_add_fusion.where_ref, s32[8]{0:T(128)} %pad_add_fusion.1.kind_ref, bf16[4,640,128]{2,1,0:T(8,128)(2,1)} %get-tuple-element.71.attnt_a.attnt_ref, bf16[4,640,128]{2,1,0:T(8,128)(2,1)} %collective-permute-done.33.attnt_b, ...), custom_call_target="tpu_custom_call" | custom-call | flops 11500000 | tf_op jit(solution)/shard_map/out_terms/pallas_call | solution.py:356
  122.9 1.1 slice.165
  123.9 7.0 %all-to-all-start = ((bf16[4,4,80,640]{3,2,1,0:T(8,128)(2,1)}), bf16[4,4,80,640]{3,2,1,0:T(8,128)(2,1)S(1)}, u32[]{:S(2)}, u32[]{:S(2)}) async-start(bf16[4,4,80,640]{3,2,1,0:T(8,128)(2,1)} %get-tuple-element.80), calls=%async_computation | async-start | bytes 3276800 | tf_op jit(solution)/shard_map/all_to_all | solution.py:475
  131.0 16.0 %result.1 = (bf16[4,128,1280]{2,1,0:T(8,128)(2,1)}, bf16[4,128,1280]{2,1,0:T(8,128)(2,1)}) custom-call(s32[3]{0:T(128)} %pad_add_fusion.where_ref, s32[4]{0:T(128)} %kind_ref.5, s32[4]{0:T(128)} %rank_ref.1, bf16[4,128,1280]{2,1,0:T(8,128)(2,1)} %x_ref.2, bf16[4,128,1280]{2,1,0:T(8,128)(2,1)} %cot_ref.3, f32[2,1280]{1,0:T(2,128)} %reshape.103.gain_ref, ...), custom_call_target="tpu_custom_call" | custom-call | flops 11500000 | tf_op jit(solution)/shard_map/result/pallas_call | solution.py:625
  147.0 1.7 fusion.24
  148.9 1.1 fusion.4
  150.0 1.1 fusion.2
  151.1 2.1 collective-permute-start.38
  153.2 1.3 fusion.1
  154.5 2.0 collective-permute-start.43
  156.5 2.4 %collective-permute-done.44 = bf16[4,80,384]{2,1,0:T(8,128)(2,1)S(1)} collective-permute-done((bf16[4,80,384]{2,1,0:T(8,128)(2,1)S(1)}, bf16[4,80,384]{2,1,0:T(8,128)(2,1)S(1)}, u32[]{:S(2)}, u32[]{:S(2)}) %collective-permute-start.44) | collective-permute-done | bytes 245792 | tf_op jit(solution)/shard_map/ppermute | solution.py:414
  158.9 1.0 convert_add_fusion.7
  159.9 4.5 %collective-permute-done.38 = bf16[4,80,512]{2,1,0:T(8,128)(2,1)S(1)} collective-permute-done((bf16[4,80,512]{2,1,0:T(8,128)(2,1)S(1)}, bf16[4,80,512]{2,1,0:T(8,128)(2,1)S(1)}, u32[]{:S(2)}, u32[]{:S(2)}) %collective-permute-start.38) | collective-permute-done | bytes 327712 | tf_op jit(solution)/shard_map/ppermute | solution.py:414
  164.4 1.1 convert_add_fusion.3
  165.5 4.6 %collective-permute-done.43 = bf16[4,80,512]{2,1,0:T(8,128)(2,1)S(1)} collective-permute-done((bf16[4,80,512]{2,1,0:T(8,128)(2,1)S(1)}, bf16[4,80,512]{2,1,0:T(8,128)(2,1)S(1)}, u32[]{:S(2)}, u32[]{:S(2)}) %collective-permute-start.43) | collective-permute-done | bytes 327712 | tf_op jit(solution)/shard_map/ppermute | solution.py:414
  170.1 1.2 convert_add_fusion.1
  171.6 1.6 collective-permute-start.39
  173.2 1.0 collective-permute-start.40
  174.2 1.8 collective-permute-start.41
  177.2 3.7 %collective-permute-start.48 = (bf16[80,896]{1,0:T(8,128)(2,1)}, bf16[80,896]{1,0:T(8,128)(2,1)}, u32[]{:S(2)}, u32[]{:S(2)}) collective-permute-start(bf16[80,896]{1,0:T(8,128)(2,1)} %get-tuple-element.102), channel_id=1, source_target_pairs={{0,4},{1,5},{2,6},{3,7},{4,0},{5,1},{6,2},{7,3},{8,12},{9,13},{10,... | collective-permute-start | bytes 430088 | tf_op jit(solution)/shard_map/ppermute | solution.py:414
  180.9 2.3 %collective-permute-done.39 = bf16[80,1024]{1,0:T(8,128)(2,1)S(1)} collective-permute-done((bf16[80,1024]{1,0:T(8,128)(2,1)S(1)}, bf16[80,1024]{1,0:T(8,128)(2,1)S(1)}, u32[]{:S(2)}, u32[]{:S(2)}) %collective-permute-start.39) | collective-permute-done | bytes 163872 | tf_op jit(solution)/shard_map/ppermute | solution.py:414
  183.3 10.5 %collective-permute-done.40 = bf16[80,1024]{1,0:T(8,128)(2,1)S(1)} collective-permute-done((bf16[80,1024]{1,0:T(8,128)(2,1)S(1)}, bf16[80,1024]{1,0:T(8,128)(2,1)S(1)}, u32[]{:S(2)}, u32[]{:S(2)}) %collective-permute-start.40) | collective-permute-done | bytes 163872 | tf_op jit(solution)/shard_map/ppermute | solution.py:414
  196.4 1.5 collective-permute-start.46
  197.9 3.4 %collective-permute-done.42 = bf16[80,1024]{1,0:T(8,128)(2,1)} collective-permute-done((bf16[80,1024]{1,0:T(8,128)(2,1)}, bf16[80,1024]{1,0:T(8,128)(2,1)}, u32[]{:S(2)}, u32[]{:S(2)}) %collective-permute-start.42) | collective-permute-done | bytes 163872 | tf_op jit(solution)/shard_map/ppermute | solution.py:414
  201.3 1.0 convert_select_fusion.3
  202.9 1.6 collective-permute-start.51
  204.5 2.8 %collective-permute-done.45 = bf16[2,80,384]{2,1,0:T(8,128)(2,1)S(1)} collective-permute-done((bf16[2,80,384]{2,1,0:T(8,128)(2,1)S(1)}, bf16[2,80,384]{2,1,0:T(8,128)(2,1)S(1)}, u32[]{:S(2)}, u32[]{:S(2)}) %collective-permute-start.45) | collective-permute-done | bytes 122912 | tf_op jit(solution)/shard_map/ppermute | solution.py:414
  207.9 1.1 add_add_fusion.1
  209.1 3.1 %collective-permute-done.50 = bf16[80,384]{1,0:T(8,128)(2,1)S(1)} collective-permute-done((bf16[80,384]{1,0:T(8,128)(2,1)S(1)}, bf16[80,384]{1,0:T(8,128)(2,1)S(1)}, u32[]{:S(2)}, u32[]{:S(2)}) %collective-permute-start.50) | collective-permute-done | bytes 61472 | tf_op jit(solution)/shard_map/ppermute | solution.py:414
  213.0 5.6 %collective-permute-done.52 = bf16[80,1536]{1,0:T(8,128)(2,1)S(1)} collective-permute-done((bf16[80,1536]{1,0:T(8,128)(2,1)S(1)}, bf16[80,1536]{1,0:T(8,128)(2,1)S(1)}, u32[]{:S(2)}, u32[]{:S(2)}) %collective-permute-start.52) | collective-permute-done | bytes 245792 | tf_op jit(solution)/shard_map/ppermute | solution.py:414
  218.8 1.2 fusion
  (185 shorter events, 21.5 us)
Async XLA Ops:
  2.7 14.2 %copy-start.2 = (bf16[2,160,1920]{2,1,0:T(8,128)(2,1)S(1)}, bf16[2,160,1920]{2,1,0:T(8,128)(2,1)}, u32[]{:S(2)}) copy-start(bf16[2,160,1920]{2,1,0:T(8,128)(2,1)} %param.11) | copy-start | bytes 3686404
  2.7 13.4 %copy-start.25 = (bf16[1,80,2560]{2,1,0:T(8,128)(2,1)}, bf16[1,80,2560]{2,1,0:T(8,128)(2,1)S(1)}, u32[]{:S(2)}) copy-start(bf16[1,80,2560]{2,1,0:T(8,128)(2,1)S(1)} %pad_maximum_fusion.2) | copy-start | bytes 1228804
  2.7 13.4 %collective-permute-start.4 = (bf16[1,80,2560]{2,1,0:T(8,128)(2,1)S(1)}, bf16[1,80,2560]{2,1,0:T(8,128)(2,1)S(1)}, u32[]{:S(2)}, u32[]{:S(2)}) collective-permute-start(bf16[1,80,2560]{2,1,0:T(8,128)(2,1)S(1)} %pad_maximum_fusion.2), channel_id=1, source_target_pairs={{0,2},{1,3},{2,4},{3,5},{4,6},{5,7},{6,0},{7,1},{8,10},{9,11},{10,... | collective-permute-start | bytes 1228808 | tf_op jit(solution)/shard_map/ppermute | solution.py:414
  4.5 1.2 collective-permute-start
  5.7 8.4 %collective-permute-start.1 = (f32[2,320]{1,0:T(2,128)S(1)}, f32[2,320]{1,0:T(2,128)S(1)}, u32[]{:S(2)}, u32[]{:S(2)}) collective-permute-start(f32[2,320]{1,0:T(2,128)S(1)} %pad_maximum_fusion.5), channel_id=1, source_target_pairs={{0,2},{1,3},{2,4},{3,5},{4,6},{5,7},{6,0},{7,1},{8,10},{9,11},{10,... | collective-permute-start | bytes 7688 | tf_op jit(solution)/shard_map/ppermute | solution.py:414
  7.3 7.8 %collective-permute-start.2 = (f32[2,320]{1,0:T(2,128)S(1)}, f32[2,320]{1,0:T(2,128)S(1)}, u32[]{:S(2)}, u32[]{:S(2)}) collective-permute-start(f32[2,320]{1,0:T(2,128)S(1)} %pad_maximum_fusion.5), channel_id=1, source_target_pairs={{0,4},{1,5},{2,6},{3,7},{4,0},{5,1},{6,2},{7,3},{8,12},{9,13},{10,... | collective-permute-start | bytes 7688 | tf_op jit(solution)/shard_map/ppermute | solution.py:414
  8.6 6.6 %collective-permute-start.3 = (f32[2,320]{1,0:T(2,128)S(1)}, f32[2,320]{1,0:T(2,128)S(1)}, u32[]{:S(2)}, u32[]{:S(2)}) collective-permute-start(f32[2,320]{1,0:T(2,128)S(1)} %pad_maximum_fusion.5), channel_id=1, source_target_pairs={{0,6},{1,7},{2,0},{3,1},{4,2},{5,3},{6,4},{7,5},{8,14},{9,15},{10,... | collective-permute-start | bytes 7688 | tf_op jit(solution)/shard_map/ppermute | solution.py:414
  17.0 23.7 %copy-start = (bf16[4,80,2560]{2,1,0:T(8,128)(2,1)}, bf16[4,80,2560]{2,1,0:T(8,128)(2,1)S(1)}, u32[]{:S(2)}) copy-start(bf16[4,80,2560]{2,1,0:T(8,128)(2,1)S(1)} %pad_maximum_fusion.rest_0_) | copy-start | bytes 4915204
  17.0 19.3 %copy-start.27 = (s32[4]{0:T(128)S(1)}, s32[4]{0:T(128)}, u32[]{:S(2)}) copy-start(s32[4]{0:T(128)} %kind_ref.5) | copy-start | bytes 52
  17.0 13.8 %collective-permute-start.5 = (bf16[4,80,2560]{2,1,0:T(8,128)(2,1)S(1)}, bf16[4,80,2560]{2,1,0:T(8,128)(2,1)}, u32[]{:S(2)}, u32[]{:S(2)}) collective-permute-start(bf16[4,80,2560]{2,1,0:T(8,128)(2,1)S(1)} %pad_maximum_fusion.rest_0_), channel_id=1, source_target_pairs={{0,1},{1,0},{2,3},{3,2},{4,5},{5,4},{6,7},{7,6},{8,9},{9,8},{10,11... | collective-permute-start | bytes 4915208 | tf_op jit(solution)/shard_map/ppermute | solution.py:414
  17.9 11.2 %collective-permute-start.6 = (bf16[1,80,2560]{2,1,0:T(8,128)(2,1)S(1)}, bf16[1,80,2560]{2,1,0:T(8,128)(2,1)}, u32[]{:S(2)}, u32[]{:S(2)}) collective-permute-start(bf16[1,80,2560]{2,1,0:T(8,128)(2,1)S(1)} %copy-done.5), channel_id=1, source_target_pairs={{0,2},{1,3},{2,4},{3,5},{4,6},{5,7},{6,0},{7,1},{8,10},{9,11},{10,... | collective-permute-start | bytes 1228808 | tf_op jit(solution)/shard_map/ppermute | solution.py:414
  18.7 10.9 %collective-permute-start.7 = (bf16[1,80,2560]{2,1,0:T(8,128)(2,1)S(1)}, bf16[1,80,2560]{2,1,0:T(8,128)(2,1)}, u32[]{:S(2)}, u32[]{:S(2)}) collective-permute-start(bf16[1,80,2560]{2,1,0:T(8,128)(2,1)S(1)} %copy-done.5), channel_id=1, source_target_pairs={{0,8},{1,9},{2,10},{3,11},{4,12},{5,13},{6,14},{7,15},{8,0},{9,1},... | collective-permute-start | bytes 1228808 | tf_op jit(solution)/shard_map/ppermute | solution.py:414
  20.2 10.7 %collective-permute-start.8 = (bf16[1,80,2560]{2,1,0:T(8,128)(2,1)S(1)}, bf16[1,80,2560]{2,1,0:T(8,128)(2,1)}, u32[]{:S(2)}, u32[]{:S(2)}) collective-permute-start(bf16[1,80,2560]{2,1,0:T(8,128)(2,1)S(1)} %copy-done.5), channel_id=1, source_target_pairs={{0,16},{1,17},{2,18},{3,19},{4,20},{5,21},{6,22},{7,23},{8,24},{9,... | collective-permute-start | bytes 1228808 | tf_op jit(solution)/shard_map/ppermute | solution.py:414
  30.8 6.0 %collective-permute-start.15 = (bf16[4,1280,128]{2,1,0:T(8,128)(2,1)}, bf16[4,1280,128]{2,1,0:T(8,128)(2,1)}, u32[]{:S(2)}, u32[]{:S(2)}) collective-permute-start(bf16[4,1280,128]{2,1,0:T(8,128)(2,1)} %get-tuple-element.55.ht_a), channel_id=1, source_target_pairs={{0,1},{1,0},{2,3},{3,2},{4,5},{5,4},{6,7},{7,6},{8,9},{9,8},{10,11... | collective-permute-start | bytes 3932168 | tf_op jit(solution)/shard_map/ppermute | solution.py:414
  30.8 13.9 %collective-permute-start.13 = (bf16[1,80,2560]{2,1,0:T(8,128)(2,1)}, bf16[1,80,2560]{2,1,0:T(8,128)(2,1)}, u32[]{:S(2)}, u32[]{:S(2)}) collective-permute-start(bf16[1,80,2560]{2,1,0:T(8,128)(2,1)} %collective-permute-done.6.rest_10_), channel_id=1, source_target_pairs={{0,8},{1,9},{2,10},{3,11},{4,12},{5,13},{6,14},{7,15},{8,0},{9,1},... | collective-permute-start | bytes 1228808 | tf_op jit(solution)/shard_map/ppermute | solution.py:414
  31.4 13.3 %collective-permute-start.14 = (bf16[1,80,2560]{2,1,0:T(8,128)(2,1)}, bf16[1,80,2560]{2,1,0:T(8,128)(2,1)}, u32[]{:S(2)}, u32[]{:S(2)}) collective-permute-start(bf16[1,80,2560]{2,1,0:T(8,128)(2,1)} %collective-permute-done.6.rest_10_), channel_id=1, source_target_pairs={{0,16},{1,17},{2,18},{3,19},{4,20},{5,21},{6,22},{7,23},{8,24},{9,... | collective-permute-start | bytes 1228808 | tf_op jit(solution)/shard_map/ppermute | solution.py:414
  32.9 11.8 %collective-permute-start.12 = (bf16[1,80,2560]{2,1,0:T(8,128)(2,1)}, bf16[1,80,2560]{2,1,0:T(8,128)(2,1)}, u32[]{:S(2)}, u32[]{:S(2)}) collective-permute-start(bf16[1,80,2560]{2,1,0:T(8,128)(2,1)} %copy-done.25), channel_id=1, source_target_pairs={{0,6},{1,7},{2,0},{3,1},{4,2},{5,3},{6,4},{7,5},{8,14},{9,15},{10,... | collective-permute-start | bytes 1228808 | tf_op jit(solution)/shard_map/ppermute | solution.py:414
  35.6 9.1 %collective-permute-start.9 = (bf16[1,80,2560]{2,1,0:T(8,128)(2,1)S(1)}, bf16[1,80,2560]{2,1,0:T(8,128)(2,1)}, u32[]{:S(2)}, u32[]{:S(2)}) collective-permute-start(bf16[1,80,2560]{2,1,0:T(8,128)(2,1)S(1)} %copy-done.5), channel_id=1, source_target_pairs={{0,1},{1,0},{2,3},{3,2},{4,5},{5,4},{6,7},{7,6},{8,9},{9,8},{10,11... | collective-permute-start | bytes 1228808 | tf_op jit(solution)/shard_map/ppermute | solution.py:414
  44.7 3.0 %collective-permute-start.18 = (bf16[1,80,2560]{2,1,0:T(8,128)(2,1)}, bf16[1,80,2560]{2,1,0:T(8,128)(2,1)S(1)}, u32[]{:S(2)}, u32[]{:S(2)}) collective-permute-start(bf16[1,80,2560]{2,1,0:T(8,128)(2,1)} %collective-permute-done.6.rest_10_), channel_id=1, source_target_pairs={{0,1},{1,0},{2,3},{3,2},{4,5},{5,4},{6,7},{7,6},{8,9},{9,8},{10,11... | collective-permute-start | bytes 1228808 | tf_op jit(solution)/shard_map/ppermute | solution.py:414
  44.8 50.2 %copy-start.1 = (bf16[4,128,1280]{2,1,0:T(8,128)(2,1)S(1)}, bf16[4,128,1280]{2,1,0:T(8,128)(2,1)}, u32[]{:S(2)}) copy-start(bf16[4,128,1280]{2,1,0:T(8,128)(2,1)} %cot_ref.3) | copy-start | bytes 3932164
  44.8 4.4 %collective-permute-start.11 = (bf16[1,80,2560]{2,1,0:T(8,128)(2,1)}, bf16[1,80,2560]{2,1,0:T(8,128)(2,1)S(1)}, u32[]{:S(2)}, u32[]{:S(2)}) collective-permute-start(bf16[1,80,2560]{2,1,0:T(8,128)(2,1)} %collective-permute-done.8.rest_6_), channel_id=1, source_target_pairs={{0,1},{1,0},{2,3},{3,2},{4,5},{5,4},{6,7},{7,6},{8,9},{9,8},{10,11... | collective-permute-start | bytes 1228808 | tf_op jit(solution)/shard_map/ppermute | solution.py:414
  45.4 4.8 %collective-permute-start.10 = (bf16[1,80,2560]{2,1,0:T(8,128)(2,1)}, bf16[1,80,2560]{2,1,0:T(8,128)(2,1)S(1)}, u32[]{:S(2)}, u32[]{:S(2)}) collective-permute-start(bf16[1,80,2560]{2,1,0:T(8,128)(2,1)} %collective-permute-done.7.rest_4_), channel_id=1, source_target_pairs={{0,1},{1,0},{2,3},{3,2},{4,5},{5,4},{6,7},{7,6},{8,9},{9,8},{10,11... | collective-permute-start | bytes 1228808 | tf_op jit(solution)/shard_map/ppermute | solution.py:414
  45.5 12.5 %collective-permute-start.21 = (bf16[1,80,2560]{2,1,0:T(8,128)(2,1)}, bf16[1,80,2560]{2,1,0:T(8,128)(2,1)S(1)}, u32[]{:S(2)}, u32[]{:S(2)}) collective-permute-start(bf16[1,80,2560]{2,1,0:T(8,128)(2,1)} %collective-permute-done.13.rest_12_), channel_id=1, source_target_pairs={{0,16},{1,17},{2,18},{3,19},{4,20},{5,21},{6,22},{7,23},{8,24},{9,... | collective-permute-start | bytes 1228808 | tf_op jit(solution)/shard_map/ppermute | solution.py:414
  46.0 12.7 %collective-permute-start.16 = (bf16[1,80,2560]{2,1,0:T(8,128)(2,1)S(1)}, bf16[1,80,2560]{2,1,0:T(8,128)(2,1)S(1)}, u32[]{:S(2)}, u32[]{:S(2)}) collective-permute-start(bf16[1,80,2560]{2,1,0:T(8,128)(2,1)S(1)} %fusion.5), channel_id=1, source_target_pairs={{0,2},{1,3},{2,4},{3,5},{4,6},{5,7},{6,0},{7,1},{8,10},{9,11},{10,... | collective-permute-start | bytes 1228808 | tf_op jit(solution)/shard_map/ppermute | solution.py:414
  47.7 27.0 %copy-start.6 = (bf16[1,80,2560]{2,1,0:T(8,128)(2,1)}, bf16[1,80,2560]{2,1,0:T(8,128)(2,1)S(1)}, u32[]{:S(2)}) copy-start(bf16[1,80,2560]{2,1,0:T(8,128)(2,1)S(1)} %collective-permute-done.18.rest_11_) | copy-start | bytes 1228804
  47.7 21.5 %collective-permute-start.28 = (bf16[1,80,2560]{2,1,0:T(8,128)(2,1)S(1)}, bf16[1,80,2560]{2,1,0:T(8,128)(2,1)S(1)}, u32[]{:S(2)}, u32[]{:S(2)}) collective-permute-start(bf16[1,80,2560]{2,1,0:T(8,128)(2,1)S(1)} %fusion.5), channel_id=1, source_target_pairs={{0,6},{1,7},{2,0},{3,1},{4,2},{5,3},{6,4},{7,5},{8,14},{9,15},{10,... | collective-permute-start | bytes 1228808 | tf_op jit(solution)/shard_map/ppermute | solution.py:414
  49.2 25.6 %copy-start.7 = (bf16[1,80,2560]{2,1,0:T(8,128)(2,1)}, bf16[1,80,2560]{2,1,0:T(8,128)(2,1)S(1)}, u32[]{:S(2)}) copy-start(bf16[1,80,2560]{2,1,0:T(8,128)(2,1)S(1)} %collective-permute-done.11.rest_7_) | copy-start | bytes 1228804
  49.2 20.1 %collective-permute-start.24 = (bf16[1,80,2560]{2,1,0:T(8,128)(2,1)}, bf16[1,80,2560]{2,1,0:T(8,128)(2,1)S(1)}, u32[]{:S(2)}, u32[]{:S(2)}) collective-permute-start(bf16[1,80,2560]{2,1,0:T(8,128)(2,1)} %collective-permute-done.12.rest_18_), channel_id=1, source_target_pairs={{0,8},{1,9},{2,10},{3,11},{4,12},{5,13},{6,14},{7,15},{8,0},{9,1},... | collective-permute-start | bytes 1228808 | tf_op jit(solution)/shard_map/ppermute | solution.py:414
  50.1 24.6 %copy-start.8 = (bf16[1,80,2560]{2,1,0:T(8,128)(2,1)}, bf16[1,80,2560]{2,1,0:T(8,128)(2,1)S(1)}, u32[]{:S(2)}) copy-start(bf16[1,80,2560]{2,1,0:T(8,128)(2,1)S(1)} %collective-permute-done.10.rest_5_) | copy-start | bytes 1228804
  50.1 19.7 %collective-permute-start.26 = (bf16[1,80,2560]{2,1,0:T(8,128)(2,1)}, bf16[1,80,2560]{2,1,0:T(8,128)(2,1)S(1)}, u32[]{:S(2)}, u32[]{:S(2)}) collective-permute-start(bf16[1,80,2560]{2,1,0:T(8,128)(2,1)} %collective-permute-done.12.rest_18_), channel_id=1, source_target_pairs={{0,16},{1,17},{2,18},{3,19},{4,20},{5,21},{6,22},{7,23},{8,24},{9,... | collective-permute-start | bytes 1228808 | tf_op jit(solution)/shard_map/ppermute | solution.py:414
  57.9 11.9 %collective-permute-start.23 = (bf16[1,80,2560]{2,1,0:T(8,128)(2,1)}, bf16[1,80,2560]{2,1,0:T(8,128)(2,1)S(1)}, u32[]{:S(2)}, u32[]{:S(2)}) collective-permute-start(bf16[1,80,2560]{2,1,0:T(8,128)(2,1)} %collective-permute-done.12.rest_18_), channel_id=1, source_target_pairs={{0,1},{1,0},{2,3},{3,2},{4,5},{5,4},{6,7},{7,6},{8,9},{9,8},{10,11... | collective-permute-start | bytes 1228808 | tf_op jit(solution)/shard_map/ppermute | solution.py:414
  58.7 11.6 %copy-start.10 = (bf16[1,80,2560]{2,1,0:T(8,128)(2,1)}, bf16[1,80,2560]{2,1,0:T(8,128)(2,1)S(1)}, u32[]{:S(2)}) copy-start(bf16[1,80,2560]{2,1,0:T(8,128)(2,1)S(1)} %collective-permute-done.16.rest_8_) | copy-start | bytes 1228804
  58.7 11.6 %collective-permute-start.22 = (bf16[1,80,2560]{2,1,0:T(8,128)(2,1)S(1)}, bf16[1,80,2560]{2,1,0:T(8,128)(2,1)S(1)}, u32[]{:S(2)}, u32[]{:S(2)}) collective-permute-start(bf16[1,80,2560]{2,1,0:T(8,128)(2,1)S(1)} %collective-permute-done.21.rest_16_), channel_id=1, source_target_pairs={{0,1},{1,0},{2,3},{3,2},{4,5},{5,4},{6,7},{7,6},{8,9},{9,8},{10,11... | collective-permute-start | bytes 1228808 | tf_op jit(solution)/shard_map/ppermute | solution.py:414
  69.3 2.0 collective-permute-start.20
  69.3 3.1 %collective-permute-start.19 = (bf16[1,80,2560]{2,1,0:T(8,128)(2,1)}, bf16[1,80,2560]{2,1,0:T(8,128)(2,1)S(1)}, u32[]{:S(2)}, u32[]{:S(2)}) collective-permute-start(bf16[1,80,2560]{2,1,0:T(8,128)(2,1)} %collective-permute-done.13.rest_12_), channel_id=1, source_target_pairs={{0,1},{1,0},{2,3},{3,2},{4,5},{5,4},{6,7},{7,6},{8,9},{9,8},{10,11... | collective-permute-start | bytes 1228808 | tf_op jit(solution)/shard_map/ppermute | solution.py:414
  69.8 2.6 %collective-permute-start.17 = (bf16[1,80,2560]{2,1,0:T(8,128)(2,1)S(1)}, bf16[1,80,2560]{2,1,0:T(8,128)(2,1)S(1)}, u32[]{:S(2)}, u32[]{:S(2)}) collective-permute-start(bf16[1,80,2560]{2,1,0:T(8,128)(2,1)S(1)} %collective-permute-done.16.rest_8_), channel_id=1, source_target_pairs={{0,1},{1,0},{2,3},{3,2},{4,5},{5,4},{6,7},{7,6},{8,9},{9,8},{10,11... | collective-permute-start | bytes 1228808 | tf_op jit(solution)/shard_map/ppermute | solution.py:414
  69.9 2.9 %collective-permute-start.29 = (bf16[1,80,2560]{2,1,0:T(8,128)(2,1)S(1)}, bf16[1,80,2560]{2,1,0:T(8,128)(2,1)S(1)}, u32[]{:S(2)}, u32[]{:S(2)}) collective-permute-start(bf16[1,80,2560]{2,1,0:T(8,128)(2,1)S(1)} %collective-permute-done.28.rest_24_), channel_id=1, source_target_pairs={{0,1},{1,0},{2,3},{3,2},{4,5},{5,4},{6,7},{7,6},{8,9},{9,8},{10,11... | collective-permute-start | bytes 1228808 | tf_op jit(solution)/shard_map/ppermute | solution.py:414
  70.3 3.6 %collective-permute-start.25 = (bf16[1,80,2560]{2,1,0:T(8,128)(2,1)S(1)}, bf16[1,80,2560]{2,1,0:T(8,128)(2,1)S(1)}, u32[]{:S(2)}, u32[]{:S(2)}) collective-permute-start(bf16[1,80,2560]{2,1,0:T(8,128)(2,1)S(1)} %collective-permute-done.24.rest_20_), channel_id=1, source_target_pairs={{0,1},{1,0},{2,3},{3,2},{4,5},{5,4},{6,7},{7,6},{8,9},{9,8},{10,11... | collective-permute-start | bytes 1228808 | tf_op jit(solution)/shard_map/ppermute | solution.py:414
  71.2 3.5 %collective-permute-start.27 = (bf16[1,80,2560]{2,1,0:T(8,128)(2,1)S(1)}, bf16[1,80,2560]{2,1,0:T(8,128)(2,1)}, u32[]{:S(2)}, u32[]{:S(2)}) collective-permute-start(bf16[1,80,2560]{2,1,0:T(8,128)(2,1)S(1)} %collective-permute-done.26.rest_22_), channel_id=1, source_target_pairs={{0,1},{1,0},{2,3},{3,2},{4,5},{5,4},{6,7},{7,6},{8,9},{9,8},{10,11... | collective-permute-start | bytes 1228808 | tf_op jit(solution)/shard_map/ppermute | solution.py:414
  94.4 2.5 %collective-permute-start.30 = (bf16[4,128,640]{2,1,0:T(8,128)(2,1)}, bf16[4,128,640]{2,1,0:T(8,128)(2,1)}, u32[]{:S(2)}, u32[]{:S(2)}) collective-permute-start(bf16[4,128,640]{2,1,0:T(8,128)(2,1)} %get-tuple-element.64.rest_0_.dq_ref), channel_id=1, source_target_pairs={{0,1},{1,0},{2,3},{3,2},{4,5},{5,4},{6,7},{7,6},{8,9},{9,8},{10,11... | collective-permute-start | bytes 1966088 | tf_op jit(solution)/shard_map/ppermute | solution.py:414
  94.5 4.3 %collective-permute-start.31 = (bf16[4,128,640]{2,1,0:T(8,128)(2,1)}, bf16[4,128,640]{2,1,0:T(8,128)(2,1)}, u32[]{:S(2)}, u32[]{:S(2)}) collective-permute-start(bf16[4,128,640]{2,1,0:T(8,128)(2,1)} %get-tuple-element.65.rest_2_.dk_ref), channel_id=1, source_target_pairs={{0,1},{1,0},{2,3},{3,2},{4,5},{5,4},{6,7},{7,6},{8,9},{9,8},{10,11... | collective-permute-start | bytes 1966088 | tf_op jit(solution)/shard_map/ppermute | solution.py:414
  95.0 19.8 %copy-start.3 = (bf16[4,640,128]{2,1,0:T(8,128)(2,1)S(1)}, bf16[4,640,128]{2,1,0:T(8,128)(2,1)}, u32[]{:S(2)}) copy-start(bf16[4,640,128]{2,1,0:T(8,128)(2,1)} %get-tuple-element.71.attnt_a.attnt_ref) | copy-start | bytes 1966084
  95.0 5.7 %collective-permute-start.32 = (bf16[4,128,640]{2,1,0:T(8,128)(2,1)}, bf16[4,128,640]{2,1,0:T(8,128)(2,1)}, u32[]{:S(2)}, u32[]{:S(2)}) collective-permute-start(bf16[4,128,640]{2,1,0:T(8,128)(2,1)} %get-tuple-element.66.rest_4_.dv_ref), channel_id=1, source_target_pairs={{0,1},{1,0},{2,3},{3,2},{4,5},{5,4},{6,7},{7,6},{8,9},{9,8},{10,11... | collective-permute-start | bytes 1966088 | tf_op jit(solution)/shard_map/ppermute | solution.py:414
  95.1 19.8 %collective-permute-start.34 = (bf16[4,128,1280]{2,1,0:T(8,128)(2,1)S(1)}, bf16[4,128,1280]{2,1,0:T(8,128)(2,1)}, u32[]{:S(2)}, u32[]{:S(2)}) collective-permute-start(bf16[4,128,1280]{2,1,0:T(8,128)(2,1)S(1)} %copy-done.1), channel_id=1, source_target_pairs={{0,1},{1,0},{2,3},{3,2},{4,5},{5,4},{6,7},{7,6},{8,9},{9,8},{10,11... | collective-permute-start | bytes 3932168 | tf_op jit(solution)/shard_map/ppermute | solution.py:414
  112.0 36.7 %collective-permute-start.35 = (bf16[2,4,80,1024]{3,2,1,0:T(8,128)(2,1)}, bf16[2,4,80,1024]{3,2,1,0:T(8,128)(2,1)}, u32[]{:S(2)}, u32[]{:S(2)}) collective-permute-start(bf16[2,4,80,1024]{3,2,1,0:T(8,128)(2,1)} %get-tuple-element.67), channel_id=1, source_target_pairs={{0,16},{1,17},{2,18},{3,19},{4,20},{5,21},{6,22},{7,23},{8,24},{9,... | collective-permute-start | bytes 3932168 | tf_op jit(solution)/shard_map/ppermute | solution.py:414
  113.2 35.6 %collective-permute-start.36 = (bf16[2,4,80,896]{3,2,1,0:T(8,128)(2,1)}, bf16[2,4,80,896]{3,2,1,0:T(8,128)(2,1)}, u32[]{:S(2)}, u32[]{:S(2)}) collective-permute-start(bf16[2,4,80,896]{3,2,1,0:T(8,128)(2,1)} %get-tuple-element.75), channel_id=1, source_target_pairs={{0,8},{1,9},{2,10},{3,11},{4,12},{5,13},{6,14},{7,15},{8,0},{9,1},... | collective-permute-start | bytes 3440648 | tf_op jit(solution)/shard_map/ppermute | solution.py:414
  114.8 2.2 %collective-permute-start.33 = (bf16[4,640,128]{2,1,0:T(8,128)(2,1)S(1)}, bf16[4,640,128]{2,1,0:T(8,128)(2,1)}, u32[]{:S(2)}, u32[]{:S(2)}) collective-permute-start(bf16[4,640,128]{2,1,0:T(8,128)(2,1)S(1)} %copy-done.3), channel_id=1, source_target_pairs={{0,1},{1,0},{2,3},{3,2},{4,5},{5,4},{6,7},{7,6},{8,9},{9,8},{10,11... | collective-permute-start | bytes 1966088 | tf_op jit(solution)/shard_map/ppermute | solution.py:414
  123.9 71.2 %all-to-all-start = ((bf16[4,4,80,640]{3,2,1,0:T(8,128)(2,1)}), bf16[4,4,80,640]{3,2,1,0:T(8,128)(2,1)S(1)}, u32[]{:S(2)}, u32[]{:S(2)}) async-start(bf16[4,4,80,640]{3,2,1,0:T(8,128)(2,1)} %get-tuple-element.80), calls=%async_computation | async-start | bytes 3276800 | tf_op jit(solution)/shard_map/all_to_all | solution.py:475
  149.9 9.0 %collective-permute-start.44 = (bf16[4,80,384]{2,1,0:T(8,128)(2,1)S(1)}, bf16[4,80,384]{2,1,0:T(8,128)(2,1)S(1)}, u32[]{:S(2)}, u32[]{:S(2)}) collective-permute-start(bf16[4,80,384]{2,1,0:T(8,128)(2,1)S(1)} %fusion.4), channel_id=1, source_target_pairs={{0,16},{1,17},{2,18},{3,19},{4,20},{5,21},{6,22},{7,23},{8,24},{9,... | collective-permute-start | bytes 737288 | tf_op jit(solution)/shard_map/ppermute | solution.py:414
  151.1 13.3 %collective-permute-start.38 = (bf16[4,80,512]{2,1,0:T(8,128)(2,1)S(1)}, bf16[4,80,512]{2,1,0:T(8,128)(2,1)S(1)}, u32[]{:S(2)}, u32[]{:S(2)}) collective-permute-start(bf16[4,80,512]{2,1,0:T(8,128)(2,1)S(1)} %fusion.2), channel_id=1, source_target_pairs={{0,16},{1,17},{2,18},{3,19},{4,20},{5,21},{6,22},{7,23},{8,24},{9,... | collective-permute-start | bytes 983048 | tf_op jit(solution)/shard_map/ppermute | solution.py:414
  154.4 11.0 %collective-permute-start.37 = (bf16[4,80,512]{2,1,0:T(8,128)(2,1)S(1)}, bf16[4,80,512]{2,1,0:T(8,128)(2,1)S(1)}, u32[]{:S(2)}, u32[]{:S(2)}) collective-permute-start(bf16[4,80,512]{2,1,0:T(8,128)(2,1)S(1)} %get-tuple-element.89), channel_id=1, source_target_pairs={{0,8},{1,9},{2,10},{3,11},{4,12},{5,13},{6,14},{7,15},{8,0},{9,1},... | collective-permute-start | bytes 983048 | tf_op jit(solution)/shard_map/ppermute | solution.py:414
  154.5 15.6 %collective-permute-start.43 = (bf16[4,80,512]{2,1,0:T(8,128)(2,1)S(1)}, bf16[4,80,512]{2,1,0:T(8,128)(2,1)S(1)}, u32[]{:S(2)}, u32[]{:S(2)}) collective-permute-start(bf16[4,80,512]{2,1,0:T(8,128)(2,1)S(1)} %get-tuple-element.88), channel_id=1, source_target_pairs={{0,8},{1,9},{2,10},{3,11},{4,12},{5,13},{6,14},{7,15},{8,0},{9,1},... | collective-permute-start | bytes 983048 | tf_op jit(solution)/shard_map/ppermute | solution.py:414
  171.6 11.6 %collective-permute-start.39 = (bf16[80,1024]{1,0:T(8,128)(2,1)S(1)}, bf16[80,1024]{1,0:T(8,128)(2,1)S(1)}, u32[]{:S(2)}, u32[]{:S(2)}) collective-permute-start(bf16[80,1024]{1,0:T(8,128)(2,1)S(1)} %get-tuple-element.95), channel_id=1, source_target_pairs={{0,2},{1,3},{2,4},{3,5},{4,6},{5,7},{6,0},{7,1},{8,10},{9,11},{10,... | collective-permute-start | bytes 491528 | tf_op jit(solution)/shard_map/ppermute | solution.py:414
  173.2 20.6 %collective-permute-start.40 = (bf16[80,1024]{1,0:T(8,128)(2,1)S(1)}, bf16[80,1024]{1,0:T(8,128)(2,1)S(1)}, u32[]{:S(2)}, u32[]{:S(2)}) collective-permute-start(bf16[80,1024]{1,0:T(8,128)(2,1)S(1)} %get-tuple-element.97), channel_id=1, source_target_pairs={{0,4},{1,5},{2,6},{3,7},{4,0},{5,1},{6,2},{7,3},{8,12},{9,13},{10,... | collective-permute-start | bytes 491528 | tf_op jit(solution)/shard_map/ppermute | solution.py:414
  174.2 19.6 %collective-permute-start.41 = (bf16[80,1024]{1,0:T(8,128)(2,1)S(1)}, bf16[80,1024]{1,0:T(8,128)(2,1)S(1)}, u32[]{:S(2)}, u32[]{:S(2)}) collective-permute-start(bf16[80,1024]{1,0:T(8,128)(2,1)S(1)} %get-tuple-element.96), channel_id=1, source_target_pairs={{0,6},{1,7},{2,0},{3,1},{4,2},{5,3},{6,4},{7,5},{8,14},{9,15},{10,... | collective-permute-start | bytes 491528 | tf_op jit(solution)/shard_map/ppermute | solution.py:414
  177.0 30.9 %collective-permute-start.47 = (bf16[80,896]{1,0:T(8,128)(2,1)}, bf16[80,896]{1,0:T(8,128)(2,1)}, u32[]{:S(2)}, u32[]{:S(2)}) collective-permute-start(bf16[80,896]{1,0:T(8,128)(2,1)} %get-tuple-element.100), channel_id=1, source_target_pairs={{0,2},{1,3},{2,4},{3,5},{4,6},{5,7},{6,0},{7,1},{8,10},{9,11},{10,... | collective-permute-start | bytes 430088 | tf_op jit(solution)/shard_map/ppermute | solution.py:414
  177.2 30.7 %collective-permute-start.48 = (bf16[80,896]{1,0:T(8,128)(2,1)}, bf16[80,896]{1,0:T(8,128)(2,1)}, u32[]{:S(2)}, u32[]{:S(2)}) collective-permute-start(bf16[80,896]{1,0:T(8,128)(2,1)} %get-tuple-element.102), channel_id=1, source_target_pairs={{0,4},{1,5},{2,6},{3,7},{4,0},{5,1},{6,2},{7,3},{8,12},{9,13},{10,... | collective-permute-start | bytes 430088 | tf_op jit(solution)/shard_map/ppermute | solution.py:414
  183.3 24.6 %collective-permute-start.49 = (bf16[80,896]{1,0:T(8,128)(2,1)}, bf16[80,896]{1,0:T(8,128)(2,1)}, u32[]{:S(2)}, u32[]{:S(2)}) collective-permute-start(bf16[80,896]{1,0:T(8,128)(2,1)} %get-tuple-element.101), channel_id=1, source_target_pairs={{0,6},{1,7},{2,0},{3,1},{4,2},{5,3},{6,4},{7,5},{8,14},{9,15},{10,... | collective-permute-start | bytes 430088 | tf_op jit(solution)/shard_map/ppermute | solution.py:414
  194.6 6.7 %collective-permute-start.42 = (bf16[80,1024]{1,0:T(8,128)(2,1)}, bf16[80,1024]{1,0:T(8,128)(2,1)}, u32[]{:S(2)}, u32[]{:S(2)}) collective-permute-start(bf16[80,1024]{1,0:T(8,128)(2,1)} %get-tuple-element.83), channel_id=1, source_target_pairs={{0,8},{1,9},{2,10},{3,11},{4,12},{5,13},{6,14},{7,15},{8,0},{9,1},... | collective-permute-start | bytes 491528 | tf_op jit(solution)/shard_map/ppermute | solution.py:414
  196.4 6.5 %collective-permute-start.46 = (bf16[2,80,256]{2,1,0:T(8,128)(2,1)S(1)}, bf16[2,80,256]{2,1,0:T(8,128)(2,1)S(1)}, u32[]{:S(2)}, u32[]{:S(2)}) collective-permute-start(bf16[2,80,256]{2,1,0:T(8,128)(2,1)S(1)} %pad_maximum_fusion.4), channel_id=1, source_target_pairs={{0,8},{1,9},{2,10},{3,11},{4,12},{5,13},{6,14},{7,15},{8,0},{9,1},... | collective-permute-start | bytes 245768 | tf_op jit(solution)/shard_map/ppermute | solution.py:414
  202.3 4.9 %collective-permute-start.45 = (bf16[2,80,384]{2,1,0:T(8,128)(2,1)S(1)}, bf16[2,80,384]{2,1,0:T(8,128)(2,1)S(1)}, u32[]{:S(2)}, u32[]{:S(2)}) collective-permute-start(bf16[2,80,384]{2,1,0:T(8,128)(2,1)S(1)} %slice.194), channel_id=1, source_target_pairs={{0,16},{1,17},{2,18},{3,19},{4,20},{5,21},{6,22},{7,23},{8,24},{9,... | collective-permute-start | bytes 368648 | tf_op jit(solution)/shard_map/ppermute | solution.py:414
  202.9 6.1 %collective-permute-start.51 = (bf16[80,256]{1,0:T(8,128)(2,1)S(1)}, bf16[80,256]{1,0:T(8,128)(2,1)S(1)}, u32[]{:S(2)}, u32[]{:S(2)}) collective-permute-start(bf16[80,256]{1,0:T(8,128)(2,1)S(1)} %fusion.18), channel_id=1, source_target_pairs={{0,16},{1,17},{2,18},{3,19},{4,20},{5,21},{6,22},{7,23},{8,24},{9,... | collective-permute-start | bytes 122888 | tf_op jit(solution)/shard_map/ppermute | solution.py:414
  207.3 4.9 %collective-permute-start.50 = (bf16[80,384]{1,0:T(8,128)(2,1)S(1)}, bf16[80,384]{1,0:T(8,128)(2,1)S(1)}, u32[]{:S(2)}, u32[]{:S(2)}) collective-permute-start(bf16[80,384]{1,0:T(8,128)(2,1)S(1)} %fusion.17), channel_id=1, source_target_pairs={{0,8},{1,9},{2,10},{3,11},{4,12},{5,13},{6,14},{7,15},{8,0},{9,1},... | collective-permute-start | bytes 184328 | tf_op jit(solution)/shard_map/ppermute | solution.py:414
  212.3 6.3 %collective-permute-start.52 = (bf16[80,1536]{1,0:T(8,128)(2,1)S(1)}, bf16[80,1536]{1,0:T(8,128)(2,1)S(1)}, u32[]{:S(2)}, u32[]{:S(2)}) collective-permute-start(bf16[80,1536]{1,0:T(8,128)(2,1)S(1)} %fusion.6), channel_id=1, source_target_pairs={{0,8},{1,9},{2,10},{3,11},{4,12},{5,13},{6,14},{7,15},{8,0},{9,1},... | collective-permute-start | bytes 737288 | tf_op jit(solution)/shard_map/ppermute | solution.py:414
  (19 other events, 47.7 us)

commit v4 on v2

--- a/solution.py
+++ b/solution.py
@@ -588,8 +588,8 @@
         far_x_other = sibling(far_x, far_other)
         far_y_other = sibling(far_y, far_other)
         back_other = sibling(back, far_other)
-        far_across = send(tied(far_x, back_x, back_y), route["y"])
-        back_across = send(tied(diagonal, near_across), route["z"][3])
+        far_across = send(tied(far_x, back), route["y"])
+        back_across = send(tied(diagonal, back), route["z"][3])
         weights = [quarters, quarters_other, near, near_other, near_x, near_x_other, near_y, near_y_other]
         weights += [near_across, sibling(near_across), far, far_other, far_x, far_x_other, far_y, far_y_other]
         weights += [far_across, sibling(far_across), back, back_other, back_x, sibling(back_x)]

time: 214 us -> 214 us (level)
  waiting for transfers between devices: 65.2 us -> 72.7 us
  starting transfers between devices: 62.6 us -> 55.2 us
    ppermute x56, starting transfers between devices: 62.6 us -> 55.2 us  [send(): return lax.ppermute(value, AXES, route)]
    ppermute x56, waiting for transfers between devices: 65.2 us -> 72.7 us  [send(): return lax.ppermute(value, AXES, route)]
  transfers between devices with their start and end apart: 56 -> 56, of which waited for: 25 -> 30; matrix products, arithmetic and copies ran while one was open for 7% -> 7% of each run, Pallas kernels for 29% -> 28%
where the time goes in v4:
time: 214 us
  waiting for transfers between devices  72.7 us (34%)
  Pallas kernels  60.7 us (28%)
  starting transfers between devices  55.2 us (26%)
  other arithmetic  16.7 us (8%)
  local copies, waits for them, and re-layouts  7.3 us (3%)
    ppermute x56, waiting for transfers between devices, send(): return lax.ppermute(value, AXES, route)  72.7 us
    ppermute x56, starting transfers between devices, send(): return lax.ppermute(value, AXES, route)  55.2 us
    pallas_call x1, Pallas kernels, shards(): pl.pallas_call(functools.partial(layer_kernel, routed, n_weights), out_sh...  19.4 us
    pallas_call x1, Pallas kernels, results(): pl.pallas_call(functools.partial(result_kernel, routed, n_weights), out_s...  16.1 us
    pallas_call x1, Pallas kernels, qkv_terms(): pl.pallas_call(qkv_terms_kernel, out_shape=[jax.ShapeDtypeStruct((2, 4, r...  11.3 us
    pallas_call x1, Pallas kernels, out_terms(): pl.pallas_call(out_terms_kernel, out_shape=[jax.ShapeDtypeStruct((4, rows...  5.78 us
    pallas_call x1, Pallas kernels, normed(): pl.pallas_call(norm_kernel, out_shape=[jax.ShapeDtypeStruct(blocks.shape,...  4.31 us
  transfers between devices with their start and end apart: 56, of which 30 were waited for; matrix products, arithmetic and copies ran while one was open for 7% of the time, Pallas kernels for 28%

profile of v4, /device:TPU:8, one launch (start us, length us, event | category | flops | bytes accessed | tf_op | source)
XLA Modules:
  0.0 213.9 jit_solution(2663864068136669511)
XLA Ops:
  0.7 1.0 constant_dynamic-slice_fusion.2
  2.7 1.6 collective-permute-start.4
  5.7 1.6 collective-permute-start.1
  7.3 1.2 collective-permute-start.2
  9.6 4.5 %collective-permute-done.1 = f32[2,320]{1,0:T(2,128)S(1)} collective-permute-done((f32[2,320]{1,0:T(2,128)S(1)}, f32[2,320]{1,0:T(2,128)S(1)}, u32[]{:S(2)}, u32[]{:S(2)}) %collective-permute-start.1) | collective-permute-done | bytes 2592 | tf_op jit(solution)/shard_map/ppermute | solution.py:418
  16.1 1.6 pad_maximum_fusion.rest_0_
  18.6 1.5 collective-permute-start.7
  20.1 1.5 collective-permute-start.8
  21.7 4.3 %norm.1 = (bf16[4,128,1280]{2,1,0:T(8,128)(2,1)}, bf16[4,1280,128]{2,1,0:T(8,128)(2,1)}) custom-call(s32[4]{0:T(128)} %kind_ref.5, bf16[4,128,1280]{2,1,0:T(8,128)(2,1)} %x_ref.2, f32[2,1280]{1,0:T(2,128)} %reshape.101.gain_ref), custom_call_target="tpu_custom_call" | custom-call | flops 11500000 | tf_op jit(solution)/shard_map/norm/pallas_call | solution.py:542
  26.0 3.8 %collective-permute-done.6.rest_10_ = bf16[1,80,2560]{2,1,0:T(8,128)(2,1)} collective-permute-done((bf16[1,80,2560]{2,1,0:T(8,128)(2,1)S(1)}, bf16[1,80,2560]{2,1,0:T(8,128)(2,1)}, u32[]{:S(2)}, u32[]{:S(2)}) %collective-permute-start.6) | collective-permute-done | bytes 409632 | tf_op jit(solution)/shard_map/ppermute | solution.py:418
  30.2 1.3 collective-permute-done.8.rest_6_
  32.9 1.5 collective-permute-start.14
  34.5 2.9 %collective-permute-start.12 = (bf16[1,80,2560]{2,1,0:T(8,128)(2,1)}, bf16[1,80,2560]{2,1,0:T(8,128)(2,1)}, u32[]{:S(2)}, u32[]{:S(2)}) collective-permute-start(bf16[1,80,2560]{2,1,0:T(8,128)(2,1)} %copy-done.30), channel_id=1, source_target_pairs={{0,6},{1,7},{2,0},{3,1},{4,2},{5,3},{6,4},{7,5},{8,14},{9,15},{10,... | collective-permute-start | bytes 1228808 | tf_op jit(solution)/shard_map/ppermute | solution.py:418
  38.8 3.8 %left_factor.1.left = bf16[2,2,640,512]{3,2,1,0:T(8,128)(2,1)} custom-call(s32[3]{0:T(128)} %pad_add_fusion.where_ref, s32[8]{0:T(128)} %pad_add_fusion.1.kind_ref, bf16[4,1280,128]{2,1,0:T(8,128)(2,1)} %get-tuple-element.56.ht_a, bf16[4,1280,128]{2,1,0:T(8,128)(2,1)} %collective-permute-done.15.ht_b), custom_call_target="tpu_custom_call" | custom-call | flops 11500000 | tf_op jit(solution)/shard_map/left_factor/pallas_call | solution.py:343
  42.6 3.4 %collective-permute-done.12.rest_18_ = bf16[1,80,2560]{2,1,0:T(8,128)(2,1)} collective-permute-done((bf16[1,80,2560]{2,1,0:T(8,128)(2,1)}, bf16[1,80,2560]{2,1,0:T(8,128)(2,1)}, u32[]{:S(2)}, u32[]{:S(2)}) %collective-permute-start.12) | collective-permute-done | bytes 409632 | tf_op jit(solution)/shard_map/ppermute | solution.py:418
  46.0 1.0 fusion.7
  48.1 1.5 collective-permute-start.16
  49.6 1.0 collective-permute-start.28
  51.2 1.5 collective-permute-start.26
  52.7 7.5 %collective-permute-done.21.rest_16_ = bf16[1,80,2560]{2,1,0:T(8,128)(2,1)S(1)} collective-permute-done((bf16[1,80,2560]{2,1,0:T(8,128)(2,1)}, bf16[1,80,2560]{2,1,0:T(8,128)(2,1)S(1)}, u32[]{:S(2)}, u32[]{:S(2)}) %collective-permute-start.21) | collective-permute-done | bytes 409632 | tf_op jit(solution)/shard_map/ppermute | solution.py:418
  60.9 10.0 %collective-permute-done.28.rest_24_ = bf16[1,80,2560]{2,1,0:T(8,128)(2,1)S(1)} collective-permute-done((bf16[1,80,2560]{2,1,0:T(8,128)(2,1)S(1)}, bf16[1,80,2560]{2,1,0:T(8,128)(2,1)S(1)}, u32[]{:S(2)}, u32[]{:S(2)}) %collective-permute-start.28) | collective-permute-done | bytes 409632 | tf_op jit(solution)/shard_map/ppermute | solution.py:418
  73.0 1.0 collective-permute-done.19.rest_13_
  74.4 1.2 collective-permute-done.25.rest_21_
  76.4 19.4 %layer.1 = (bf16[4,640,128]{2,1,0:T(8,128)(2,1)}, bf16[4,128,640]{2,1,0:T(8,128)(2,1)}, bf16[4,128,640]{2,1,0:T(8,128)(2,1)}, bf16[4,128,640]{2,1,0:T(8,128)(2,1)}) custom-call(s32[3]{0:T(128)} %pad_add_fusion.where_ref, s32[4]{0:T(128)} %kind_ref.5, bf16[4,128,1280]{2,1,0:T(8,128)(2,1)} %get-tuple-element.48.h_ref, bf16[4,128,1280]{2,1,0:T(8,128)(2,1)} %cot_ref.3, ...), custom_call_target="tpu_custom_call" | custom-call | flops 11500000 | tf_op jit(solution)/shard_map/layer/pallas_call | solution.py:608
  96.9 1.3 collective-permute-done.30.rest_1_
  98.2 1.9 collective-permute-done.31.rest_3_
  100.1 0.9 collective-permute-done.32.rest_5_
  101.9 11.3 %qkv_terms.1 = (bf16[2,4,80,1024]{3,2,1,0:T(8,128)(2,1)}, bf16[2,4,80,896]{3,2,1,0:T(8,128)(2,1)}, f32[4,80,1920]{2,1,0:T(8,128)}, f32[4,80,1024]{2,1,0:T(8,128)}, f32[4,80,896]{2,1,0:T(8,128)}) custom-call(bf16[2,2,640,512]{3,2,1,0:T(8,128)(2,1)} %left_factor.1.left, bf16[4,128,640]{2,1,0:T(8,128)(2,1)} %get-tuple-element.65.rest_0_.dq_ref, ...), custom_call_target="tpu_custom_call" | custom-call | flops 11500000 | tf_op jit(solution)/shard_map/qkv_terms/pallas_call | solution.py:376
  113.2 1.5 collective-permute-start.36
  114.7 1.2 collective-permute-start.37
  115.9 5.8 %out_terms.1 = (f32[4,80,640]{2,1,0:T(8,128)}, f32[4,80,640]{2,1,0:T(8,128)}, bf16[2,4,80,640]{3,2,1,0:T(8,128)(2,1)}) custom-call(s32[3]{0:T(128)} %pad_add_fusion.where_ref, s32[8]{0:T(128)} %pad_add_fusion.1.kind_ref, bf16[4,640,128]{2,1,0:T(8,128)(2,1)} %get-tuple-element.72.attnt_a.attnt_ref, bf16[4,640,128]{2,1,0:T(8,128)(2,1)} %collective-permute-done.33.attnt_b, ...), custom_call_target="tpu_custom_call" | custom-call | flops 11500000 | tf_op jit(solution)/shard_map/out_terms/pallas_call | solution.py:357
  122.6 16.1 %result.1 = (bf16[4,128,1280]{2,1,0:T(8,128)(2,1)}, bf16[4,128,1280]{2,1,0:T(8,128)(2,1)}) custom-call(s32[3]{0:T(128)} %pad_add_fusion.where_ref, s32[4]{0:T(128)} %kind_ref.5, s32[4]{0:T(128)} %rank_ref.1, bf16[4,128,1280]{2,1,0:T(8,128)(2,1)} %x_ref.2, bf16[4,128,1280]{2,1,0:T(8,128)(2,1)} %cot_ref.3, f32[2,1280]{1,0:T(2,128)} %reshape.101.gain_ref, ...), custom_call_target="tpu_custom_call" | custom-call | flops 11500000 | tf_op jit(solution)/shard_map/result/pallas_call | solution.py:622
  138.9 2.7 %collective-permute-done.35 = bf16[2,4,80,640]{3,2,1,0:T(8,128)(2,1)} collective-permute-done((bf16[2,4,80,640]{3,2,1,0:T(8,128)(2,1)}, bf16[2,4,80,640]{3,2,1,0:T(8,128)(2,1)}, u32[]{:S(2)}, u32[]{:S(2)}) %collective-permute-start.35) | collective-permute-done | bytes 819232 | tf_op jit(solution)/shard_map/ppermute | solution.py:418
  142.1 2.4 %collective-permute-done.36 = bf16[2,4,80,1024]{3,2,1,0:T(8,128)(2,1)} collective-permute-done((bf16[2,4,80,1024]{3,2,1,0:T(8,128)(2,1)}, bf16[2,4,80,1024]{3,2,1,0:T(8,128)(2,1)}, u32[]{:S(2)}, u32[]{:S(2)}) %collective-permute-start.36) | collective-permute-done | bytes 1310752 | tf_op jit(solution)/shard_map/ppermute | solution.py:418
  144.5 1.5 fusion.5
  146.0 1.1 collective-permute-start.38
  147.2 1.0 collective-permute-start.44
  148.1 1.0 fusion.6
  149.1 1.4 collective-permute-start.45
  150.6 1.1 fusion.1
  151.7 1.1 fusion.4
  152.8 2.3 %collective-permute-start.50 = (bf16[4,80,640]{2,1,0:T(8,128)(2,1)S(1)}, bf16[4,80,640]{2,1,0:T(8,128)(2,1)S(1)}, u32[]{:S(2)}, u32[]{:S(2)}) collective-permute-start(bf16[4,80,640]{2,1,0:T(8,128)(2,1)S(1)} %fusion.1), channel_id=1, source_target_pairs={{0,4},{1,5},{2,6},{3,7},{4,0},{5,1},{6,2},{7,3},{8,12},{9,13},{10,... | collective-permute-start | bytes 1228808 | tf_op jit(solution)/shard_map/ppermute | solution.py:418
  156.1 1.0 convert_add_fusion.9
  157.1 5.1 %collective-permute-done.44 = bf16[4,80,512]{2,1,0:T(8,128)(2,1)S(1)} collective-permute-done((bf16[4,80,512]{2,1,0:T(8,128)(2,1)S(1)}, bf16[4,80,512]{2,1,0:T(8,128)(2,1)S(1)}, u32[]{:S(2)}, u32[]{:S(2)}) %collective-permute-start.44) | collective-permute-done | bytes 327712 | tf_op jit(solution)/shard_map/ppermute | solution.py:418
  162.3 1.3 convert_add_fusion.7
  163.8 1.6 collective-permute-start.46
  165.4 2.3 %collective-permute-start.47 = (bf16[80,896]{1,0:T(8,128)(2,1)S(1)}, bf16[80,896]{1,0:T(8,128)(2,1)S(1)}, u32[]{:S(2)}, u32[]{:S(2)}) collective-permute-start(bf16[80,896]{1,0:T(8,128)(2,1)S(1)} %get-tuple-element.104), channel_id=1, source_target_pairs={{0,4},{1,5},{2,6},{3,7},{4,0},{5,1},{6,2},{7,3},{8,12},{9,13},{10,... | collective-permute-start | bytes 430088 | tf_op jit(solution)/shard_map/ppermute | solution.py:418
  167.9 1.1 convert_add_fusion.5
  169.3 1.8 collective-permute-start.40
  171.1 7.0 %collective-permute-done.50 = bf16[4,80,640]{2,1,0:T(8,128)(2,1)S(1)} collective-permute-done((bf16[4,80,640]{2,1,0:T(8,128)(2,1)S(1)}, bf16[4,80,640]{2,1,0:T(8,128)(2,1)S(1)}, u32[]{:S(2)}, u32[]{:S(2)}) %collective-permute-start.50) | collective-permute-done | bytes 409632 | tf_op jit(solution)/shard_map/ppermute | solution.py:418
  178.1 3.4 %collective-permute-start.41 = (bf16[80,1024]{1,0:T(8,128)(2,1)S(1)}, bf16[80,1024]{1,0:T(8,128)(2,1)S(1)}, u32[]{:S(2)}, u32[]{:S(2)}) collective-permute-start(bf16[80,1024]{1,0:T(8,128)(2,1)S(1)} %get-tuple-element.97), channel_id=1, source_target_pairs={{0,4},{1,5},{2,6},{3,7},{4,0},{5,1},{6,2},{7,3},{8,12},{9,13},{10,... | collective-permute-start | bytes 491528 | tf_op jit(solution)/shard_map/ppermute | solution.py:418
  181.5 1.1 fusion.2
  182.6 5.8 %collective-permute-start.42 = (bf16[80,1024]{1,0:T(8,128)(2,1)S(1)}, bf16[80,1024]{1,0:T(8,128)(2,1)S(1)}, u32[]{:S(2)}, u32[]{:S(2)}) collective-permute-start(bf16[80,1024]{1,0:T(8,128)(2,1)S(1)} %get-tuple-element.96), channel_id=1, source_target_pairs={{0,6},{1,7},{2,0},{3,1},{4,2},{5,3},{6,4},{7,5},{8,14},{9,15},{10,... | collective-permute-start | bytes 491528 | tf_op jit(solution)/shard_map/ppermute | solution.py:418
  188.4 3.5 %collective-permute-done.48 = bf16[80,896]{1,0:T(8,128)(2,1)S(1)} collective-permute-done((bf16[80,896]{1,0:T(8,128)(2,1)S(1)}, bf16[80,896]{1,0:T(8,128)(2,1)S(1)}, u32[]{:S(2)}, u32[]{:S(2)}) %collective-permute-start.48) | collective-permute-done | bytes 143392 | tf_op jit(solution)/shard_map/ppermute | solution.py:418
  192.9 1.2 collective-permute-start.53
  194.7 1.8 collective-permute-start.49
  196.4 1.3 collective-permute-done.41
  197.7 1.2 collective-permute-done.42
  200.5 1.4 collective-permute-start.52
  201.9 1.9 collective-permute-done.54
  204.0 1.8 collective-permute-done.43
  205.9 1.2 copy-done.2
  207.1 1.2 fusion
  209.5 3.5 %collective-permute-done.55 = bf16[80,640]{1,0:T(8,128)(2,1)S(1)} collective-permute-done((bf16[80,640]{1,0:T(8,128)(2,1)S(1)}, bf16[80,640]{1,0:T(8,128)(2,1)S(1)}, u32[]{:S(2)}, u32[]{:S(2)}) %collective-permute-start.55) | collective-permute-done | bytes 102432 | tf_op jit(solution)/shard_map/ppermute | solution.py:418
  (196 shorter events, 25.9 us)
Async XLA Ops:
  2.7 13.4 %collective-permute-start.4 = (bf16[1,80,2560]{2,1,0:T(8,128)(2,1)S(1)}, bf16[1,80,2560]{2,1,0:T(8,128)(2,1)S(1)}, u32[]{:S(2)}, u32[]{:S(2)}) collective-permute-start(bf16[1,80,2560]{2,1,0:T(8,128)(2,1)S(1)} %pad_maximum_fusion.1), channel_id=1, source_target_pairs={{0,2},{1,3},{2,4},{3,5},{4,6},{5,7},{6,0},{7,1},{8,10},{9,11},{10,... | collective-permute-start | bytes 1228808 | tf_op jit(solution)/shard_map/ppermute | solution.py:418
  4.5 1.2 collective-permute-start
  5.7 8.4 %collective-permute-start.1 = (f32[2,320]{1,0:T(2,128)S(1)}, f32[2,320]{1,0:T(2,128)S(1)}, u32[]{:S(2)}, u32[]{:S(2)}) collective-permute-start(f32[2,320]{1,0:T(2,128)S(1)} %pad_maximum_fusion.4), channel_id=1, source_target_pairs={{0,2},{1,3},{2,4},{3,5},{4,6},{5,7},{6,0},{7,1},{8,10},{9,11},{10,... | collective-permute-start | bytes 7688 | tf_op jit(solution)/shard_map/ppermute | solution.py:418
  7.3 7.8 %collective-permute-start.2 = (f32[2,320]{1,0:T(2,128)S(1)}, f32[2,320]{1,0:T(2,128)S(1)}, u32[]{:S(2)}, u32[]{:S(2)}) collective-permute-start(f32[2,320]{1,0:T(2,128)S(1)} %pad_maximum_fusion.4), channel_id=1, source_target_pairs={{0,4},{1,5},{2,6},{3,7},{4,0},{5,1},{6,2},{7,3},{8,12},{9,13},{10,... | collective-permute-start | bytes 7688 | tf_op jit(solution)/shard_map/ppermute | solution.py:418
  8.5 6.6 %collective-permute-start.3 = (f32[2,320]{1,0:T(2,128)S(1)}, f32[2,320]{1,0:T(2,128)S(1)}, u32[]{:S(2)}, u32[]{:S(2)}) collective-permute-start(f32[2,320]{1,0:T(2,128)S(1)} %pad_maximum_fusion.4), channel_id=1, source_target_pairs={{0,6},{1,7},{2,0},{3,1},{4,2},{5,3},{6,4},{7,5},{8,14},{9,15},{10,... | collective-permute-start | bytes 7688 | tf_op jit(solution)/shard_map/ppermute | solution.py:418
  16.1 15.4 %copy-start.4 = (bf16[1,80,2560]{2,1,0:T(8,128)(2,1)}, bf16[1,80,2560]{2,1,0:T(8,128)(2,1)S(1)}, u32[]{:S(2)}) copy-start(bf16[1,80,2560]{2,1,0:T(8,128)(2,1)S(1)} %collective-permute-done.4.rest_2_) | copy-start | bytes 1228804
  17.7 24.9 %copy-start = (bf16[4,80,2560]{2,1,0:T(8,128)(2,1)}, bf16[4,80,2560]{2,1,0:T(8,128)(2,1)S(1)}, u32[]{:S(2)}) copy-start(bf16[4,80,2560]{2,1,0:T(8,128)(2,1)S(1)} %pad_maximum_fusion.rest_0_) | copy-start | bytes 4915204
  17.7 20.4 %copy-start.32 = (s32[4]{0:T(128)S(1)}, s32[4]{0:T(128)}, u32[]{:S(2)}) copy-start(s32[4]{0:T(128)} %kind_ref.5) | copy-start | bytes 52
  17.7 13.8 %collective-permute-start.5 = (bf16[4,80,2560]{2,1,0:T(8,128)(2,1)S(1)}, bf16[4,80,2560]{2,1,0:T(8,128)(2,1)}, u32[]{:S(2)}, u32[]{:S(2)}) collective-permute-start(bf16[4,80,2560]{2,1,0:T(8,128)(2,1)S(1)} %pad_maximum_fusion.rest_0_), channel_id=1, source_target_pairs={{0,1},{1,0},{2,3},{3,2},{4,5},{5,4},{6,7},{7,6},{8,9},{9,8},{10,11... | collective-permute-start | bytes 4915208 | tf_op jit(solution)/shard_map/ppermute | solution.py:418
  17.8 12.0 %collective-permute-start.6 = (bf16[1,80,2560]{2,1,0:T(8,128)(2,1)S(1)}, bf16[1,80,2560]{2,1,0:T(8,128)(2,1)}, u32[]{:S(2)}, u32[]{:S(2)}) collective-permute-start(bf16[1,80,2560]{2,1,0:T(8,128)(2,1)S(1)} %collective-permute-done.4.rest_2_), channel_id=1, source_target_pairs={{0,2},{1,3},{2,4},{3,5},{4,6},{5,7},{6,0},{7,1},{8,10},{9,11},{10,... | collective-permute-start | bytes 1228808 | tf_op jit(solution)/shard_map/ppermute | solution.py:418
  18.6 11.5 %collective-permute-start.7 = (bf16[1,80,2560]{2,1,0:T(8,128)(2,1)S(1)}, bf16[1,80,2560]{2,1,0:T(8,128)(2,1)S(1)}, u32[]{:S(2)}, u32[]{:S(2)}) collective-permute-start(bf16[1,80,2560]{2,1,0:T(8,128)(2,1)S(1)} %collective-permute-done.4.rest_2_), channel_id=1, source_target_pairs={{0,8},{1,9},{2,10},{3,11},{4,12},{5,13},{6,14},{7,15},{8,0},{9,1},... | collective-permute-start | bytes 1228808 | tf_op jit(solution)/shard_map/ppermute | solution.py:418
  20.1 11.4 %collective-permute-start.8 = (bf16[1,80,2560]{2,1,0:T(8,128)(2,1)S(1)}, bf16[1,80,2560]{2,1,0:T(8,128)(2,1)}, u32[]{:S(2)}, u32[]{:S(2)}) collective-permute-start(bf16[1,80,2560]{2,1,0:T(8,128)(2,1)S(1)} %collective-permute-done.4.rest_2_), channel_id=1, source_target_pairs={{0,16},{1,17},{2,18},{3,19},{4,20},{5,21},{6,22},{7,23},{8,24},{9,... | collective-permute-start | bytes 1228808 | tf_op jit(solution)/shard_map/ppermute | solution.py:418
  31.5 7.2 %collective-permute-start.15 = (bf16[4,1280,128]{2,1,0:T(8,128)(2,1)}, bf16[4,1280,128]{2,1,0:T(8,128)(2,1)}, u32[]{:S(2)}, u32[]{:S(2)}) collective-permute-start(bf16[4,1280,128]{2,1,0:T(8,128)(2,1)} %get-tuple-element.56.ht_a), channel_id=1, source_target_pairs={{0,1},{1,0},{2,3},{3,2},{4,5},{5,4},{6,7},{7,6},{8,9},{9,8},{10,11... | collective-permute-start | bytes 3932168 | tf_op jit(solution)/shard_map/ppermute | solution.py:418
  31.5 6.5 %collective-permute-start.9 = (bf16[1,80,2560]{2,1,0:T(8,128)(2,1)S(1)}, bf16[1,80,2560]{2,1,0:T(8,128)(2,1)S(1)}, u32[]{:S(2)}, u32[]{:S(2)}) collective-permute-start(bf16[1,80,2560]{2,1,0:T(8,128)(2,1)S(1)} %collective-permute-done.4.rest_2_), channel_id=1, source_target_pairs={{0,1},{1,0},{2,3},{3,2},{4,5},{5,4},{6,7},{7,6},{8,9},{9,8},{10,11... | collective-permute-start | bytes 1228808 | tf_op jit(solution)/shard_map/ppermute | solution.py:418
  32.0 14.0 %collective-permute-start.13 = (bf16[1,80,2560]{2,1,0:T(8,128)(2,1)}, bf16[1,80,2560]{2,1,0:T(8,128)(2,1)}, u32[]{:S(2)}, u32[]{:S(2)}) collective-permute-start(bf16[1,80,2560]{2,1,0:T(8,128)(2,1)} %collective-permute-done.6.rest_10_), channel_id=1, source_target_pairs={{0,8},{1,9},{2,10},{3,11},{4,12},{5,13},{6,14},{7,15},{8,0},{9,1},... | collective-permute-start | bytes 1228808 | tf_op jit(solution)/shard_map/ppermute | solution.py:418
  32.9 13.1 %collective-permute-start.14 = (bf16[1,80,2560]{2,1,0:T(8,128)(2,1)}, bf16[1,80,2560]{2,1,0:T(8,128)(2,1)}, u32[]{:S(2)}, u32[]{:S(2)}) collective-permute-start(bf16[1,80,2560]{2,1,0:T(8,128)(2,1)} %collective-permute-done.6.rest_10_), channel_id=1, source_target_pairs={{0,16},{1,17},{2,18},{3,19},{4,20},{5,21},{6,22},{7,23},{8,24},{9,... | collective-permute-start | bytes 1228808 | tf_op jit(solution)/shard_map/ppermute | solution.py:418
  34.5 11.6 %collective-permute-start.12 = (bf16[1,80,2560]{2,1,0:T(8,128)(2,1)}, bf16[1,80,2560]{2,1,0:T(8,128)(2,1)}, u32[]{:S(2)}, u32[]{:S(2)}) collective-permute-start(bf16[1,80,2560]{2,1,0:T(8,128)(2,1)} %copy-done.30), channel_id=1, source_target_pairs={{0,6},{1,7},{2,0},{3,1},{4,2},{5,3},{6,4},{7,5},{8,14},{9,15},{10,... | collective-permute-start | bytes 1228808 | tf_op jit(solution)/shard_map/ppermute | solution.py:418
  38.1 11.5 %collective-permute-start.11 = (bf16[1,80,2560]{2,1,0:T(8,128)(2,1)}, bf16[1,80,2560]{2,1,0:T(8,128)(2,1)}, u32[]{:S(2)}, u32[]{:S(2)}) collective-permute-start(bf16[1,80,2560]{2,1,0:T(8,128)(2,1)} %collective-permute-done.8.rest_6_), channel_id=1, source_target_pairs={{0,1},{1,0},{2,3},{3,2},{4,5},{5,4},{6,7},{7,6},{8,9},{9,8},{10,11... | collective-permute-start | bytes 1228808 | tf_op jit(solution)/shard_map/ppermute | solution.py:418
  42.6 31.4 %copy-start.1 = (bf16[4,128,1280]{2,1,0:T(8,128)(2,1)S(1)}, bf16[4,128,1280]{2,1,0:T(8,128)(2,1)}, u32[]{:S(2)}) copy-start(bf16[4,128,1280]{2,1,0:T(8,128)(2,1)} %cot_ref.3) | copy-start | bytes 3932164
  46.0 4.6 %collective-permute-start.18 = (bf16[1,80,2560]{2,1,0:T(8,128)(2,1)}, bf16[1,80,2560]{2,1,0:T(8,128)(2,1)S(1)}, u32[]{:S(2)}, u32[]{:S(2)}) collective-permute-start(bf16[1,80,2560]{2,1,0:T(8,128)(2,1)} %collective-permute-done.6.rest_10_), channel_id=1, source_target_pairs={{0,1},{1,0},{2,3},{3,2},{4,5},{5,4},{6,7},{7,6},{8,9},{9,8},{10,11... | collective-permute-start | bytes 1228808 | tf_op jit(solution)/shard_map/ppermute | solution.py:418
  47.1 4.1 %collective-permute-start.10 = (bf16[1,80,2560]{2,1,0:T(8,128)(2,1)S(1)}, bf16[1,80,2560]{2,1,0:T(8,128)(2,1)S(1)}, u32[]{:S(2)}, u32[]{:S(2)}) collective-permute-start(bf16[1,80,2560]{2,1,0:T(8,128)(2,1)S(1)} %copy-done.6), channel_id=1, source_target_pairs={{0,1},{1,0},{2,3},{3,2},{4,5},{5,4},{6,7},{7,6},{8,9},{9,8},{10,11... | collective-permute-start | bytes 1228808 | tf_op jit(solution)/shard_map/ppermute | solution.py:418
  47.6 12.5 %collective-permute-start.21 = (bf16[1,80,2560]{2,1,0:T(8,128)(2,1)}, bf16[1,80,2560]{2,1,0:T(8,128)(2,1)S(1)}, u32[]{:S(2)}, u32[]{:S(2)}) collective-permute-start(bf16[1,80,2560]{2,1,0:T(8,128)(2,1)} %collective-permute-done.13.rest_12_), channel_id=1, source_target_pairs={{0,16},{1,17},{2,18},{3,19},{4,20},{5,21},{6,22},{7,23},{8,24},{9,... | collective-permute-start | bytes 1228808 | tf_op jit(solution)/shard_map/ppermute | solution.py:418
  48.1 12.8 %collective-permute-start.16 = (bf16[1,80,2560]{2,1,0:T(8,128)(2,1)S(1)}, bf16[1,80,2560]{2,1,0:T(8,128)(2,1)S(1)}, u32[]{:S(2)}, u32[]{:S(2)}) collective-permute-start(bf16[1,80,2560]{2,1,0:T(8,128)(2,1)S(1)} %fusion.7), channel_id=1, source_target_pairs={{0,2},{1,3},{2,4},{3,5},{4,6},{5,7},{6,0},{7,1},{8,10},{9,11},{10,... | collective-permute-start | bytes 1228808 | tf_op jit(solution)/shard_map/ppermute | solution.py:418
  49.6 21.3 %collective-permute-start.28 = (bf16[1,80,2560]{2,1,0:T(8,128)(2,1)S(1)}, bf16[1,80,2560]{2,1,0:T(8,128)(2,1)S(1)}, u32[]{:S(2)}, u32[]{:S(2)}) collective-permute-start(bf16[1,80,2560]{2,1,0:T(8,128)(2,1)S(1)} %fusion.7), channel_id=1, source_target_pairs={{0,6},{1,7},{2,0},{3,1},{4,2},{5,3},{6,4},{7,5},{8,14},{9,15},{10,... | collective-permute-start | bytes 1228808 | tf_op jit(solution)/shard_map/ppermute | solution.py:418
  50.6 25.8 %copy-start.8 = (bf16[1,80,2560]{2,1,0:T(8,128)(2,1)}, bf16[1,80,2560]{2,1,0:T(8,128)(2,1)S(1)}, u32[]{:S(2)}) copy-start(bf16[1,80,2560]{2,1,0:T(8,128)(2,1)S(1)} %collective-permute-done.18.rest_11_) | copy-start | bytes 1228804
  50.6 20.3 %collective-permute-start.24 = (bf16[1,80,2560]{2,1,0:T(8,128)(2,1)}, bf16[1,80,2560]{2,1,0:T(8,128)(2,1)S(1)}, u32[]{:S(2)}, u32[]{:S(2)}) collective-permute-start(bf16[1,80,2560]{2,1,0:T(8,128)(2,1)} %collective-permute-done.12.rest_18_), channel_id=1, source_target_pairs={{0,8},{1,9},{2,10},{3,11},{4,12},{5,13},{6,14},{7,15},{8,0},{9,1},... | collective-permute-start | bytes 1228808 | tf_op jit(solution)/shard_map/ppermute | solution.py:418
  51.2 25.2 %copy-start.9 = (bf16[1,80,2560]{2,1,0:T(8,128)(2,1)}, bf16[1,80,2560]{2,1,0:T(8,128)(2,1)S(1)}, u32[]{:S(2)}) copy-start(bf16[1,80,2560]{2,1,0:T(8,128)(2,1)S(1)} %collective-permute-done.10.rest_5_) | copy-start | bytes 1228804
  51.2 20.3 %collective-permute-start.26 = (bf16[1,80,2560]{2,1,0:T(8,128)(2,1)}, bf16[1,80,2560]{2,1,0:T(8,128)(2,1)S(1)}, u32[]{:S(2)}, u32[]{:S(2)}) collective-permute-start(bf16[1,80,2560]{2,1,0:T(8,128)(2,1)} %collective-permute-done.12.rest_18_), channel_id=1, source_target_pairs={{0,16},{1,17},{2,18},{3,19},{4,20},{5,21},{6,22},{7,23},{8,24},{9,... | collective-permute-start | bytes 1228808 | tf_op jit(solution)/shard_map/ppermute | solution.py:418
  60.2 16.2 %copy-start.10 = (bf16[1,80,2560]{2,1,0:T(8,128)(2,1)}, bf16[1,80,2560]{2,1,0:T(8,128)(2,1)S(1)}, u32[]{:S(2)}) copy-start(bf16[1,80,2560]{2,1,0:T(8,128)(2,1)S(1)} %collective-permute-done.21.rest_16_) | copy-start | bytes 1228804
  60.2 11.3 %collective-permute-start.23 = (bf16[1,80,2560]{2,1,0:T(8,128)(2,1)}, bf16[1,80,2560]{2,1,0:T(8,128)(2,1)S(1)}, u32[]{:S(2)}, u32[]{:S(2)}) collective-permute-start(bf16[1,80,2560]{2,1,0:T(8,128)(2,1)} %collective-permute-done.12.rest_18_), channel_id=1, source_target_pairs={{0,1},{1,0},{2,3},{3,2},{4,5},{5,4},{6,7},{7,6},{8,9},{9,8},{10,11... | collective-permute-start | bytes 1228808 | tf_op jit(solution)/shard_map/ppermute | solution.py:418
  60.9 15.5 %copy-start.11 = (bf16[1,80,2560]{2,1,0:T(8,128)(2,1)}, bf16[1,80,2560]{2,1,0:T(8,128)(2,1)S(1)}, u32[]{:S(2)}) copy-start(bf16[1,80,2560]{2,1,0:T(8,128)(2,1)S(1)} %collective-permute-done.16.rest_8_) | copy-start | bytes 1228804
  60.9 11.0 %collective-permute-start.22 = (bf16[1,80,2560]{2,1,0:T(8,128)(2,1)S(1)}, bf16[1,80,2560]{2,1,0:T(8,128)(2,1)S(1)}, u32[]{:S(2)}, u32[]{:S(2)}) collective-permute-start(bf16[1,80,2560]{2,1,0:T(8,128)(2,1)S(1)} %collective-permute-done.21.rest_16_), channel_id=1, source_target_pairs={{0,1},{1,0},{2,3},{3,2},{4,5},{5,4},{6,7},{7,6},{8,9},{9,8},{10,11... | collective-permute-start | bytes 1228808 | tf_op jit(solution)/shard_map/ppermute | solution.py:418
  70.9 2.0 collective-permute-start.20
  70.9 3.1 %collective-permute-start.19 = (bf16[1,80,2560]{2,1,0:T(8,128)(2,1)}, bf16[1,80,2560]{2,1,0:T(8,128)(2,1)S(1)}, u32[]{:S(2)}, u32[]{:S(2)}) collective-permute-start(bf16[1,80,2560]{2,1,0:T(8,128)(2,1)} %collective-permute-done.13.rest_12_), channel_id=1, source_target_pairs={{0,1},{1,0},{2,3},{3,2},{4,5},{5,4},{6,7},{7,6},{8,9},{9,8},{10,11... | collective-permute-start | bytes 1228808 | tf_op jit(solution)/shard_map/ppermute | solution.py:418
  71.4 2.8 %collective-permute-start.17 = (bf16[1,80,2560]{2,1,0:T(8,128)(2,1)S(1)}, bf16[1,80,2560]{2,1,0:T(8,128)(2,1)S(1)}, u32[]{:S(2)}, u32[]{:S(2)}) collective-permute-start(bf16[1,80,2560]{2,1,0:T(8,128)(2,1)S(1)} %collective-permute-done.16.rest_8_), channel_id=1, source_target_pairs={{0,1},{1,0},{2,3},{3,2},{4,5},{5,4},{6,7},{7,6},{8,9},{9,8},{10,11... | collective-permute-start | bytes 1228808 | tf_op jit(solution)/shard_map/ppermute | solution.py:418
  71.5 2.9 %collective-permute-start.29 = (bf16[1,80,2560]{2,1,0:T(8,128)(2,1)S(1)}, bf16[1,80,2560]{2,1,0:T(8,128)(2,1)S(1)}, u32[]{:S(2)}, u32[]{:S(2)}) collective-permute-start(bf16[1,80,2560]{2,1,0:T(8,128)(2,1)S(1)} %collective-permute-done.28.rest_24_), channel_id=1, source_target_pairs={{0,1},{1,0},{2,3},{3,2},{4,5},{5,4},{6,7},{7,6},{8,9},{9,8},{10,11... | collective-permute-start | bytes 1228808 | tf_op jit(solution)/shard_map/ppermute | solution.py:418
  71.9 3.6 %collective-permute-start.25 = (bf16[1,80,2560]{2,1,0:T(8,128)(2,1)S(1)}, bf16[1,80,2560]{2,1,0:T(8,128)(2,1)S(1)}, u32[]{:S(2)}, u32[]{:S(2)}) collective-permute-start(bf16[1,80,2560]{2,1,0:T(8,128)(2,1)S(1)} %collective-permute-done.24.rest_20_), channel_id=1, source_target_pairs={{0,1},{1,0},{2,3},{3,2},{4,5},{5,4},{6,7},{7,6},{8,9},{9,8},{10,11... | collective-permute-start | bytes 1228808 | tf_op jit(solution)/shard_map/ppermute | solution.py:418
  72.9 3.5 %collective-permute-start.27 = (bf16[1,80,2560]{2,1,0:T(8,128)(2,1)S(1)}, bf16[1,80,2560]{2,1,0:T(8,128)(2,1)}, u32[]{:S(2)}, u32[]{:S(2)}) collective-permute-start(bf16[1,80,2560]{2,1,0:T(8,128)(2,1)S(1)} %collective-permute-done.26.rest_22_), channel_id=1, source_target_pairs={{0,1},{1,0},{2,3},{3,2},{4,5},{5,4},{6,7},{7,6},{8,9},{9,8},{10,11... | collective-permute-start | bytes 1228808 | tf_op jit(solution)/shard_map/ppermute | solution.py:418
  74.0 41.8 %collective-permute-start.34 = (bf16[4,128,1280]{2,1,0:T(8,128)(2,1)S(1)}, bf16[4,128,1280]{2,1,0:T(8,128)(2,1)}, u32[]{:S(2)}, u32[]{:S(2)}) collective-permute-start(bf16[4,128,1280]{2,1,0:T(8,128)(2,1)S(1)} %copy-done.1), channel_id=1, source_target_pairs={{0,1},{1,0},{2,3},{3,2},{4,5},{5,4},{6,7},{7,6},{8,9},{9,8},{10,11... | collective-permute-start | bytes 3932168 | tf_op jit(solution)/shard_map/ppermute | solution.py:418
  95.9 2.4 %collective-permute-start.30 = (bf16[4,128,640]{2,1,0:T(8,128)(2,1)}, bf16[4,128,640]{2,1,0:T(8,128)(2,1)S(1)}, u32[]{:S(2)}, u32[]{:S(2)}) collective-permute-start(bf16[4,128,640]{2,1,0:T(8,128)(2,1)} %get-tuple-element.65.rest_0_.dq_ref), channel_id=1, source_target_pairs={{0,1},{1,0},{2,3},{3,2},{4,5},{5,4},{6,7},{7,6},{8,9},{9,8},{10,11... | collective-permute-start | bytes 1966088 | tf_op jit(solution)/shard_map/ppermute | solution.py:418
  96.3 3.8 %collective-permute-start.31 = (bf16[4,128,640]{2,1,0:T(8,128)(2,1)}, bf16[4,128,640]{2,1,0:T(8,128)(2,1)S(1)}, u32[]{:S(2)}, u32[]{:S(2)}) collective-permute-start(bf16[4,128,640]{2,1,0:T(8,128)(2,1)} %get-tuple-element.66.rest_2_.dk_ref), channel_id=1, source_target_pairs={{0,1},{1,0},{2,3},{3,2},{4,5},{5,4},{6,7},{7,6},{8,9},{9,8},{10,11... | collective-permute-start | bytes 1966088 | tf_op jit(solution)/shard_map/ppermute | solution.py:418
  96.4 4.6 %collective-permute-start.32 = (bf16[4,128,640]{2,1,0:T(8,128)(2,1)}, bf16[4,128,640]{2,1,0:T(8,128)(2,1)S(1)}, u32[]{:S(2)}, u32[]{:S(2)}) collective-permute-start(bf16[4,128,640]{2,1,0:T(8,128)(2,1)} %get-tuple-element.67.rest_4_.dv_ref), channel_id=1, source_target_pairs={{0,1},{1,0},{2,3},{3,2},{4,5},{5,4},{6,7},{7,6},{8,9},{9,8},{10,11... | collective-permute-start | bytes 1966088 | tf_op jit(solution)/shard_map/ppermute | solution.py:418
  96.8 19.1 %collective-permute-start.33 = (bf16[4,640,128]{2,1,0:T(8,128)(2,1)}, bf16[4,640,128]{2,1,0:T(8,128)(2,1)}, u32[]{:S(2)}, u32[]{:S(2)}) collective-permute-start(bf16[4,640,128]{2,1,0:T(8,128)(2,1)} %get-tuple-element.72.attnt_a.attnt_ref), channel_id=1, source_target_pairs={{0,1},{1,0},{2,3},{3,2},{4,5},{5,4},{6,7},{7,6},{8,9},{9,8},{10,11... | collective-permute-start | bytes 1966088 | tf_op jit(solution)/shard_map/ppermute | solution.py:418
  113.2 31.3 %collective-permute-start.36 = (bf16[2,4,80,1024]{3,2,1,0:T(8,128)(2,1)}, bf16[2,4,80,1024]{3,2,1,0:T(8,128)(2,1)}, u32[]{:S(2)}, u32[]{:S(2)}) collective-permute-start(bf16[2,4,80,1024]{3,2,1,0:T(8,128)(2,1)} %get-tuple-element.68), channel_id=1, source_target_pairs={{0,16},{1,17},{2,18},{3,19},{4,20},{5,21},{6,22},{7,23},{8,24},{9,... | collective-permute-start | bytes 3932168 | tf_op jit(solution)/shard_map/ppermute | solution.py:418
  114.7 27.5 %collective-permute-start.37 = (bf16[2,4,80,896]{3,2,1,0:T(8,128)(2,1)}, bf16[2,4,80,896]{3,2,1,0:T(8,128)(2,1)}, u32[]{:S(2)}, u32[]{:S(2)}) collective-permute-start(bf16[2,4,80,896]{3,2,1,0:T(8,128)(2,1)} %get-tuple-element.77), channel_id=1, source_target_pairs={{0,8},{1,9},{2,10},{3,11},{4,12},{5,13},{6,14},{7,15},{8,0},{9,1},... | collective-permute-start | bytes 3440648 | tf_op jit(solution)/shard_map/ppermute | solution.py:418
  121.6 20.0 %collective-permute-start.35 = (bf16[2,4,80,640]{3,2,1,0:T(8,128)(2,1)}, bf16[2,4,80,640]{3,2,1,0:T(8,128)(2,1)}, u32[]{:S(2)}, u32[]{:S(2)}) collective-permute-start(bf16[2,4,80,640]{3,2,1,0:T(8,128)(2,1)} %get-tuple-element.76), channel_id=1, source_target_pairs={{0,2},{1,3},{2,0},{3,1},{4,6},{5,7},{6,4},{7,5},{8,10},{9,11},{10,... | collective-permute-start | bytes 2457608 | tf_op jit(solution)/shard_map/ppermute | solution.py:418
  146.0 11.1 %collective-permute-start.38 = (bf16[4,80,512]{2,1,0:T(8,128)(2,1)S(1)}, bf16[4,80,512]{2,1,0:T(8,128)(2,1)S(1)}, u32[]{:S(2)}, u32[]{:S(2)}) collective-permute-start(bf16[4,80,512]{2,1,0:T(8,128)(2,1)S(1)} %get-tuple-element.90), channel_id=1, source_target_pairs={{0,8},{1,9},{2,10},{3,11},{4,12},{5,13},{6,14},{7,15},{8,0},{9,1},... | collective-permute-start | bytes 983048 | tf_op jit(solution)/shard_map/ppermute | solution.py:418
  147.2 15.1 %collective-permute-start.44 = (bf16[4,80,512]{2,1,0:T(8,128)(2,1)S(1)}, bf16[4,80,512]{2,1,0:T(8,128)(2,1)S(1)}, u32[]{:S(2)}, u32[]{:S(2)}) collective-permute-start(bf16[4,80,512]{2,1,0:T(8,128)(2,1)S(1)} %get-tuple-element.91), channel_id=1, source_target_pairs={{0,8},{1,9},{2,10},{3,11},{4,12},{5,13},{6,14},{7,15},{8,0},{9,1},... | collective-permute-start | bytes 983048 | tf_op jit(solution)/shard_map/ppermute | solution.py:418
  149.1 7.0 %collective-permute-start.45 = (bf16[4,80,384]{2,1,0:T(8,128)(2,1)S(1)}, bf16[4,80,384]{2,1,0:T(8,128)(2,1)S(1)}, u32[]{:S(2)}, u32[]{:S(2)}) collective-permute-start(bf16[4,80,384]{2,1,0:T(8,128)(2,1)S(1)} %fusion.6), channel_id=1, source_target_pairs={{0,16},{1,17},{2,18},{3,19},{4,20},{5,21},{6,22},{7,23},{8,24},{9,... | collective-permute-start | bytes 737288 | tf_op jit(solution)/shard_map/ppermute | solution.py:418
  152.8 25.3 %collective-permute-start.50 = (bf16[4,80,640]{2,1,0:T(8,128)(2,1)S(1)}, bf16[4,80,640]{2,1,0:T(8,128)(2,1)S(1)}, u32[]{:S(2)}, u32[]{:S(2)}) collective-permute-start(bf16[4,80,640]{2,1,0:T(8,128)(2,1)S(1)} %fusion.1), channel_id=1, source_target_pairs={{0,4},{1,5},{2,6},{3,7},{4,0},{5,1},{6,2},{7,3},{8,12},{9,13},{10,... | collective-permute-start | bytes 1228808 | tf_op jit(solution)/shard_map/ppermute | solution.py:418
  155.1 12.8 %collective-permute-start.39 = (bf16[4,80,512]{2,1,0:T(8,128)(2,1)S(1)}, bf16[4,80,512]{2,1,0:T(8,128)(2,1)S(1)}, u32[]{:S(2)}, u32[]{:S(2)}) collective-permute-start(bf16[4,80,512]{2,1,0:T(8,128)(2,1)S(1)} %fusion.4), channel_id=1, source_target_pairs={{0,16},{1,17},{2,18},{3,19},{4,20},{5,21},{6,22},{7,23},{8,24},{9,... | collective-permute-start | bytes 983048 | tf_op jit(solution)/shard_map/ppermute | solution.py:418
  163.8 18.8 %collective-permute-start.46 = (bf16[80,896]{1,0:T(8,128)(2,1)S(1)}, bf16[80,896]{1,0:T(8,128)(2,1)S(1)}, u32[]{:S(2)}, u32[]{:S(2)}) collective-permute-start(bf16[80,896]{1,0:T(8,128)(2,1)S(1)} %get-tuple-element.102), channel_id=1, source_target_pairs={{0,2},{1,3},{2,4},{3,5},{4,6},{5,7},{6,0},{7,1},{8,10},{9,11},{10,... | collective-permute-start | bytes 430088 | tf_op jit(solution)/shard_map/ppermute | solution.py:418
  165.4 23.1 %collective-permute-start.47 = (bf16[80,896]{1,0:T(8,128)(2,1)S(1)}, bf16[80,896]{1,0:T(8,128)(2,1)S(1)}, u32[]{:S(2)}, u32[]{:S(2)}) collective-permute-start(bf16[80,896]{1,0:T(8,128)(2,1)S(1)} %get-tuple-element.104), channel_id=1, source_target_pairs={{0,4},{1,5},{2,6},{3,7},{4,0},{5,1},{6,2},{7,3},{8,12},{9,13},{10,... | collective-permute-start | bytes 430088 | tf_op jit(solution)/shard_map/ppermute | solution.py:418
  167.6 24.3 %collective-permute-start.48 = (bf16[80,896]{1,0:T(8,128)(2,1)S(1)}, bf16[80,896]{1,0:T(8,128)(2,1)S(1)}, u32[]{:S(2)}, u32[]{:S(2)}) collective-permute-start(bf16[80,896]{1,0:T(8,128)(2,1)S(1)} %get-tuple-element.103), channel_id=1, source_target_pairs={{0,6},{1,7},{2,0},{3,1},{4,2},{5,3},{6,4},{7,5},{8,14},{9,15},{10,... | collective-permute-start | bytes 430088 | tf_op jit(solution)/shard_map/ppermute | solution.py:418
  169.3 25.4 %collective-permute-start.40 = (bf16[80,1024]{1,0:T(8,128)(2,1)S(1)}, bf16[80,1024]{1,0:T(8,128)(2,1)S(1)}, u32[]{:S(2)}, u32[]{:S(2)}) collective-permute-start(bf16[80,1024]{1,0:T(8,128)(2,1)S(1)} %get-tuple-element.95), channel_id=1, source_target_pairs={{0,2},{1,3},{2,4},{3,5},{4,6},{5,7},{6,0},{7,1},{8,10},{9,11},{10,... | collective-permute-start | bytes 491528 | tf_op jit(solution)/shard_map/ppermute | solution.py:418
  178.1 19.6 %collective-permute-start.41 = (bf16[80,1024]{1,0:T(8,128)(2,1)S(1)}, bf16[80,1024]{1,0:T(8,128)(2,1)S(1)}, u32[]{:S(2)}, u32[]{:S(2)}) collective-permute-start(bf16[80,1024]{1,0:T(8,128)(2,1)S(1)} %get-tuple-element.97), channel_id=1, source_target_pairs={{0,4},{1,5},{2,6},{3,7},{4,0},{5,1},{6,2},{7,3},{8,12},{9,13},{10,... | collective-permute-start | bytes 491528 | tf_op jit(solution)/shard_map/ppermute | solution.py:418
  182.6 16.2 %collective-permute-start.42 = (bf16[80,1024]{1,0:T(8,128)(2,1)S(1)}, bf16[80,1024]{1,0:T(8,128)(2,1)S(1)}, u32[]{:S(2)}, u32[]{:S(2)}) collective-permute-start(bf16[80,1024]{1,0:T(8,128)(2,1)S(1)} %get-tuple-element.96), channel_id=1, source_target_pairs={{0,6},{1,7},{2,0},{3,1},{4,2},{5,3},{6,4},{7,5},{8,14},{9,15},{10,... | collective-permute-start | bytes 491528 | tf_op jit(solution)/shard_map/ppermute | solution.py:418
  192.0 8.4 %collective-permute-start.51 = (bf16[2,80,384]{2,1,0:T(8,128)(2,1)S(1)}, bf16[2,80,384]{2,1,0:T(8,128)(2,1)S(1)}, u32[]{:S(2)}, u32[]{:S(2)}) collective-permute-start(bf16[2,80,384]{2,1,0:T(8,128)(2,1)S(1)} %slice.200), channel_id=1, source_target_pairs={{0,16},{1,17},{2,18},{3,19},{4,20},{5,21},{6,22},{7,23},{8,24},{9,... | collective-permute-start | bytes 368648 | tf_op jit(solution)/shard_map/ppermute | solution.py:418
  192.9 6.9 %collective-permute-start.53 = (bf16[2,80,256]{2,1,0:T(8,128)(2,1)S(1)}, bf16[2,80,256]{2,1,0:T(8,128)(2,1)S(1)}, u32[]{:S(2)}, u32[]{:S(2)}) collective-permute-start(bf16[2,80,256]{2,1,0:T(8,128)(2,1)S(1)} %pad_maximum_fusion.3), channel_id=1, source_target_pairs={{0,8},{1,9},{2,10},{3,11},{4,12},{5,13},{6,14},{7,15},{8,0},{9,1},... | collective-permute-start | bytes 245768 | tf_op jit(solution)/shard_map/ppermute | solution.py:418
  194.7 9.2 %collective-permute-start.49 = (bf16[80,896]{1,0:T(8,128)(2,1)S(1)}, bf16[80,896]{1,0:T(8,128)(2,1)S(1)}, u32[]{:S(2)}, u32[]{:S(2)}) collective-permute-start(bf16[80,896]{1,0:T(8,128)(2,1)S(1)} %get-tuple-element.87), channel_id=1, source_target_pairs={{0,8},{1,9},{2,10},{3,11},{4,12},{5,13},{6,14},{7,15},{8,0},{9,1},... | collective-permute-start | bytes 430088 | tf_op jit(solution)/shard_map/ppermute | solution.py:418
  198.9 6.8 %collective-permute-start.43 = (bf16[80,1024]{1,0:T(8,128)(2,1)S(1)}, bf16[80,1024]{1,0:T(8,128)(2,1)S(1)}, u32[]{:S(2)}, u32[]{:S(2)}) collective-permute-start(bf16[80,1024]{1,0:T(8,128)(2,1)S(1)} %get-tuple-element.85), channel_id=1, source_target_pairs={{0,8},{1,9},{2,10},{3,11},{4,12},{5,13},{6,14},{7,15},{8,0},{9,1},... | collective-permute-start | bytes 491528 | tf_op jit(solution)/shard_map/ppermute | solution.py:418
  199.8 4.1 %collective-permute-start.54 = (bf16[80,256]{1,0:T(8,128)(2,1)S(1)}, bf16[80,256]{1,0:T(8,128)(2,1)S(1)}, u32[]{:S(2)}, u32[]{:S(2)}) collective-permute-start(bf16[80,256]{1,0:T(8,128)(2,1)S(1)} %fusion.16), channel_id=1, source_target_pairs={{0,16},{1,17},{2,18},{3,19},{4,20},{5,21},{6,22},{7,23},{8,24},{9,... | collective-permute-start | bytes 122888 | tf_op jit(solution)/shard_map/ppermute | solution.py:418
  200.5 7.8 %collective-permute-start.52 = (bf16[80,384]{1,0:T(8,128)(2,1)S(1)}, bf16[80,384]{1,0:T(8,128)(2,1)S(1)}, u32[]{:S(2)}, u32[]{:S(2)}) collective-permute-start(bf16[80,384]{1,0:T(8,128)(2,1)S(1)} %fusion.15), channel_id=1, source_target_pairs={{0,8},{1,9},{2,10},{3,11},{4,12},{5,13},{6,14},{7,15},{8,0},{9,1},... | collective-permute-start | bytes 184328 | tf_op jit(solution)/shard_map/ppermute | solution.py:418
  208.3 4.7 %collective-permute-start.55 = (bf16[80,640]{1,0:T(8,128)(2,1)S(1)}, bf16[80,640]{1,0:T(8,128)(2,1)S(1)}, u32[]{:S(2)}, u32[]{:S(2)}) collective-permute-start(bf16[80,640]{1,0:T(8,128)(2,1)S(1)} %fusion.20), channel_id=1, source_target_pairs={{0,8},{1,9},{2,10},{3,11},{4,12},{5,13},{6,14},{7,15},{8,0},{9,1},... | collective-permute-start | bytes 307208 | tf_op jit(solution)/shard_map/ppermute | solution.py:418
  (26 other events, 102.3 us)

commit v5 on v4

--- a/solution.py
+++ b/solution.py
@@ -641,14 +641,16 @@
         )
         out_near = send(out_sent, route["z1"])
         encoded, block_grad = results(tied(attnt, out_own))
-        out_near, *arrived = lax.optimization_barrier((out_near, *arrived, encoded))[:3]
+        out_near = tied(out_near, encoded)
+        out_value = (out_far + out_near[1].astype(F32)).astype(BF16)
+        *arrived, out_value = lax.optimization_barrier((*arrived, out_value))
+        out_next = send(out_value, route["z2"])
         parts = []
         for first, last in STEPS:
             step_arrived = (arrived[0][..., first], arrived[1][..., last])
             own = jnp.concatenate([terms[2][..., :QKV_CUT][..., first], terms[2][..., QKV_CUT:][..., last]], axis=2)
             step_terms = (None, None, own, terms[3][..., first], terms[4][..., last])
             parts.append(line_parts(reduce_plane(step_terms, step_arrived, route), z))
-        out_next = send((out_far + out_near[1].astype(F32)).astype(BF16), route["z2"])
         shares = [add_line(part[0], send_line(part, route)) for part in parts]
         out_total = tied(out_own + out_near[0].astype(F32) + out_next.astype(F32), *parts[1])
         terms = plane_terms(out_total, OUT_CUT)

time: 214 us -> 213 us (level)
  transfers between devices with their start and end apart: 56 -> 56, of which waited for: 30 -> 31; matrix products, arithmetic and copies ran while one was open for 7% -> 7% of each run, Pallas kernels for 28% -> 29%
where the time goes in v5:
time: 213 us; the launch traced here: 212 us
  waiting for transfers between devices  72.5 us (34%)
  Pallas kernels  61 us (29%)
  starting transfers between devices  53.7 us (25%)
  other arithmetic  16.4 us (8%)
  local copies, waits for them, and re-layouts  7.18 us (3%)
    ppermute x56, waiting for transfers between devices, send(): return lax.ppermute(value, AXES, route)  72.5 us
    ppermute x56, starting transfers between devices, send(): return lax.ppermute(value, AXES, route)  53.7 us
    pallas_call x1, Pallas kernels, shards(): pl.pallas_call(functools.partial(layer_kernel, routed, n_weights), out_sh...  19.7 us
    pallas_call x1, Pallas kernels, results(): pl.pallas_call(functools.partial(result_kernel, routed, n_weights), out_s...  16.1 us
    pallas_call x1, Pallas kernels, qkv_terms(): pl.pallas_call(qkv_terms_kernel, out_shape=[jax.ShapeDtypeStruct((2, 4, r...  11.3 us
    pallas_call x1, Pallas kernels, out_terms(): pl.pallas_call(out_terms_kernel, out_shape=[jax.ShapeDtypeStruct((4, rows...  5.76 us
    pallas_call x1, Pallas kernels, normed(): pl.pallas_call(norm_kernel, out_shape=[jax.ShapeDtypeStruct(blocks.shape,...  4.31 us
  transfers between devices with their start and end apart: 56, of which 31 were waited for; matrix products, arithmetic and copies ran while one was open for 7% of the time, Pallas kernels for 29%

profile of v5, /device:TPU:8, one launch (start us, length us, event | category | flops | bytes accessed | tf_op | source)
XLA Modules:
  0.0 212.1 jit_solution(17125889196538090115)
XLA Ops:
  0.7 1.0 constant_dynamic-slice_fusion.2
  1.7 0.9 constant_dynamic-slice_fusion.1
  2.7 1.6 collective-permute-start.4
  5.7 1.6 collective-permute-start.1
  7.3 1.2 collective-permute-start.2
  9.6 4.5 %collective-permute-done.1 = f32[2,320]{1,0:T(2,128)S(1)} collective-permute-done((f32[2,320]{1,0:T(2,128)S(1)}, f32[2,320]{1,0:T(2,128)S(1)}, u32[]{:S(2)}, u32[]{:S(2)}) %collective-permute-start.1) | collective-permute-done | bytes 2592 | tf_op jit(solution)/shard_map/ppermute | solution.py:418
  16.1 1.6 pad_maximum_fusion.rest_0_
  18.7 1.5 collective-permute-start.7
  20.1 1.5 collective-permute-start.8
  21.7 4.3 %norm.1 = (bf16[4,128,1280]{2,1,0:T(8,128)(2,1)}, bf16[4,1280,128]{2,1,0:T(8,128)(2,1)}) custom-call(s32[4]{0:T(128)} %kind_ref.5, bf16[4,128,1280]{2,1,0:T(8,128)(2,1)} %x_ref.2, f32[2,1280]{1,0:T(2,128)} %reshape.101.gain_ref), custom_call_target="tpu_custom_call" | custom-call | flops 11500000 | tf_op jit(solution)/shard_map/norm/pallas_call | solution.py:542
  26.0 3.8 %collective-permute-done.6.rest_10_ = bf16[1,80,2560]{2,1,0:T(8,128)(2,1)} collective-permute-done((bf16[1,80,2560]{2,1,0:T(8,128)(2,1)S(1)}, bf16[1,80,2560]{2,1,0:T(8,128)(2,1)}, u32[]{:S(2)}, u32[]{:S(2)}) %collective-permute-start.6) | collective-permute-done | bytes 409632 | tf_op jit(solution)/shard_map/ppermute | solution.py:418
  30.3 1.2 collective-permute-done.8.rest_6_
  32.6 1.5 collective-permute-start.14
  34.1 2.6 %collective-permute-start.12 = (bf16[1,80,2560]{2,1,0:T(8,128)(2,1)}, bf16[1,80,2560]{2,1,0:T(8,128)(2,1)}, u32[]{:S(2)}, u32[]{:S(2)}) collective-permute-start(bf16[1,80,2560]{2,1,0:T(8,128)(2,1)} %copy-done.28), channel_id=1, source_target_pairs={{0,6},{1,7},{2,0},{3,1},{4,2},{5,3},{6,4},{7,5},{8,14},{9,15},{10,... | collective-permute-start | bytes 1228808 | tf_op jit(solution)/shard_map/ppermute | solution.py:418
  38.5 3.8 %left_factor.1.left = bf16[2,2,640,512]{3,2,1,0:T(8,128)(2,1)} custom-call(s32[3]{0:T(128)} %pad_add_fusion.where_ref, s32[8]{0:T(128)} %pad_add_fusion.1.kind_ref, bf16[4,1280,128]{2,1,0:T(8,128)(2,1)} %get-tuple-element.57.ht_a, bf16[4,1280,128]{2,1,0:T(8,128)(2,1)} %collective-permute-done.15.ht_b), custom_call_target="tpu_custom_call" | custom-call | flops 11500000 | tf_op jit(solution)/shard_map/left_factor/pallas_call | solution.py:343
  42.3 3.2 %collective-permute-done.12.rest_18_ = bf16[1,80,2560]{2,1,0:T(8,128)(2,1)} collective-permute-done((bf16[1,80,2560]{2,1,0:T(8,128)(2,1)}, bf16[1,80,2560]{2,1,0:T(8,128)(2,1)}, u32[]{:S(2)}, u32[]{:S(2)}) %collective-permute-start.12) | collective-permute-done | bytes 409632 | tf_op jit(solution)/shard_map/ppermute | solution.py:418
  45.4 1.0 fusion.7
  47.0 1.8 collective-permute-start.16
  49.6 0.9 collective-permute-start.24
  50.5 1.5 collective-permute-start.26
  52.0 7.0 %collective-permute-done.21.rest_16_ = bf16[1,80,2560]{2,1,0:T(8,128)(2,1)S(1)} collective-permute-done((bf16[1,80,2560]{2,1,0:T(8,128)(2,1)}, bf16[1,80,2560]{2,1,0:T(8,128)(2,1)S(1)}, u32[]{:S(2)}, u32[]{:S(2)}) %collective-permute-start.21) | collective-permute-done | bytes 409632 | tf_op jit(solution)/shard_map/ppermute | solution.py:418
  59.8 10.6 %collective-permute-done.28.rest_24_ = bf16[1,80,2560]{2,1,0:T(8,128)(2,1)S(1)} collective-permute-done((bf16[1,80,2560]{2,1,0:T(8,128)(2,1)S(1)}, bf16[1,80,2560]{2,1,0:T(8,128)(2,1)S(1)}, u32[]{:S(2)}, u32[]{:S(2)}) %collective-permute-start.28) | collective-permute-done | bytes 409632 | tf_op jit(solution)/shard_map/ppermute | solution.py:418
  73.9 1.2 collective-permute-done.29.rest_25_
  75.1 1.2 collective-permute-done.25.rest_21_
  77.1 19.7 %layer.1 = (bf16[4,640,128]{2,1,0:T(8,128)(2,1)}, bf16[4,128,640]{2,1,0:T(8,128)(2,1)}, bf16[4,128,640]{2,1,0:T(8,128)(2,1)}, bf16[4,128,640]{2,1,0:T(8,128)(2,1)}) custom-call(s32[3]{0:T(128)} %pad_add_fusion.where_ref, s32[4]{0:T(128)} %kind_ref.5, bf16[4,128,1280]{2,1,0:T(8,128)(2,1)} %get-tuple-element.49.h_ref, bf16[4,128,1280]{2,1,0:T(8,128)(2,1)} %cot_ref.3, ...), custom_call_target="tpu_custom_call" | custom-call | flops 11500000 | tf_op jit(solution)/shard_map/layer/pallas_call | solution.py:608
  97.9 1.3 collective-permute-done.30.rest_1_
  99.2 1.9 collective-permute-done.31.rest_3_
  101.1 0.9 collective-permute-done.32.rest_5_
  102.9 11.3 %qkv_terms.1 = (bf16[2,4,80,1024]{3,2,1,0:T(8,128)(2,1)}, bf16[2,4,80,896]{3,2,1,0:T(8,128)(2,1)}, f32[4,80,1920]{2,1,0:T(8,128)}, f32[4,80,1024]{2,1,0:T(8,128)}, f32[4,80,896]{2,1,0:T(8,128)}) custom-call(bf16[2,2,640,512]{3,2,1,0:T(8,128)(2,1)} %left_factor.1.left, bf16[4,128,640]{2,1,0:T(8,128)(2,1)} %get-tuple-element.66.rest_0_.dq_ref, ...), custom_call_target="tpu_custom_call" | custom-call | flops 11500000 | tf_op jit(solution)/shard_map/qkv_terms/pallas_call | solution.py:376
  114.2 3.1 %collective-permute-start.35 = (bf16[2,4,80,1024]{3,2,1,0:T(8,128)(2,1)}, bf16[2,4,80,1024]{3,2,1,0:T(8,128)(2,1)}, u32[]{:S(2)}, u32[]{:S(2)}) collective-permute-start(bf16[2,4,80,1024]{3,2,1,0:T(8,128)(2,1)} %get-tuple-element.69), channel_id=1, source_target_pairs={{0,16},{1,17},{2,18},{3,19},{4,20},{5,21},{6,22},{7,23},{8,24},{9,... | collective-permute-start | bytes 3932168 | tf_op jit(solution)/shard_map/ppermute | solution.py:418
  117.3 1.5 collective-permute-start.36
  118.8 5.8 %out_terms.1 = (f32[4,80,640]{2,1,0:T(8,128)}, f32[4,80,640]{2,1,0:T(8,128)}, bf16[2,4,80,640]{3,2,1,0:T(8,128)(2,1)}) custom-call(s32[3]{0:T(128)} %pad_add_fusion.where_ref, s32[8]{0:T(128)} %pad_add_fusion.1.kind_ref, bf16[4,640,128]{2,1,0:T(8,128)(2,1)} %get-tuple-element.73.attnt_a.attnt_ref, bf16[4,640,128]{2,1,0:T(8,128)(2,1)} %collective-permute-done.33.attnt_b, ...), custom_call_target="tpu_custom_call" | custom-call | flops 11500000 | tf_op jit(solution)/shard_map/out_terms/pallas_call | solution.py:357
  124.6 16.1 %result.1 = (bf16[4,128,1280]{2,1,0:T(8,128)(2,1)}, bf16[4,128,1280]{2,1,0:T(8,128)(2,1)}) custom-call(s32[3]{0:T(128)} %pad_add_fusion.where_ref, s32[4]{0:T(128)} %kind_ref.5, s32[4]{0:T(128)} %rank_ref.1, bf16[4,128,1280]{2,1,0:T(8,128)(2,1)} %x_ref.2, bf16[4,128,1280]{2,1,0:T(8,128)(2,1)} %cot_ref.3, f32[2,1280]{1,0:T(2,128)} %reshape.101.gain_ref, ...), custom_call_target="tpu_custom_call" | custom-call | flops 11500000 | tf_op jit(solution)/shard_map/result/pallas_call | solution.py:622
  140.9 3.7 %collective-permute-done.37 = bf16[2,4,80,640]{3,2,1,0:T(8,128)(2,1)} collective-permute-done((bf16[2,4,80,640]{3,2,1,0:T(8,128)(2,1)}, bf16[2,4,80,640]{3,2,1,0:T(8,128)(2,1)}, u32[]{:S(2)}, u32[]{:S(2)}) %collective-permute-start.37) | collective-permute-done | bytes 819232 | tf_op jit(solution)/shard_map/ppermute | solution.py:418
  144.6 1.1 fusion.2
  145.7 1.0 collective-permute-done.35
  146.7 1.4 fusion.5
  148.0 1.6 collective-permute-start.38
  150.1 1.0 fusion.6
  151.1 1.8 collective-permute-start.45
  152.9 1.0 fusion.4
  155.6 4.4 %collective-permute-done.45 = bf16[4,80,384]{2,1,0:T(8,128)(2,1)S(1)} collective-permute-done((bf16[4,80,384]{2,1,0:T(8,128)(2,1)S(1)}, bf16[4,80,384]{2,1,0:T(8,128)(2,1)S(1)}, u32[]{:S(2)}, u32[]{:S(2)}) %collective-permute-start.45) | collective-permute-done | bytes 245792 | tf_op jit(solution)/shard_map/ppermute | solution.py:418
  160.1 1.0 convert_add_fusion.9
  161.1 3.3 %collective-permute-done.44 = bf16[4,80,512]{2,1,0:T(8,128)(2,1)S(1)} collective-permute-done((bf16[4,80,512]{2,1,0:T(8,128)(2,1)S(1)}, bf16[4,80,512]{2,1,0:T(8,128)(2,1)S(1)}, u32[]{:S(2)}, u32[]{:S(2)}) %collective-permute-start.44) | collective-permute-done | bytes 327712 | tf_op jit(solution)/shard_map/ppermute | solution.py:418
  164.4 1.2 convert_add_fusion.7
  165.9 1.3 collective-permute-start.47
  167.2 1.9 collective-permute-start.48
  169.2 1.1 convert_add_fusion.5
  170.8 3.5 %collective-permute-done.50 = bf16[4,80,640]{2,1,0:T(8,128)(2,1)S(1)} collective-permute-done((bf16[4,80,640]{2,1,0:T(8,128)(2,1)S(1)}, bf16[4,80,640]{2,1,0:T(8,128)(2,1)S(1)}, u32[]{:S(2)}, u32[]{:S(2)}) %collective-permute-start.50) | collective-permute-done | bytes 409632 | tf_op jit(solution)/shard_map/ppermute | solution.py:418
  174.3 3.7 %collective-permute-start.41 = (bf16[80,1024]{1,0:T(8,128)(2,1)S(1)}, bf16[80,1024]{1,0:T(8,128)(2,1)S(1)}, u32[]{:S(2)}, u32[]{:S(2)}) collective-permute-start(bf16[80,1024]{1,0:T(8,128)(2,1)S(1)} %get-tuple-element.99), channel_id=1, source_target_pairs={{0,4},{1,5},{2,6},{3,7},{4,0},{5,1},{6,2},{7,3},{8,12},{9,13},{10,... | collective-permute-start | bytes 491528 | tf_op jit(solution)/shard_map/ppermute | solution.py:418
  178.0 1.2 fusion.1
  179.2 3.5 %collective-permute-done.46 = bf16[80,896]{1,0:T(8,128)(2,1)S(1)} collective-permute-done((bf16[80,896]{1,0:T(8,128)(2,1)S(1)}, bf16[80,896]{1,0:T(8,128)(2,1)S(1)}, u32[]{:S(2)}, u32[]{:S(2)}) %collective-permute-start.46) | collective-permute-done | bytes 143392 | tf_op jit(solution)/shard_map/ppermute | solution.py:418
  182.7 5.8 %collective-permute-start.42 = (bf16[80,1024]{1,0:T(8,128)(2,1)S(1)}, bf16[80,1024]{1,0:T(8,128)(2,1)S(1)}, u32[]{:S(2)}, u32[]{:S(2)}) collective-permute-start(bf16[80,1024]{1,0:T(8,128)(2,1)S(1)} %get-tuple-element.98), channel_id=1, source_target_pairs={{0,6},{1,7},{2,0},{3,1},{4,2},{5,3},{6,4},{7,5},{8,14},{9,15},{10,... | collective-permute-start | bytes 491528 | tf_op jit(solution)/shard_map/ppermute | solution.py:418
  188.5 3.4 %collective-permute-done.48 = bf16[80,896]{1,0:T(8,128)(2,1)S(1)} collective-permute-done((bf16[80,896]{1,0:T(8,128)(2,1)S(1)}, bf16[80,896]{1,0:T(8,128)(2,1)S(1)}, u32[]{:S(2)}, u32[]{:S(2)}) %collective-permute-start.48) | collective-permute-done | bytes 143392 | tf_op jit(solution)/shard_map/ppermute | solution.py:418
  192.1 1.7 collective-permute-start.51
  194.4 1.6 collective-permute-start.49
  196.5 1.4 collective-permute-start.43
  198.8 1.2 collective-permute-start.52
  200.1 2.3 %collective-permute-done.54 = bf16[80,256]{1,0:T(8,128)(2,1)S(1)} collective-permute-done((bf16[80,256]{1,0:T(8,128)(2,1)S(1)}, bf16[80,256]{1,0:T(8,128)(2,1)S(1)}, u32[]{:S(2)}, u32[]{:S(2)}) %collective-permute-start.54) | collective-permute-done | bytes 40992 | tf_op jit(solution)/shard_map/ppermute | solution.py:418
  202.6 1.5 collective-permute-done.43
  204.1 1.2 copy-done.2
  205.3 1.2 fusion
  206.6 1.1 collective-permute-start.55
  208.2 3.1 %collective-permute-done.55 = bf16[80,640]{1,0:T(8,128)(2,1)S(1)} collective-permute-done((bf16[80,640]{1,0:T(8,128)(2,1)S(1)}, bf16[80,640]{1,0:T(8,128)(2,1)S(1)}, u32[]{:S(2)}, u32[]{:S(2)}) %collective-permute-start.55) | collective-permute-done | bytes 102432 | tf_op jit(solution)/shard_map/ppermute | solution.py:418
  (192 shorter events, 24.1 us)
Async XLA Ops:
  2.7 13.4 %collective-permute-start.4 = (bf16[1,80,2560]{2,1,0:T(8,128)(2,1)S(1)}, bf16[1,80,2560]{2,1,0:T(8,128)(2,1)S(1)}, u32[]{:S(2)}, u32[]{:S(2)}) collective-permute-start(bf16[1,80,2560]{2,1,0:T(8,128)(2,1)S(1)} %pad_maximum_fusion.1), channel_id=1, source_target_pairs={{0,2},{1,3},{2,4},{3,5},{4,6},{5,7},{6,0},{7,1},{8,10},{9,11},{10,... | collective-permute-start | bytes 1228808 | tf_op jit(solution)/shard_map/ppermute | solution.py:418
  4.5 1.2 collective-permute-start
  5.7 8.4 %collective-permute-start.1 = (f32[2,320]{1,0:T(2,128)S(1)}, f32[2,320]{1,0:T(2,128)S(1)}, u32[]{:S(2)}, u32[]{:S(2)}) collective-permute-start(f32[2,320]{1,0:T(2,128)S(1)} %pad_maximum_fusion.4), channel_id=1, source_target_pairs={{0,2},{1,3},{2,4},{3,5},{4,6},{5,7},{6,0},{7,1},{8,10},{9,11},{10,... | collective-permute-start | bytes 7688 | tf_op jit(solution)/shard_map/ppermute | solution.py:418
  7.3 7.8 %collective-permute-start.2 = (f32[2,320]{1,0:T(2,128)S(1)}, f32[2,320]{1,0:T(2,128)S(1)}, u32[]{:S(2)}, u32[]{:S(2)}) collective-permute-start(f32[2,320]{1,0:T(2,128)S(1)} %pad_maximum_fusion.4), channel_id=1, source_target_pairs={{0,4},{1,5},{2,6},{3,7},{4,0},{5,1},{6,2},{7,3},{8,12},{9,13},{10,... | collective-permute-start | bytes 7688 | tf_op jit(solution)/shard_map/ppermute | solution.py:418
  8.5 6.6 %collective-permute-start.3 = (f32[2,320]{1,0:T(2,128)S(1)}, f32[2,320]{1,0:T(2,128)S(1)}, u32[]{:S(2)}, u32[]{:S(2)}) collective-permute-start(f32[2,320]{1,0:T(2,128)S(1)} %pad_maximum_fusion.4), channel_id=1, source_target_pairs={{0,6},{1,7},{2,0},{3,1},{4,2},{5,3},{6,4},{7,5},{8,14},{9,15},{10,... | collective-permute-start | bytes 7688 | tf_op jit(solution)/shard_map/ppermute | solution.py:418
  16.1 15.4 %copy-start.4 = (bf16[1,80,2560]{2,1,0:T(8,128)(2,1)}, bf16[1,80,2560]{2,1,0:T(8,128)(2,1)S(1)}, u32[]{:S(2)}) copy-start(bf16[1,80,2560]{2,1,0:T(8,128)(2,1)S(1)} %collective-permute-done.4.rest_2_) | copy-start | bytes 1228804
  17.7 24.6 %copy-start = (bf16[4,80,2560]{2,1,0:T(8,128)(2,1)}, bf16[4,80,2560]{2,1,0:T(8,128)(2,1)S(1)}, u32[]{:S(2)}) copy-start(bf16[4,80,2560]{2,1,0:T(8,128)(2,1)S(1)} %pad_maximum_fusion.rest_0_) | copy-start | bytes 4915204
  17.7 20.2 %copy-start.30 = (s32[4]{0:T(128)S(1)}, s32[4]{0:T(128)}, u32[]{:S(2)}) copy-start(s32[4]{0:T(128)} %kind_ref.5) | copy-start | bytes 52
  17.7 13.8 %collective-permute-start.5 = (bf16[4,80,2560]{2,1,0:T(8,128)(2,1)S(1)}, bf16[4,80,2560]{2,1,0:T(8,128)(2,1)}, u32[]{:S(2)}, u32[]{:S(2)}) collective-permute-start(bf16[4,80,2560]{2,1,0:T(8,128)(2,1)S(1)} %pad_maximum_fusion.rest_0_), channel_id=1, source_target_pairs={{0,1},{1,0},{2,3},{3,2},{4,5},{5,4},{6,7},{7,6},{8,9},{9,8},{10,11... | collective-permute-start | bytes 4915208 | tf_op jit(solution)/shard_map/ppermute | solution.py:418
  17.8 12.0 %collective-permute-start.6 = (bf16[1,80,2560]{2,1,0:T(8,128)(2,1)S(1)}, bf16[1,80,2560]{2,1,0:T(8,128)(2,1)}, u32[]{:S(2)}, u32[]{:S(2)}) collective-permute-start(bf16[1,80,2560]{2,1,0:T(8,128)(2,1)S(1)} %collective-permute-done.4.rest_2_), channel_id=1, source_target_pairs={{0,2},{1,3},{2,4},{3,5},{4,6},{5,7},{6,0},{7,1},{8,10},{9,11},{10,... | collective-permute-start | bytes 1228808 | tf_op jit(solution)/shard_map/ppermute | solution.py:418
  18.7 11.6 %collective-permute-start.7 = (bf16[1,80,2560]{2,1,0:T(8,128)(2,1)S(1)}, bf16[1,80,2560]{2,1,0:T(8,128)(2,1)}, u32[]{:S(2)}, u32[]{:S(2)}) collective-permute-start(bf16[1,80,2560]{2,1,0:T(8,128)(2,1)S(1)} %collective-permute-done.4.rest_2_), channel_id=1, source_target_pairs={{0,8},{1,9},{2,10},{3,11},{4,12},{5,13},{6,14},{7,15},{8,0},{9,1},... | collective-permute-start | bytes 1228808 | tf_op jit(solution)/shard_map/ppermute | solution.py:418
  20.1 11.4 %collective-permute-start.8 = (bf16[1,80,2560]{2,1,0:T(8,128)(2,1)S(1)}, bf16[1,80,2560]{2,1,0:T(8,128)(2,1)}, u32[]{:S(2)}, u32[]{:S(2)}) collective-permute-start(bf16[1,80,2560]{2,1,0:T(8,128)(2,1)S(1)} %collective-permute-done.4.rest_2_), channel_id=1, source_target_pairs={{0,16},{1,17},{2,18},{3,19},{4,20},{5,21},{6,22},{7,23},{8,24},{9,... | collective-permute-start | bytes 1228808 | tf_op jit(solution)/shard_map/ppermute | solution.py:418
  31.5 5.9 %collective-permute-start.15 = (bf16[4,1280,128]{2,1,0:T(8,128)(2,1)}, bf16[4,1280,128]{2,1,0:T(8,128)(2,1)}, u32[]{:S(2)}, u32[]{:S(2)}) collective-permute-start(bf16[4,1280,128]{2,1,0:T(8,128)(2,1)} %get-tuple-element.57.ht_a), channel_id=1, source_target_pairs={{0,1},{1,0},{2,3},{3,2},{4,5},{5,4},{6,7},{7,6},{8,9},{9,8},{10,11... | collective-permute-start | bytes 3932168 | tf_op jit(solution)/shard_map/ppermute | solution.py:418
  31.5 5.9 %collective-permute-start.9 = (bf16[1,80,2560]{2,1,0:T(8,128)(2,1)S(1)}, bf16[1,80,2560]{2,1,0:T(8,128)(2,1)S(1)}, u32[]{:S(2)}, u32[]{:S(2)}) collective-permute-start(bf16[1,80,2560]{2,1,0:T(8,128)(2,1)S(1)} %collective-permute-done.4.rest_2_), channel_id=1, source_target_pairs={{0,1},{1,0},{2,3},{3,2},{4,5},{5,4},{6,7},{7,6},{8,9},{9,8},{10,11... | collective-permute-start | bytes 1228808 | tf_op jit(solution)/shard_map/ppermute | solution.py:418
  32.0 13.4 %collective-permute-start.13 = (bf16[1,80,2560]{2,1,0:T(8,128)(2,1)}, bf16[1,80,2560]{2,1,0:T(8,128)(2,1)}, u32[]{:S(2)}, u32[]{:S(2)}) collective-permute-start(bf16[1,80,2560]{2,1,0:T(8,128)(2,1)} %collective-permute-done.6.rest_10_), channel_id=1, source_target_pairs={{0,8},{1,9},{2,10},{3,11},{4,12},{5,13},{6,14},{7,15},{8,0},{9,1},... | collective-permute-start | bytes 1228808 | tf_op jit(solution)/shard_map/ppermute | solution.py:418
  32.6 12.9 %collective-permute-start.14 = (bf16[1,80,2560]{2,1,0:T(8,128)(2,1)}, bf16[1,80,2560]{2,1,0:T(8,128)(2,1)}, u32[]{:S(2)}, u32[]{:S(2)}) collective-permute-start(bf16[1,80,2560]{2,1,0:T(8,128)(2,1)} %collective-permute-done.6.rest_10_), channel_id=1, source_target_pairs={{0,16},{1,17},{2,18},{3,19},{4,20},{5,21},{6,22},{7,23},{8,24},{9,... | collective-permute-start | bytes 1228808 | tf_op jit(solution)/shard_map/ppermute | solution.py:418
  34.1 11.4 %collective-permute-start.12 = (bf16[1,80,2560]{2,1,0:T(8,128)(2,1)}, bf16[1,80,2560]{2,1,0:T(8,128)(2,1)}, u32[]{:S(2)}, u32[]{:S(2)}) collective-permute-start(bf16[1,80,2560]{2,1,0:T(8,128)(2,1)} %copy-done.28), channel_id=1, source_target_pairs={{0,6},{1,7},{2,0},{3,1},{4,2},{5,3},{6,4},{7,5},{8,14},{9,15},{10,... | collective-permute-start | bytes 1228808 | tf_op jit(solution)/shard_map/ppermute | solution.py:418
  37.4 11.4 %collective-permute-start.11 = (bf16[1,80,2560]{2,1,0:T(8,128)(2,1)}, bf16[1,80,2560]{2,1,0:T(8,128)(2,1)S(1)}, u32[]{:S(2)}, u32[]{:S(2)}) collective-permute-start(bf16[1,80,2560]{2,1,0:T(8,128)(2,1)} %collective-permute-done.8.rest_6_), channel_id=1, source_target_pairs={{0,1},{1,0},{2,3},{3,2},{4,5},{5,4},{6,7},{7,6},{8,9},{9,8},{10,11... | collective-permute-start | bytes 1228808 | tf_op jit(solution)/shard_map/ppermute | solution.py:418
  37.4 12.2 %collective-permute-start.10 = (bf16[1,80,2560]{2,1,0:T(8,128)(2,1)}, bf16[1,80,2560]{2,1,0:T(8,128)(2,1)}, u32[]{:S(2)}, u32[]{:S(2)}) collective-permute-start(bf16[1,80,2560]{2,1,0:T(8,128)(2,1)} %collective-permute-done.7.rest_4_), channel_id=1, source_target_pairs={{0,1},{1,0},{2,3},{3,2},{4,5},{5,4},{6,7},{7,6},{8,9},{9,8},{10,11... | collective-permute-start | bytes 1228808 | tf_op jit(solution)/shard_map/ppermute | solution.py:418
  42.3 28.6 %copy-start.1 = (bf16[4,128,1280]{2,1,0:T(8,128)(2,1)S(1)}, bf16[4,128,1280]{2,1,0:T(8,128)(2,1)}, u32[]{:S(2)}) copy-start(bf16[4,128,1280]{2,1,0:T(8,128)(2,1)} %cot_ref.3) | copy-start | bytes 3932164
  45.4 5.1 %collective-permute-start.18 = (bf16[1,80,2560]{2,1,0:T(8,128)(2,1)}, bf16[1,80,2560]{2,1,0:T(8,128)(2,1)S(1)}, u32[]{:S(2)}, u32[]{:S(2)}) collective-permute-start(bf16[1,80,2560]{2,1,0:T(8,128)(2,1)} %collective-permute-done.6.rest_10_), channel_id=1, source_target_pairs={{0,1},{1,0},{2,3},{3,2},{4,5},{5,4},{6,7},{7,6},{8,9},{9,8},{10,11... | collective-permute-start | bytes 1228808 | tf_op jit(solution)/shard_map/ppermute | solution.py:418
  46.5 12.5 %collective-permute-start.21 = (bf16[1,80,2560]{2,1,0:T(8,128)(2,1)}, bf16[1,80,2560]{2,1,0:T(8,128)(2,1)S(1)}, u32[]{:S(2)}, u32[]{:S(2)}) collective-permute-start(bf16[1,80,2560]{2,1,0:T(8,128)(2,1)} %collective-permute-done.13.rest_12_), channel_id=1, source_target_pairs={{0,16},{1,17},{2,18},{3,19},{4,20},{5,21},{6,22},{7,23},{8,24},{9,... | collective-permute-start | bytes 1228808 | tf_op jit(solution)/shard_map/ppermute | solution.py:418
  47.0 12.7 %collective-permute-start.16 = (bf16[1,80,2560]{2,1,0:T(8,128)(2,1)S(1)}, bf16[1,80,2560]{2,1,0:T(8,128)(2,1)S(1)}, u32[]{:S(2)}, u32[]{:S(2)}) collective-permute-start(bf16[1,80,2560]{2,1,0:T(8,128)(2,1)S(1)} %fusion.7), channel_id=1, source_target_pairs={{0,2},{1,3},{2,4},{3,5},{4,6},{5,7},{6,0},{7,1},{8,10},{9,11},{10,... | collective-permute-start | bytes 1228808 | tf_op jit(solution)/shard_map/ppermute | solution.py:418
  48.8 28.3 %copy-start.6 = (bf16[1,80,2560]{2,1,0:T(8,128)(2,1)}, bf16[1,80,2560]{2,1,0:T(8,128)(2,1)S(1)}, u32[]{:S(2)}) copy-start(bf16[1,80,2560]{2,1,0:T(8,128)(2,1)S(1)} %collective-permute-done.11.rest_7_) | copy-start | bytes 1228804
  48.8 21.6 %collective-permute-start.28 = (bf16[1,80,2560]{2,1,0:T(8,128)(2,1)S(1)}, bf16[1,80,2560]{2,1,0:T(8,128)(2,1)S(1)}, u32[]{:S(2)}, u32[]{:S(2)}) collective-permute-start(bf16[1,80,2560]{2,1,0:T(8,128)(2,1)S(1)} %fusion.7), channel_id=1, source_target_pairs={{0,6},{1,7},{2,0},{3,1},{4,2},{5,3},{6,4},{7,5},{8,14},{9,15},{10,... | collective-permute-start | bytes 1228808 | tf_op jit(solution)/shard_map/ppermute | solution.py:418
  49.6 20.9 %collective-permute-start.24 = (bf16[1,80,2560]{2,1,0:T(8,128)(2,1)}, bf16[1,80,2560]{2,1,0:T(8,128)(2,1)S(1)}, u32[]{:S(2)}, u32[]{:S(2)}) collective-permute-start(bf16[1,80,2560]{2,1,0:T(8,128)(2,1)} %collective-permute-done.12.rest_18_), channel_id=1, source_target_pairs={{0,8},{1,9},{2,10},{3,11},{4,12},{5,13},{6,14},{7,15},{8,0},{9,1},... | collective-permute-start | bytes 1228808 | tf_op jit(solution)/shard_map/ppermute | solution.py:418
  50.5 26.6 %copy-start.7 = (bf16[1,80,2560]{2,1,0:T(8,128)(2,1)}, bf16[1,80,2560]{2,1,0:T(8,128)(2,1)S(1)}, u32[]{:S(2)}) copy-start(bf16[1,80,2560]{2,1,0:T(8,128)(2,1)S(1)} %collective-permute-done.18.rest_11_) | copy-start | bytes 1228804
  50.5 20.4 %collective-permute-start.26 = (bf16[1,80,2560]{2,1,0:T(8,128)(2,1)}, bf16[1,80,2560]{2,1,0:T(8,128)(2,1)S(1)}, u32[]{:S(2)}, u32[]{:S(2)}) collective-permute-start(bf16[1,80,2560]{2,1,0:T(8,128)(2,1)} %collective-permute-done.12.rest_18_), channel_id=1, source_target_pairs={{0,16},{1,17},{2,18},{3,19},{4,20},{5,21},{6,22},{7,23},{8,24},{9,... | collective-permute-start | bytes 1228808 | tf_op jit(solution)/shard_map/ppermute | solution.py:418
  59.0 18.1 %copy-start.8 = (bf16[1,80,2560]{2,1,0:T(8,128)(2,1)}, bf16[1,80,2560]{2,1,0:T(8,128)(2,1)S(1)}, u32[]{:S(2)}) copy-start(bf16[1,80,2560]{2,1,0:T(8,128)(2,1)S(1)} %collective-permute-done.21.rest_16_) | copy-start | bytes 1228804
  59.0 12.1 %collective-permute-start.23 = (bf16[1,80,2560]{2,1,0:T(8,128)(2,1)}, bf16[1,80,2560]{2,1,0:T(8,128)(2,1)S(1)}, u32[]{:S(2)}, u32[]{:S(2)}) collective-permute-start(bf16[1,80,2560]{2,1,0:T(8,128)(2,1)} %collective-permute-done.12.rest_18_), channel_id=1, source_target_pairs={{0,1},{1,0},{2,3},{3,2},{4,5},{5,4},{6,7},{7,6},{8,9},{9,8},{10,11... | collective-permute-start | bytes 1228808 | tf_op jit(solution)/shard_map/ppermute | solution.py:418
  59.7 17.3 %copy-start.9 = (bf16[1,80,2560]{2,1,0:T(8,128)(2,1)}, bf16[1,80,2560]{2,1,0:T(8,128)(2,1)S(1)}, u32[]{:S(2)}) copy-start(bf16[1,80,2560]{2,1,0:T(8,128)(2,1)S(1)} %collective-permute-done.16.rest_8_) | copy-start | bytes 1228804
  59.8 11.7 %collective-permute-start.22 = (bf16[1,80,2560]{2,1,0:T(8,128)(2,1)S(1)}, bf16[1,80,2560]{2,1,0:T(8,128)(2,1)S(1)}, u32[]{:S(2)}, u32[]{:S(2)}) collective-permute-start(bf16[1,80,2560]{2,1,0:T(8,128)(2,1)S(1)} %collective-permute-done.21.rest_16_), channel_id=1, source_target_pairs={{0,1},{1,0},{2,3},{3,2},{4,5},{5,4},{6,7},{7,6},{8,9},{9,8},{10,11... | collective-permute-start | bytes 1228808 | tf_op jit(solution)/shard_map/ppermute | solution.py:418
  70.4 2.0 collective-permute-start.20
  70.4 2.5 %collective-permute-start.19 = (bf16[1,80,2560]{2,1,0:T(8,128)(2,1)}, bf16[1,80,2560]{2,1,0:T(8,128)(2,1)S(1)}, u32[]{:S(2)}, u32[]{:S(2)}) collective-permute-start(bf16[1,80,2560]{2,1,0:T(8,128)(2,1)} %collective-permute-done.13.rest_12_), channel_id=1, source_target_pairs={{0,1},{1,0},{2,3},{3,2},{4,5},{5,4},{6,7},{7,6},{8,9},{9,8},{10,11... | collective-permute-start | bytes 1228808 | tf_op jit(solution)/shard_map/ppermute | solution.py:418
  70.9 47.9 %collective-permute-start.34 = (bf16[4,128,1280]{2,1,0:T(8,128)(2,1)S(1)}, bf16[4,128,1280]{2,1,0:T(8,128)(2,1)}, u32[]{:S(2)}, u32[]{:S(2)}) collective-permute-start(bf16[4,128,1280]{2,1,0:T(8,128)(2,1)S(1)} %copy-done.1), channel_id=1, source_target_pairs={{0,1},{1,0},{2,3},{3,2},{4,5},{5,4},{6,7},{7,6},{8,9},{9,8},{10,11... | collective-permute-start | bytes 3932168 | tf_op jit(solution)/shard_map/ppermute | solution.py:418
  71.0 2.8 %collective-permute-start.17 = (bf16[1,80,2560]{2,1,0:T(8,128)(2,1)S(1)}, bf16[1,80,2560]{2,1,0:T(8,128)(2,1)S(1)}, u32[]{:S(2)}, u32[]{:S(2)}) collective-permute-start(bf16[1,80,2560]{2,1,0:T(8,128)(2,1)S(1)} %collective-permute-done.16.rest_8_), channel_id=1, source_target_pairs={{0,1},{1,0},{2,3},{3,2},{4,5},{5,4},{6,7},{7,6},{8,9},{9,8},{10,11... | collective-permute-start | bytes 1228808 | tf_op jit(solution)/shard_map/ppermute | solution.py:418
  71.5 3.6 %collective-permute-start.29 = (bf16[1,80,2560]{2,1,0:T(8,128)(2,1)S(1)}, bf16[1,80,2560]{2,1,0:T(8,128)(2,1)S(1)}, u32[]{:S(2)}, u32[]{:S(2)}) collective-permute-start(bf16[1,80,2560]{2,1,0:T(8,128)(2,1)S(1)} %collective-permute-done.28.rest_24_), channel_id=1, source_target_pairs={{0,1},{1,0},{2,3},{3,2},{4,5},{5,4},{6,7},{7,6},{8,9},{9,8},{10,11... | collective-permute-start | bytes 1228808 | tf_op jit(solution)/shard_map/ppermute | solution.py:418
  72.3 3.9 %collective-permute-start.25 = (bf16[1,80,2560]{2,1,0:T(8,128)(2,1)S(1)}, bf16[1,80,2560]{2,1,0:T(8,128)(2,1)S(1)}, u32[]{:S(2)}, u32[]{:S(2)}) collective-permute-start(bf16[1,80,2560]{2,1,0:T(8,128)(2,1)S(1)} %collective-permute-done.24.rest_20_), channel_id=1, source_target_pairs={{0,1},{1,0},{2,3},{3,2},{4,5},{5,4},{6,7},{7,6},{8,9},{9,8},{10,11... | collective-permute-start | bytes 1228808 | tf_op jit(solution)/shard_map/ppermute | solution.py:418
  72.9 4.1 %collective-permute-start.27 = (bf16[1,80,2560]{2,1,0:T(8,128)(2,1)S(1)}, bf16[1,80,2560]{2,1,0:T(8,128)(2,1)}, u32[]{:S(2)}, u32[]{:S(2)}) collective-permute-start(bf16[1,80,2560]{2,1,0:T(8,128)(2,1)S(1)} %collective-permute-done.26.rest_22_), channel_id=1, source_target_pairs={{0,1},{1,0},{2,3},{3,2},{4,5},{5,4},{6,7},{7,6},{8,9},{9,8},{10,11... | collective-permute-start | bytes 1228808 | tf_op jit(solution)/shard_map/ppermute | solution.py:418
  96.8 2.4 %collective-permute-start.30 = (bf16[4,128,640]{2,1,0:T(8,128)(2,1)}, bf16[4,128,640]{2,1,0:T(8,128)(2,1)S(1)}, u32[]{:S(2)}, u32[]{:S(2)}) collective-permute-start(bf16[4,128,640]{2,1,0:T(8,128)(2,1)} %get-tuple-element.66.rest_0_.dq_ref), channel_id=1, source_target_pairs={{0,1},{1,0},{2,3},{3,2},{4,5},{5,4},{6,7},{7,6},{8,9},{9,8},{10,11... | collective-permute-start | bytes 1966088 | tf_op jit(solution)/shard_map/ppermute | solution.py:418
  96.9 4.2 %collective-permute-start.31 = (bf16[4,128,640]{2,1,0:T(8,128)(2,1)}, bf16[4,128,640]{2,1,0:T(8,128)(2,1)S(1)}, u32[]{:S(2)}, u32[]{:S(2)}) collective-permute-start(bf16[4,128,640]{2,1,0:T(8,128)(2,1)} %get-tuple-element.67.rest_2_.dk_ref), channel_id=1, source_target_pairs={{0,1},{1,0},{2,3},{3,2},{4,5},{5,4},{6,7},{7,6},{8,9},{9,8},{10,11... | collective-permute-start | bytes 1966088 | tf_op jit(solution)/shard_map/ppermute | solution.py:418
  97.4 4.6 %collective-permute-start.32 = (bf16[4,128,640]{2,1,0:T(8,128)(2,1)}, bf16[4,128,640]{2,1,0:T(8,128)(2,1)S(1)}, u32[]{:S(2)}, u32[]{:S(2)}) collective-permute-start(bf16[4,128,640]{2,1,0:T(8,128)(2,1)} %get-tuple-element.68.rest_4_.dv_ref), channel_id=1, source_target_pairs={{0,1},{1,0},{2,3},{3,2},{4,5},{5,4},{6,7},{7,6},{8,9},{9,8},{10,11... | collective-permute-start | bytes 1966088 | tf_op jit(solution)/shard_map/ppermute | solution.py:418
  97.5 21.3 %collective-permute-start.33 = (bf16[4,640,128]{2,1,0:T(8,128)(2,1)}, bf16[4,640,128]{2,1,0:T(8,128)(2,1)}, u32[]{:S(2)}, u32[]{:S(2)}) collective-permute-start(bf16[4,640,128]{2,1,0:T(8,128)(2,1)} %get-tuple-element.73.attnt_a.attnt_ref), channel_id=1, source_target_pairs={{0,1},{1,0},{2,3},{3,2},{4,5},{5,4},{6,7},{7,6},{8,9},{9,8},{10,11... | collective-permute-start | bytes 1966088 | tf_op jit(solution)/shard_map/ppermute | solution.py:418
  114.2 32.5 %collective-permute-start.35 = (bf16[2,4,80,1024]{3,2,1,0:T(8,128)(2,1)}, bf16[2,4,80,1024]{3,2,1,0:T(8,128)(2,1)}, u32[]{:S(2)}, u32[]{:S(2)}) collective-permute-start(bf16[2,4,80,1024]{3,2,1,0:T(8,128)(2,1)} %get-tuple-element.69), channel_id=1, source_target_pairs={{0,16},{1,17},{2,18},{3,19},{4,20},{5,21},{6,22},{7,23},{8,24},{9,... | collective-permute-start | bytes 3932168 | tf_op jit(solution)/shard_map/ppermute | solution.py:418
  117.3 28.4 %collective-permute-start.36 = (bf16[2,4,80,896]{3,2,1,0:T(8,128)(2,1)}, bf16[2,4,80,896]{3,2,1,0:T(8,128)(2,1)}, u32[]{:S(2)}, u32[]{:S(2)}) collective-permute-start(bf16[2,4,80,896]{3,2,1,0:T(8,128)(2,1)} %get-tuple-element.77), channel_id=1, source_target_pairs={{0,8},{1,9},{2,10},{3,11},{4,12},{5,13},{6,14},{7,15},{8,0},{9,1},... | collective-permute-start | bytes 3440648 | tf_op jit(solution)/shard_map/ppermute | solution.py:418
  124.5 20.1 %collective-permute-start.37 = (bf16[2,4,80,640]{3,2,1,0:T(8,128)(2,1)}, bf16[2,4,80,640]{3,2,1,0:T(8,128)(2,1)}, u32[]{:S(2)}, u32[]{:S(2)}) collective-permute-start(bf16[2,4,80,640]{3,2,1,0:T(8,128)(2,1)} %get-tuple-element.79), channel_id=1, source_target_pairs={{0,2},{1,3},{2,0},{3,1},{4,6},{5,7},{6,4},{7,5},{8,10},{9,11},{10,... | collective-permute-start | bytes 2457608 | tf_op jit(solution)/shard_map/ppermute | solution.py:418
  148.0 13.0 %collective-permute-start.38 = (bf16[4,80,512]{2,1,0:T(8,128)(2,1)S(1)}, bf16[4,80,512]{2,1,0:T(8,128)(2,1)S(1)}, u32[]{:S(2)}, u32[]{:S(2)}) collective-permute-start(bf16[4,80,512]{2,1,0:T(8,128)(2,1)S(1)} %get-tuple-element.92), channel_id=1, source_target_pairs={{0,8},{1,9},{2,10},{3,11},{4,12},{5,13},{6,14},{7,15},{8,0},{9,1},... | collective-permute-start | bytes 983048 | tf_op jit(solution)/shard_map/ppermute | solution.py:418
  149.6 14.8 %collective-permute-start.44 = (bf16[4,80,512]{2,1,0:T(8,128)(2,1)S(1)}, bf16[4,80,512]{2,1,0:T(8,128)(2,1)S(1)}, u32[]{:S(2)}, u32[]{:S(2)}) collective-permute-start(bf16[4,80,512]{2,1,0:T(8,128)(2,1)S(1)} %get-tuple-element.93), channel_id=1, source_target_pairs={{0,8},{1,9},{2,10},{3,11},{4,12},{5,13},{6,14},{7,15},{8,0},{9,1},... | collective-permute-start | bytes 983048 | tf_op jit(solution)/shard_map/ppermute | solution.py:418
  151.1 9.0 %collective-permute-start.45 = (bf16[4,80,384]{2,1,0:T(8,128)(2,1)S(1)}, bf16[4,80,384]{2,1,0:T(8,128)(2,1)S(1)}, u32[]{:S(2)}, u32[]{:S(2)}) collective-permute-start(bf16[4,80,384]{2,1,0:T(8,128)(2,1)S(1)} %fusion.6), channel_id=1, source_target_pairs={{0,16},{1,17},{2,18},{3,19},{4,20},{5,21},{6,22},{7,23},{8,24},{9,... | collective-permute-start | bytes 737288 | tf_op jit(solution)/shard_map/ppermute | solution.py:418
  154.0 20.3 %collective-permute-start.50 = (bf16[4,80,640]{2,1,0:T(8,128)(2,1)S(1)}, bf16[4,80,640]{2,1,0:T(8,128)(2,1)S(1)}, u32[]{:S(2)}, u32[]{:S(2)}) collective-permute-start(bf16[4,80,640]{2,1,0:T(8,128)(2,1)S(1)} %fusion.2), channel_id=1, source_target_pairs={{0,4},{1,5},{2,6},{3,7},{4,0},{5,1},{6,2},{7,3},{8,12},{9,13},{10,... | collective-permute-start | bytes 1228808 | tf_op jit(solution)/shard_map/ppermute | solution.py:418
  154.9 14.3 %collective-permute-start.39 = (bf16[4,80,512]{2,1,0:T(8,128)(2,1)S(1)}, bf16[4,80,512]{2,1,0:T(8,128)(2,1)S(1)}, u32[]{:S(2)}, u32[]{:S(2)}) collective-permute-start(bf16[4,80,512]{2,1,0:T(8,128)(2,1)S(1)} %fusion.4), channel_id=1, source_target_pairs={{0,16},{1,17},{2,18},{3,19},{4,20},{5,21},{6,22},{7,23},{8,24},{9,... | collective-permute-start | bytes 983048 | tf_op jit(solution)/shard_map/ppermute | solution.py:418
  165.8 16.9 %collective-permute-start.46 = (bf16[80,896]{1,0:T(8,128)(2,1)S(1)}, bf16[80,896]{1,0:T(8,128)(2,1)S(1)}, u32[]{:S(2)}, u32[]{:S(2)}) collective-permute-start(bf16[80,896]{1,0:T(8,128)(2,1)S(1)} %get-tuple-element.104), channel_id=1, source_target_pairs={{0,2},{1,3},{2,4},{3,5},{4,6},{5,7},{6,0},{7,1},{8,10},{9,11},{10,... | collective-permute-start | bytes 430088 | tf_op jit(solution)/shard_map/ppermute | solution.py:418
  165.9 22.6 %collective-permute-start.47 = (bf16[80,896]{1,0:T(8,128)(2,1)S(1)}, bf16[80,896]{1,0:T(8,128)(2,1)S(1)}, u32[]{:S(2)}, u32[]{:S(2)}) collective-permute-start(bf16[80,896]{1,0:T(8,128)(2,1)S(1)} %get-tuple-element.106), channel_id=1, source_target_pairs={{0,4},{1,5},{2,6},{3,7},{4,0},{5,1},{6,2},{7,3},{8,12},{9,13},{10,... | collective-permute-start | bytes 430088 | tf_op jit(solution)/shard_map/ppermute | solution.py:418
  167.2 24.7 %collective-permute-start.48 = (bf16[80,896]{1,0:T(8,128)(2,1)S(1)}, bf16[80,896]{1,0:T(8,128)(2,1)S(1)}, u32[]{:S(2)}, u32[]{:S(2)}) collective-permute-start(bf16[80,896]{1,0:T(8,128)(2,1)S(1)} %get-tuple-element.105), channel_id=1, source_target_pairs={{0,6},{1,7},{2,0},{3,1},{4,2},{5,3},{6,4},{7,5},{8,14},{9,15},{10,... | collective-permute-start | bytes 430088 | tf_op jit(solution)/shard_map/ppermute | solution.py:418
  170.5 23.8 %collective-permute-start.40 = (bf16[80,1024]{1,0:T(8,128)(2,1)S(1)}, bf16[80,1024]{1,0:T(8,128)(2,1)S(1)}, u32[]{:S(2)}, u32[]{:S(2)}) collective-permute-start(bf16[80,1024]{1,0:T(8,128)(2,1)S(1)} %get-tuple-element.97), channel_id=1, source_target_pairs={{0,2},{1,3},{2,4},{3,5},{4,6},{5,7},{6,0},{7,1},{8,10},{9,11},{10,... | collective-permute-start | bytes 491528 | tf_op jit(solution)/shard_map/ppermute | solution.py:418
  174.3 22.0 %collective-permute-start.41 = (bf16[80,1024]{1,0:T(8,128)(2,1)S(1)}, bf16[80,1024]{1,0:T(8,128)(2,1)S(1)}, u32[]{:S(2)}, u32[]{:S(2)}) collective-permute-start(bf16[80,1024]{1,0:T(8,128)(2,1)S(1)} %get-tuple-element.99), channel_id=1, source_target_pairs={{0,4},{1,5},{2,6},{3,7},{4,0},{5,1},{6,2},{7,3},{8,12},{9,13},{10,... | collective-permute-start | bytes 491528 | tf_op jit(solution)/shard_map/ppermute | solution.py:418
  182.7 13.7 %collective-permute-start.42 = (bf16[80,1024]{1,0:T(8,128)(2,1)S(1)}, bf16[80,1024]{1,0:T(8,128)(2,1)S(1)}, u32[]{:S(2)}, u32[]{:S(2)}) collective-permute-start(bf16[80,1024]{1,0:T(8,128)(2,1)S(1)} %get-tuple-element.98), channel_id=1, source_target_pairs={{0,6},{1,7},{2,0},{3,1},{4,2},{5,3},{6,4},{7,5},{8,14},{9,15},{10,... | collective-permute-start | bytes 491528 | tf_op jit(solution)/shard_map/ppermute | solution.py:418
  192.1 6.7 %collective-permute-start.51 = (bf16[2,80,384]{2,1,0:T(8,128)(2,1)S(1)}, bf16[2,80,384]{2,1,0:T(8,128)(2,1)S(1)}, u32[]{:S(2)}, u32[]{:S(2)}) collective-permute-start(bf16[2,80,384]{2,1,0:T(8,128)(2,1)S(1)} %slice.200), channel_id=1, source_target_pairs={{0,16},{1,17},{2,18},{3,19},{4,20},{5,21},{6,22},{7,23},{8,24},{9,... | collective-permute-start | bytes 368648 | tf_op jit(solution)/shard_map/ppermute | solution.py:418
  193.8 4.5 %collective-permute-start.53 = (bf16[2,80,256]{2,1,0:T(8,128)(2,1)S(1)}, bf16[2,80,256]{2,1,0:T(8,128)(2,1)S(1)}, u32[]{:S(2)}, u32[]{:S(2)}) collective-permute-start(bf16[2,80,256]{2,1,0:T(8,128)(2,1)S(1)} %pad_maximum_fusion.3), channel_id=1, source_target_pairs={{0,8},{1,9},{2,10},{3,11},{4,12},{5,13},{6,14},{7,15},{8,0},{9,1},... | collective-permute-start | bytes 245768 | tf_op jit(solution)/shard_map/ppermute | solution.py:418
  194.4 8.1 %collective-permute-start.49 = (bf16[80,896]{1,0:T(8,128)(2,1)S(1)}, bf16[80,896]{1,0:T(8,128)(2,1)S(1)}, u32[]{:S(2)}, u32[]{:S(2)}) collective-permute-start(bf16[80,896]{1,0:T(8,128)(2,1)S(1)} %get-tuple-element.89), channel_id=1, source_target_pairs={{0,8},{1,9},{2,10},{3,11},{4,12},{5,13},{6,14},{7,15},{8,0},{9,1},... | collective-permute-start | bytes 430088 | tf_op jit(solution)/shard_map/ppermute | solution.py:418
  196.5 7.5 %collective-permute-start.43 = (bf16[80,1024]{1,0:T(8,128)(2,1)S(1)}, bf16[80,1024]{1,0:T(8,128)(2,1)S(1)}, u32[]{:S(2)}, u32[]{:S(2)}) collective-permute-start(bf16[80,1024]{1,0:T(8,128)(2,1)S(1)} %get-tuple-element.87), channel_id=1, source_target_pairs={{0,8},{1,9},{2,10},{3,11},{4,12},{5,13},{6,14},{7,15},{8,0},{9,1},... | collective-permute-start | bytes 491528 | tf_op jit(solution)/shard_map/ppermute | solution.py:418
  198.3 4.1 %collective-permute-start.54 = (bf16[80,256]{1,0:T(8,128)(2,1)S(1)}, bf16[80,256]{1,0:T(8,128)(2,1)S(1)}, u32[]{:S(2)}, u32[]{:S(2)}) collective-permute-start(bf16[80,256]{1,0:T(8,128)(2,1)S(1)} %fusion.16), channel_id=1, source_target_pairs={{0,16},{1,17},{2,18},{3,19},{4,20},{5,21},{6,22},{7,23},{8,24},{9,... | collective-permute-start | bytes 122888 | tf_op jit(solution)/shard_map/ppermute | solution.py:418
  198.8 7.7 %collective-permute-start.52 = (bf16[80,384]{1,0:T(8,128)(2,1)S(1)}, bf16[80,384]{1,0:T(8,128)(2,1)S(1)}, u32[]{:S(2)}, u32[]{:S(2)}) collective-permute-start(bf16[80,384]{1,0:T(8,128)(2,1)S(1)} %fusion.15), channel_id=1, source_target_pairs={{0,8},{1,9},{2,10},{3,11},{4,12},{5,13},{6,14},{7,15},{8,0},{9,1},... | collective-permute-start | bytes 184328 | tf_op jit(solution)/shard_map/ppermute | solution.py:418
  206.6 4.7 %collective-permute-start.55 = (bf16[80,640]{1,0:T(8,128)(2,1)S(1)}, bf16[80,640]{1,0:T(8,128)(2,1)S(1)}, u32[]{:S(2)}, u32[]{:S(2)}) collective-permute-start(bf16[80,640]{1,0:T(8,128)(2,1)S(1)} %fusion.20), channel_id=1, source_target_pairs={{0,8},{1,9},{2,10},{3,11},{4,12},{5,13},{6,14},{7,15},{8,0},{9,1},... | collective-permute-start | bytes 307208 | tf_op jit(solution)/shard_map/ppermute | solution.py:418
  (24 other events, 100.1 us)
